TPU v7x, 32 devices: a whole 2x2x4 slice. The times are simulated.
32 devices in a mesh: dp: 16 (over z, y, core), tensor: 2 (over x).
Axes of the slice: x: 2, y: 2, z: 4, core: 2. Of those that a mesh axis runs over, the one named last changes fastest.
Arguments:
- tokens: bfloat16 [4096, 2048], P('dp'), may hold values from -6 to 6
- attn_gain: bfloat16 [2048], P('dp'), may hold values from 0.25 to 1.75
- w_query: bfloat16 [2048, 2048], P('dp', 'tensor'), may hold values from -0.125 to 0.125
- w_key: bfloat16 [2048, 512], P('dp', 'tensor'), may hold values from -0.125 to 0.125
- w_value: bfloat16 [2048, 512], P('dp', 'tensor'), may hold values from -0.125 to 0.125
- w_out: bfloat16 [2048, 2048], P('tensor', 'dp'), may hold values from -0.5 to 0.5
- mlp_gain: bfloat16 [2048], P('dp'), may hold values from 0.25 to 1.75
- w_gate: bfloat16 [2048, 8192], P('dp', 'tensor'), may hold values from -0.125 to 0.125
- w_up: bfloat16 [2048, 8192], P('dp', 'tensor'), may hold values from -0.125 to 0.125
- w_down: bfloat16 [8192, 2048], P('tensor', 'dp'), may hold values from -0.0625 to 0.0625
- segment_ids: int32 [4096], P('dp'), may hold values from 0 to 31, never falling along the last dimension, each value on 1 to 256 neighbouring positions
- cotangent: bfloat16 [4096, 2048], P('dp'), may hold values from -6 to 6
Outputs:
- output: bfloat16 [4096, 2048], P('dp')
- input_grad: float32 [4096, 2048], P('dp')
- attn_gain_grad: float32 [2048], P('dp')
- query_grad: float32 [2048, 2048], P('dp', 'tensor')
- key_grad: float32 [2048, 512], P('dp', 'tensor')
- value_grad: float32 [2048, 512], P('dp', 'tensor')
- out_grad: float32 [2048, 2048], P('tensor', 'dp')
- mlp_gain_grad: float32 [2048], P('dp')
- gate_grad: float32 [2048, 8192], P('dp', 'tensor')
- up_grad: float32 [2048, 8192], P('dp', 'tensor')
- down_grad: float32 [8192, 2048], P('tensor', 'dp')
Inputs may be any that keep to these rules, and one draw needn't show every extreme that they name: `segment_ids`: segment numbers never fall along the tokens, every number from 0 up is used, and each document spans 1 to 256 tokens, one exactly 256.
All inputs are finite; a program needn't handle non-finite values.
Results may differ from a plain program's by a relative error of at most 0.015.
Values may be sent and summed in bfloat16 or wider, within the bound.
A program may use at most 256 MiB of HBM per device.

v0:
```python
import jax
import jax.numpy as jnp
from jax import lax
from jax.sharding import PartitionSpec as P

HEAD_DIM = 64


EPSILON = 1e-05
THETA = 500000.0


def positions(segment_ids, length):
    segments = segment_ids.reshape(-1, length)
    places = jnp.arange(length, dtype=jnp.int32)[None, :]
    earlier = jnp.concatenate([segments[:, :1], segments[:, :-1]], axis=1)
    begins = jnp.where((segments != earlier) | (places == 0), places, jnp.zeros_like(places))
    return places - lax.cummax(begins, axis=1)


def rotary(position):
    halves = HEAD_DIM // 2
    inverse = THETA ** (-2.0 * jnp.arange(halves, dtype=jnp.float32) / HEAD_DIM)
    angles = position.astype(jnp.float32)[..., None] * inverse
    return (jnp.cos(angles), jnp.sin(angles))


def rotate(values, cosine, sine_table):
    halves = values.shape[-1] // 2
    front_half = values[..., :halves]
    back_half = values[..., halves:]
    cos_wide = cosine[..., None, :]
    sin_wide = sine_table[..., None, :]
    return jnp.concatenate(
        [
            front_half * cos_wide - back_half * sin_wide,
            back_half * cos_wide + front_half * sin_wide,
        ],
        axis=-1,
    )


def inv_root(values):
    return lax.rsqrt(jnp.mean(values * values, axis=-1, keepdims=True) + EPSILON)


def norm_back(values, roots, gains, grads):
    scaled = grads * gains
    return roots * scaled - values * roots**3 * jnp.mean(values * scaled, axis=-1, keepdims=True)


def block_mask(segments, offset, rows, key_reach):
    query_places = offset + jnp.arange(rows)
    key_places = jnp.arange(key_reach)
    same_doc = segments[:, None] == segments[None, :]
    return same_doc & (key_places[None, :] <= query_places[:, None])


def block_scores(query_block, key_part, allowed, scaling):
    scores = (
        jnp.einsum("qkgd,pkd->kgqp", query_block, key_part, preferred_element_type=jnp.float32)
        * scaling
    )
    return jnp.where(allowed, scores, -1e30)


def attention_forward(query_states, key_states, value_states, segments):
    length, head_count, head_dim = query_states.shape
    kv_count = key_states.shape[1]
    groups = head_count // kv_count
    window = min(512, length)
    scaling = head_dim ** (-0.5)
    query_block = query_states.reshape(window, kv_count, groups, head_dim)
    scores = block_scores(query_block, key_states, block_mask(segments, 0, window, window), scaling)
    highest = jnp.max(scores, axis=-1, keepdims=True)
    exponent = jnp.exp(scores - highest)
    summed = jnp.sum(exponent, axis=-1, keepdims=True)
    attn_probs = (exponent / summed).astype(jnp.bfloat16)
    mixture = jnp.einsum(
        "kgqp,pkd->qkgd", attn_probs, value_states, preferred_element_type=jnp.float32
    )
    outputs = mixture.reshape(window, head_count * head_dim)
    log_sums = [highest + jnp.log(summed)]
    return (outputs, log_sums)


def attention_backward(query_states, key_states, value_states, segments, log_sums, grad_mixture):
    length, head_count, head_dim = query_states.shape
    kv_count = key_states.shape[1]
    groups = head_count // kv_count
    window = min(512, length)
    scaling = head_dim ** (-0.5)
    grad_query = []
    grad_key = jnp.zeros(key_states.shape, jnp.float32)
    grad_value = jnp.zeros(value_states.shape, jnp.float32)
    for number, offset in enumerate(range(0, length, window)):
        key_reach = offset + window
        query_block = query_states.reshape(window, kv_count, groups, head_dim)
        scores = block_scores(
            query_block, key_states, block_mask(segments, offset, window, key_reach), scaling
        )
        attn_probs = jnp.exp(scores - log_sums[number])
        grad_block = grad_mixture.reshape(window, kv_count, groups, head_dim)
        grad_probs = jnp.einsum(
            "qkgd,pkd->kgqp", grad_block, value_states, preferred_element_type=jnp.float32
        )
        grad_value = grad_value.at[:key_reach].add(
            jnp.einsum(
                "kgqp,qkgd->pkd",
                attn_probs.astype(jnp.bfloat16),
                grad_block,
                preferred_element_type=jnp.float32,
            )
        )
        centered = jnp.sum(attn_probs * grad_probs, axis=-1, keepdims=True)
        grad_scores = (attn_probs * (grad_probs - centered)).astype(jnp.bfloat16)
        query_part = jnp.einsum(
            "kgqp,pkd->qkgd", grad_scores, key_states, preferred_element_type=jnp.float32
        )
        grad_query.append(query_part.reshape(window, head_count, head_dim) * scaling)
        grad_key = grad_key.at[:key_reach].add(
            jnp.einsum(
                "kgqp,qkgd->pkd", grad_scores, query_block, preferred_element_type=jnp.float32
            )
            * scaling
        )
    return (grad_query[0], grad_key, grad_value)


def local(
    tokens,
    attn_gain,
    w_query,
    w_key,
    w_value,
    w_out,
    mlp_gain,
    w_gate,
    w_up,
    w_down,
    segment_ids,
    cotangent,
):
    length = tokens.shape[0]
    inputs = tokens.astype(jnp.float32)
    cosine, sine_table = rotary(positions(segment_ids, length)[0])
    gain_one, query_full, key_full, value_full, out_full = (
        lax.all_gather(attn_gain, "dp", axis=0, tiled=True),
        lax.all_gather(w_query, "dp", axis=0, tiled=True),
        lax.all_gather(w_key, "dp", axis=0, tiled=True),
        lax.all_gather(w_value, "dp", axis=0, tiled=True),
        lax.all_gather(w_out, "dp", axis=1, tiled=True),
    )
    root_one = inv_root(inputs)
    normed = (inputs * root_one * gain_one.astype(jnp.float32)).astype(jnp.bfloat16)
    head_count = query_full.shape[1] // HEAD_DIM
    kv_count = key_full.shape[1] // HEAD_DIM
    query_pre = jnp.dot(normed, query_full, preferred_element_type=jnp.float32)
    key_pre = jnp.dot(normed, key_full, preferred_element_type=jnp.float32)
    value_states = jnp.dot(normed, value_full, preferred_element_type=jnp.float32).astype(
        jnp.bfloat16
    )
    query_states = rotate(
        query_pre.reshape(length, head_count, HEAD_DIM), cosine, sine_table
    ).astype(jnp.bfloat16)
    key_states = rotate(key_pre.reshape(length, kv_count, HEAD_DIM), cosine, sine_table).astype(
        jnp.bfloat16
    )
    value_states = value_states.reshape(length, kv_count, HEAD_DIM)
    mixture, log_sums = attention_forward(query_states, key_states, value_states, segment_ids)
    mixture = mixture.astype(jnp.bfloat16)
    attn_part = jnp.dot(mixture, out_full, preferred_element_type=jnp.float32)
    hidden = inputs + lax.psum(attn_part, "tensor")
    gain_two, gate_full, up_full, down_full = (
        lax.all_gather(mlp_gain, "dp", axis=0, tiled=True),
        lax.all_gather(w_gate, "dp", axis=0, tiled=True),
        lax.all_gather(w_up, "dp", axis=0, tiled=True),
        lax.all_gather(w_down, "dp", axis=1, tiled=True),
    )
    root_two = inv_root(hidden)
    normed_two = (hidden * root_two * gain_two.astype(jnp.float32)).astype(jnp.bfloat16)
    gate_proj = jnp.dot(normed_two, gate_full, preferred_element_type=jnp.float32)
    up_proj = jnp.dot(normed_two, up_full, preferred_element_type=jnp.float32)
    silu_value = gate_proj / (1.0 + jnp.exp(-gate_proj))
    sigmoid = 1.0 / (1.0 + jnp.exp(-gate_proj))
    activated = (silu_value * up_proj).astype(jnp.bfloat16)
    mlp_part = jnp.dot(activated, down_full, preferred_element_type=jnp.float32)
    output = hidden + lax.psum(mlp_part.astype(jnp.bfloat16), "tensor").astype(jnp.float32)
    gain_two, gate_full, up_full, down_full = (
        lax.all_gather(mlp_gain, "dp", axis=0, tiled=True),
        lax.all_gather(w_gate, "dp", axis=0, tiled=True),
        lax.all_gather(w_up, "dp", axis=0, tiled=True),
        lax.all_gather(w_down, "dp", axis=1, tiled=True),
    )
    grad_output = cotangent.astype(jnp.float32)
    grad_low = grad_output.astype(jnp.bfloat16)
    grad_act = jnp.einsum("td,fd->tf", grad_low, down_full, preferred_element_type=jnp.float32)
    grad_gate = (grad_act * up_proj * sigmoid * (1.0 + gate_proj * (1.0 - sigmoid))).astype(
        jnp.bfloat16
    )
    grad_up = (grad_act * silu_value).astype(jnp.bfloat16)
    partial_two = jnp.einsum(
        "tf,df->td", grad_gate, gate_full, preferred_element_type=jnp.float32
    ) + jnp.einsum("tf,df->td", grad_up, up_full, preferred_element_type=jnp.float32)
    grad_normed_two = lax.psum(partial_two, "tensor")
    gains_two = gain_two.astype(jnp.float32)
    grad_gain_two = jnp.sum(grad_normed_two * hidden * root_two, axis=0)
    grad_hidden = grad_output + norm_back(hidden, root_two, gains_two, grad_normed_two)
    grad_down = jnp.einsum("tf,td->fd", activated, grad_low, preferred_element_type=jnp.float32)
    grad_w_gate = jnp.einsum("td,tf->df", normed_two, grad_gate, preferred_element_type=jnp.float32)
    grad_w_up = jnp.einsum("td,tf->df", normed_two, grad_up, preferred_element_type=jnp.float32)
    mlp_grads = (
        lax.psum_scatter(grad_gain_two, "dp", scatter_dimension=0, tiled=True),
        lax.psum_scatter(grad_w_gate, "dp", scatter_dimension=0, tiled=True),
        lax.psum_scatter(grad_w_up, "dp", scatter_dimension=0, tiled=True),
        lax.psum_scatter(grad_down, "dp", scatter_dimension=1, tiled=True),
    )
    gain_one, query_full, key_full, value_full, out_full = (
        lax.all_gather(attn_gain, "dp", axis=0, tiled=True),
        lax.all_gather(w_query, "dp", axis=0, tiled=True),
        lax.all_gather(w_key, "dp", axis=0, tiled=True),
        lax.all_gather(w_value, "dp", axis=0, tiled=True),
        lax.all_gather(w_out, "dp", axis=1, tiled=True),
    )
    grad_hidden_low = grad_hidden.astype(jnp.bfloat16)
    grad_mixture = jnp.einsum(
        "td,cd->tc", grad_hidden_low, out_full, preferred_element_type=jnp.float32
    ).astype(jnp.bfloat16)
    grad_query_rot, grad_key_rot, grad_value = attention_backward(
        query_states, key_states, value_states, segment_ids, log_sums, grad_mixture
    )
    grad_query = (
        rotate(grad_query_rot, cosine, -sine_table)
        .reshape(length, head_count * HEAD_DIM)
        .astype(jnp.bfloat16)
    )
    grad_key = (
        rotate(grad_key_rot, cosine, -sine_table)
        .reshape(length, kv_count * HEAD_DIM)
        .astype(jnp.bfloat16)
    )
    grad_value_low = grad_value.reshape(length, kv_count * HEAD_DIM).astype(jnp.bfloat16)
    partial_one = jnp.einsum(
        "tc,dc->td", grad_query, query_full, preferred_element_type=jnp.float32
    )
    partial_one = partial_one + jnp.einsum(
        "tc,dc->td", grad_key, key_full, preferred_element_type=jnp.float32
    )
    partial_one = partial_one + jnp.einsum(
        "tc,dc->td", grad_value_low, value_full, preferred_element_type=jnp.float32
    )
    grad_normed = lax.psum(partial_one.astype(jnp.bfloat16), "tensor").astype(jnp.float32)
    gains_one = gain_one.astype(jnp.float32)
    grad_gain_one = jnp.sum(grad_normed * inputs * root_one, axis=0)
    grad_input = grad_hidden + norm_back(inputs, root_one, gains_one, grad_normed)
    grad_w_out = jnp.einsum(
        "tc,td->cd", mixture, grad_hidden_low, preferred_element_type=jnp.float32
    )
    grad_w_query = jnp.einsum("td,tc->dc", normed, grad_query, preferred_element_type=jnp.float32)
    grad_w_key = jnp.einsum("td,tc->dc", normed, grad_key, preferred_element_type=jnp.float32)
    grad_w_value = jnp.einsum(
        "td,tc->dc", normed, grad_value_low, preferred_element_type=jnp.float32
    )
    attn_grads = (
        lax.psum_scatter(grad_gain_one, "dp", scatter_dimension=0, tiled=True),
        lax.psum_scatter(grad_w_query, "dp", scatter_dimension=0, tiled=True),
        lax.psum_scatter(grad_w_key, "dp", scatter_dimension=0, tiled=True),
        lax.psum_scatter(grad_w_value, "dp", scatter_dimension=0, tiled=True),
        lax.psum_scatter(grad_w_out, "dp", scatter_dimension=1, tiled=True),
    )
    return (output.astype(jnp.bfloat16), grad_input) + tuple(attn_grads) + tuple(mlp_grads)


def solution(mesh):
    in_specs = (
        P("dp", None),
        P("dp"),
        P("dp", "tensor"),
        P("dp", "tensor"),
        P("dp", "tensor"),
        P("tensor", "dp"),
        P("dp"),
        P("dp", "tensor"),
        P("dp", "tensor"),
        P("tensor", "dp"),
        P("dp"),
        P("dp", None),
    )
    out_specs = (
        P("dp", None),
        P("dp", None),
        P("dp"),
        P("dp", "tensor"),
        P("dp", "tensor"),
        P("dp", "tensor"),
        P("tensor", "dp"),
        P("dp"),
        P("dp", "tensor"),
        P("dp", "tensor"),
        P("tensor", "dp"),
    )
    return jax.shard_map(local, mesh=mesh, in_specs=in_specs, out_specs=out_specs, check_vma=False)
```

profile of v0, /device:TPU:0, one launch (start us, length us, event | category | flops | bytes accessed | tf_op | source)
XLA Modules:
  0.0 2203.8 jit_solution(17762533838012826947)
XLA Ops:
  11.2 1.5 fusion.35
  13.3 23.1 %all-gather = bf16[16,1,128]{2,1,0:T(2,128)(2,1)S(1)} all-gather(bf16[1,1,128]{2,1,0:T(2,128)(2,1)} %bitcast.156), channel_id=1, replica_groups=mesh['dp'=16,'tensor'=2] {'dp'}, dimensions={0}, use_global_device_ids=true | all-gather | bytes 4352 | tf_op jit(solution)/shard_map/all_gather | solution.py:148
  36.5 1.6 fusion.12
  40.5 10.4 all-gather.12.cloned.1.call-done
  50.8 2.2 fusion.49
  53.1 36.8 %all-gather.10.cloned.1.call-done = bf16[2048,256]{1,0:T(8,128)(2,1)} async-done(((bf16[128,256]{1,0:T(8,128)(2,1)}), bf16[2048,256]{1,0:T(8,128)(2,1)}) %all-gather.10.cloned.1.call-update) | async-done | bytes 1048592 | tf_op jit(solution)/shard_map/all_gather | solution.py:151
  89.9 1.9 convolution_convert_fusion.2
  91.8 49.8 %all-gather.14.cloned.1.call-done = bf16[2048,1024]{1,0:T(8,128)(2,1)} async-done(((bf16[128,1024]{1,0:T(8,128)(2,1)}), bf16[2048,1024]{1,0:T(8,128)(2,1)}) %all-gather.14.cloned.1.call-update) | async-done | bytes 4194320 | tf_op jit(solution)/shard_map/all_gather | solution.py:149
  141.6 4.0 fusion.47
  147.2 1.3 copy-done
  149.4 45.9 %all-gather.16.cloned.1.call-done = bf16[1024,2048]{1,0:T(8,128)(2,1)} async-done(((bf16[1024,128]{1,0:T(8,128)(2,1)}), bf16[1024,2048]{1,0:T(8,128)(2,1)}) %all-gather.16.cloned.1.call-update) | async-done | bytes 4194320 | tf_op jit(solution)/shard_map/all_gather | solution.py:152
  195.3 4.8 fusion.53
  202.3 18.8 all-gather.1
  221.1 40.3 %all-reduce.8.cloned.1.call-done = f32[256,2048]{1,0:T(8,128)} async-done(((f32[256,2048]{1,0:T(8,128)}), f32[256,2048]{1,0:T(8,128)}) %all-reduce.8.cloned.1.call-update) | async-done | bytes 2097168 | tf_op jit(solution)/shard_map/psum | solution.py:173
  261.4 1.9 multiply_reduce_fusion.2
  264.5 126.0 %all-gather.20.cloned.1.call-done = bf16[2048,4096]{1,0:T(8,128)(2,1)} async-done(((bf16[128,4096]{1,0:T(8,128)(2,1)}), bf16[2048,4096]{1,0:T(8,128)(2,1)}) %all-gather.20.cloned.1.call-update) | async-done | bytes 16777232 | tf_op jit(solution)/shard_map/all_gather | solution.py:177
  390.5 12.6 fusion.55
  403.1 114.9 %all-gather.18.cloned.1.call-done = bf16[2048,4096]{1,0:T(8,128)(2,1)} async-done(((bf16[128,4096]{1,0:T(8,128)(2,1)}), bf16[2048,4096]{1,0:T(8,128)(2,1)}) %all-gather.18.cloned.1.call-update) | async-done | bytes 16777232 | tf_op jit(solution)/shard_map/all_gather | solution.py:176
  518.0 12.6 fusion.54
  530.6 118.4 %all-gather.22.cloned.1.call-done = bf16[4096,2048]{1,0:T(8,128)(2,1)} async-done(((bf16[4096,128]{1,0:T(8,128)(2,1)}), bf16[4096,2048]{1,0:T(8,128)(2,1)}) %all-gather.22.cloned.1.call-update) | async-done | bytes 16777232 | tf_op jit(solution)/shard_map/all_gather | solution.py:178
  649.0 13.7 multiply_convert_fusion
  662.7 12.2 fusion.56
  674.9 12.8 convolution_add_fusion.2
  688.6 12.6 convolution_convert_fusion
  701.2 47.8 %all-reduce.10.cloned.1.call-done = f32[256,2048]{1,0:T(8,128)} async-done(((f32[256,2048]{1,0:T(8,128)}), f32[256,2048]{1,0:T(8,128)}) %all-reduce.10.cloned.1.call-update) | async-done | bytes 2097168 | tf_op jit(solution)/shard_map/psum | solution.py:205
  749.0 2.9 multiply_reduce_fusion
  752.5 1.3 copy-done.3
  754.8 2.1 convolution_convert_fusion.1
  756.9 2.0 copy.44
  759.0 3.2 fusion.27
  766.6 1.4 copy-done.26
  770.6 1.5 fusion.6
  772.4 1.9 fusion.41
  774.4 1.9 fusion.43
  776.4 6.8 fusion.30
  783.3 5.7 fusion.45
  789.0 17.7 fusion.60
  807.0 17.6 fusion.59
  824.7 17.6 fusion.58
  844.2 1.9 fusion.18
  846.0 61.1 %all-reduce.2 = (f32[2048]{0:T(1024)S(1)}, f32[2048]{0:T(1024)S(1)}) all-reduce(f32[2048]{0:T(1024)S(1)} %get-tuple-element.53, f32[2048]{0:T(1024)S(1)} %copy-done.23), channel_id=2, replica_groups=mesh['dp'=16,'tensor'=2] {'dp'}, use_global_device_ids=true, to_apply=%region_14.15.clone | all-reduce | flops 4096 | bytes 32768
  908.4 4.6 fusion.9
  913.0 53.6 %reduce-scatter.10.cloned.1.call-done = f32[128,256]{1,0:T(8,128)} async-done(((f32[2048,256]{1,0:T(8,128)}), f32[128,256]{1,0:T(8,128)}) %reduce-scatter.10.cloned.1.call-update) | async-done | bytes 131088 | tf_op jit(solution)/shard_map/reduce_scatter | solution.py:267
  966.6 109.0 %reduce-scatter.14.cloned.1.call-done = f32[1024,128]{1,0:T(8,128)} async-done(((f32[1024,2048]{1,0:T(8,128)}), f32[1024,128]{1,0:T(8,128)}) %reduce-scatter.14.cloned.1.call-update) | async-done | bytes 524304 | tf_op jit(solution)/shard_map/reduce_scatter | solution.py:269
  1075.6 109.4 %reduce-scatter.8.cloned.1.call-done = f32[128,1024]{1,0:T(8,128)} async-done(((f32[2048,1024]{1,0:T(8,128)}), f32[128,1024]{1,0:T(8,128)}) %reduce-scatter.8.cloned.1.call-update) | async-done | bytes 524304 | tf_op jit(solution)/shard_map/reduce_scatter | solution.py:266
  1185.0 337.7 %reduce-scatter.20.cloned.1.call-done = f32[4096,128]{1,0:T(8,128)} async-done(((f32[4096,2048]{1,0:T(8,128)}), f32[4096,128]{1,0:T(8,128)}) %reduce-scatter.20.cloned.1.call-update) | async-done | bytes 2097168 | tf_op jit(solution)/shard_map/reduce_scatter | solution.py:216
  1522.6 337.1 %reduce-scatter.18.cloned.1.call-done = f32[128,4096]{1,0:T(8,128)} async-done(((f32[2048,4096]{1,0:T(8,128)}), f32[128,4096]{1,0:T(8,128)}) %reduce-scatter.18.cloned.1.call-update) | async-done | bytes 2097168 | tf_op jit(solution)/shard_map/reduce_scatter | solution.py:215
  1859.7 337.1 %reduce-scatter.16.cloned.1.call-done = f32[128,4096]{1,0:T(8,128)} async-done(((f32[2048,4096]{1,0:T(8,128)}), f32[128,4096]{1,0:T(8,128)}) %reduce-scatter.16.cloned.1.call-update) | async-done | bytes 2097168 | tf_op jit(solution)/shard_map/reduce_scatter | solution.py:214
  (128 shorter events, 25.4 us)
Async XLA Ops:
  7.2 43.7 %all-gather.12.cloned.1.call-start = ((), (), s32[]{:S(2)}) async-start(), calls=%async_computation.8 | async-start | bytes 1114112 | tf_op jit(solution)/shard_map/all_gather | solution.py:150
  7.9 82.0 %all-gather.10.cloned.1.call-start = ((), (), s32[]{:S(2)}) async-start(), calls=%async_computation.7 | async-start | bytes 1114112 | tf_op jit(solution)/shard_map/all_gather | solution.py:151
  8.7 132.9 %all-gather.14.cloned.1.call-start = ((), (), s32[]{:S(2)}) async-start(), calls=%async_computation.9 | async-start | bytes 4456448 | tf_op jit(solution)/shard_map/all_gather | solution.py:149
  9.4 185.9 %all-gather.16.cloned.1.call-start = ((), (), s32[]{:S(2)}) async-start(), calls=%async_computation.10 | async-start | bytes 4456448 | tf_op jit(solution)/shard_map/all_gather | solution.py:152
  10.0 251.4 %all-reduce.8.cloned.1.call-start = ((), (), s32[]{:S(2)}) async-start(), calls=%async_computation.11 | async-start | bytes 4194304 | tf_op jit(solution)/shard_map/psum | solution.py:173
  36.5 53.4 %copy-start.2 = (bf16[256,2048]{1,0:T(8,128)(2,1)S(1)}, bf16[256,2048]{1,0:T(8,128)(2,1)}, u32[]{:S(2)}) copy-start(bf16[256,2048]{1,0:T(8,128)(2,1)} %param.20) | copy-start | bytes 3145732
  40.5 105.1 %copy-start.13 = (f32[256,32]{0,1:T(8,128)}, f32[256,32]{0,1:T(8,128)S(1)}, u32[]{:S(2)}) copy-start(f32[256,32]{0,1:T(8,128)S(1)} %get-tuple-element.74) | copy-start | bytes 98308
  53.1 92.7 %copy-start.17 = (bf16[256,4,32]{0,2,1:T(8,128)(2,1)}, bf16[256,4,32]{0,2,1:T(8,128)(2,1)S(1)}, u32[]{:S(2)}) copy-start(bf16[256,4,32]{0,2,1:T(8,128)(2,1)S(1)} %get-tuple-element.70) | copy-start | bytes 196612
  53.1 92.7 %copy-start.19 = (bf16[256,4,32]{0,2,1:T(8,128)(2,1)}, bf16[256,4,32]{0,2,1:T(8,128)(2,1)S(1)}, u32[]{:S(2)}) copy-start(bf16[256,4,32]{0,2,1:T(8,128)(2,1)S(1)} %get-tuple-element.71) | copy-start | bytes 196612
  91.8 55.4 %copy-start.21 = (bf16[256,256]{0,1:T(8,128)(2,1)}, bf16[256,256]{0,1:T(8,128)(2,1)S(1)}, u32[]{:S(2)}) copy-start(bf16[256,256]{0,1:T(8,128)(2,1)S(1)} %convolution_convert_fusion.2) | copy-start | bytes 393220
  145.7 0.8 copy-start.10
  146.6 1.9 copy-start
  149.4 50.7 %copy-start.12 = (bf16[4,64,4,256]{3,1,2,0:T(8,128)(2,1)}, bf16[4,64,4,256]{3,1,2,0:T(8,128)(2,1)S(1)}, u32[]{:S(2)}) copy-start(bf16[4,64,4,256]{3,1,2,0:T(8,128)(2,1)S(1)} %fusion.21) | copy-start | bytes 1572868
  200.1 2.1 copy-start.25
  200.1 190.4 %all-gather.20.cloned.1.call-start = ((), (), s32[]{:S(2)}) async-start(), calls=%async_computation.13 | async-start | bytes 17825792 | tf_op jit(solution)/shard_map/all_gather | solution.py:177
  200.7 317.3 %all-gather.18.cloned.1.call-start = ((), (), s32[]{:S(2)}) async-start(), calls=%async_computation.12 | async-start | bytes 17825792 | tf_op jit(solution)/shard_map/all_gather | solution.py:176
  201.5 447.5 %all-gather.22.cloned.1.call-start = ((), (), s32[]{:S(2)}) async-start(), calls=%async_computation.14 | async-start | bytes 17825792 | tf_op jit(solution)/shard_map/all_gather | solution.py:178
  202.2 546.8 %all-reduce.10.cloned.1.call-start = ((), (), s32[]{:S(2)}) async-start(), calls=%async_computation.15 | async-start | bytes 4194304 | tf_op jit(solution)/shard_map/psum | solution.py:205
  687.8 156.4 %all-reduce.12.cloned.1.call-start = ((), (), s32[]{:S(2)}) async-start(), calls=%async_computation.23 | async-start | bytes 4194304 | tf_op jit(solution)/shard_map/psum | solution.py:188
  749.0 2.9 copy-start.4
  749.0 2.9 copy-start.6
  751.9 2.9 copy-start.27
  752.5 1.3 copy-start.3
  759.0 3.6 copy-start.1
  759.0 3.7 copy-start.5
  759.0 3.7 copy-start.16
  759.0 3.8 copy-start.22
  763.7 1.0 copy-start.11
  764.7 0.8 copy-start.18
  764.7 0.9 copy-start.20
  765.6 0.8 copy-start.14
  765.6 0.8 copy-start.15
  765.6 2.4 copy-start.26
  766.6 2.7 copy-start.7
  768.0 1.3 copy-start.8
  769.3 1.2 copy-start.9
  772.1 140.9 %reduce-scatter.12.cloned.1.call-start = ((), (), s32[]{:S(2)}) async-start(), calls=%async_computation.18 | async-start | bytes 2228224 | tf_op jit(solution)/shard_map/reduce_scatter | solution.py:268
  774.3 192.2 %reduce-scatter.10.cloned.1.call-start = ((), (), s32[]{:S(2)}) async-start(), calls=%async_computation.17 | async-start | bytes 2228224 | tf_op jit(solution)/shard_map/reduce_scatter | solution.py:267
  776.3 299.3 %reduce-scatter.14.cloned.1.call-start = ((), (), s32[]{:S(2)}) async-start(), calls=%async_computation.19 | async-start | bytes 8912896 | tf_op jit(solution)/shard_map/reduce_scatter | solution.py:269
  783.2 401.7 %reduce-scatter.8.cloned.1.call-start = ((), (), s32[]{:S(2)}) async-start(), calls=%async_computation.16 | async-start | bytes 8912896 | tf_op jit(solution)/shard_map/reduce_scatter | solution.py:266
  789.0 733.6 %reduce-scatter.20.cloned.1.call-start = ((), (), s32[]{:S(2)}) async-start(), calls=%async_computation.22 | async-start | bytes 35651584 | tf_op jit(solution)/shard_map/reduce_scatter | solution.py:216
  806.7 1053.0 %reduce-scatter.18.cloned.1.call-start = ((), (), s32[]{:S(2)}) async-start(), calls=%async_computation.21 | async-start | bytes 35651584 | tf_op jit(solution)/shard_map/reduce_scatter | solution.py:215
  824.7 1372.2 %reduce-scatter.16.cloned.1.call-start = ((), (), s32[]{:S(2)}) async-start(), calls=%async_computation.20 | async-start | bytes 35651584 | tf_op jit(solution)/shard_map/reduce_scatter | solution.py:214
  842.3 0.7 copy-start.28
  842.3 3.8 copy-start.23
  842.3 66.1 %copy-start.24 = (f32[256]{0:T(256)S(1)}, f32[256]{0:T(256)}, u32[]{:S(2)}) copy-start(f32[256]{0:T(256)} %get-tuple-element.75) | copy-start | bytes 3076
Sparse Core Ops, SparseCore 0:
  10.2 40.6 all-gather.11
  53.0 36.8 all-gather.9
  92.1 49.4 all-gather.13
  143.6 51.6 all-gather.15
  200.2 61.0 all-reduce.7
  263.6 126.8 all-gather.19
  392.9 125.0 all-gather.17
  520.4 128.5 all-gather.21
  687.9 61.0 all-reduce.9
  772.2 63.0 all-reduce.11
  840.1 61.6 reduce-scatter.11
  906.0 60.5 reduce-scatter.9
  971.7 103.7 reduce-scatter.13
  1080.6 104.2 reduce-scatter.7
  1190.2 332.3 reduce-scatter.19
  1527.9 331.7 reduce-scatter.17
  1865.0 331.8 reduce-scatter.15
where the time goes:
time: 2210 us; the launch traced here: 2200 us
  waiting for transfers between devices  1880 us (85%)
  matrix products  171 us (8%)
  blocking collectives  103 us (5%)
    reduce_scatter x1, waiting for transfers between devices, local(): lax.psum_scatter(grad_down, 'dp', scatter_dimension=1, tiled=True)  338 us
    reduce_scatter x1, waiting for transfers between devices, local(): lax.psum_scatter(grad_w_gate, 'dp', scatter_dimension=0, tiled=True)  337 us
    reduce_scatter x1, waiting for transfers between devices, local(): lax.psum_scatter(grad_w_up, 'dp', scatter_dimension=0, tiled=True)  337 us
    all_gather x1, waiting for transfers between devices, local(): lax.all_gather(w_up, 'dp', axis=0, tiled=True)  126 us
    all_gather x1, waiting for transfers between devices, local(): lax.all_gather(w_down, 'dp', axis=1, tiled=True)  118 us
    all_gather x1, waiting for transfers between devices, local(): lax.all_gather(w_gate, 'dp', axis=0, tiled=True)  115 us
    reduce_scatter x1, waiting for transfers between devices, local(): lax.psum_scatter(grad_w_query, 'dp', scatter_dimension=0, tiled=True)  109 us
    reduce_scatter x1, waiting for transfers between devices, local(): lax.psum_scatter(grad_w_out, 'dp', scatter_dimension=1, tiled=True)  109 us
  transfers between devices with their start and end apart: 17, of which 15 were waited for; matrix products, arithmetic and copies ran while one was open for 6% of the time, Pallas kernels for 0%

commit v1 on v0

v1 whole, which is shorter than its diff:
```python
import functools

import jax
import jax.numpy as jnp
from jax import lax
from jax.experimental import pallas as pl
from jax.experimental.pallas import tpu as pltpu
from jax.sharding import PartitionSpec as P

HEAD_DIM = 64
EPSILON = 1e-05
THETA = 500000.0
MESH = pl.DeviceIdType.MESH
ANY = pl.BlockSpec(memory_space=pl.ANY)
VMEM = pl.BlockSpec(memory_space=pltpu.VMEM)
F32 = jnp.float32
BF16 = jnp.bfloat16
DMA = pltpu.SemaphoreType.DMA


class Place:
    def __init__(self, mid):
        self.mid = mid
        self.d = lax.axis_index("dp")
        self.x = lax.axis_index("tensor")
        self.c = self.d % 2
        self.m = (self.d // 2) % mid
        self.z = self.d // (2 * mid)
        self.lo = self.z % 2

    def dp(self, z, m, c):
        return (z * self.mid + m) * 2 + c

    def peer(self, k):
        return xor(self.z, k // 2), xor(self.c, k % 2)

    def other_m(self, j):
        return (self.m + 1 + j) % self.mid


def xor(a, k):
    if k == 0:
        return a
    low = a % 2
    high = a // 2
    if k % 2:
        low = 1 - low
    if k // 2:
        high = 1 - high
    return high * 2 + low


def remote(src, dst, send, recv, device):
    copy = pltpu.make_async_remote_copy(
        src_ref=src, dst_ref=dst, send_sem=send, recv_sem=recv, device_id=device, device_id_type=MESH
    )
    return copy


def greet(devices):
    barrier = pltpu.get_barrier_semaphore()
    for device in devices:
        pl.semaphore_signal(barrier, inc=1, device_id=device, device_id_type=MESH)
    pl.semaphore_wait(barrier, len(devices))


def gather_kernel(
    mid, tok, cot, ids, wa, wm, tokg, cotg, idsg, fa, fm,
    tok_s, tok_r, ids_s, ids_r, a_s, a_r, af_s, m_s, m_r, mf_s, loc,
):
    p = Place(mid)
    half = tok.shape[0] // 2
    greet(
        [(p.dp(z, p.m, c), p.x) for z, c in map(p.peer, range(1, 8))]
        + [(p.dp(p.z, p.other_m(j), p.c), p.x) for j in range(mid - 1)]
        + [(p.d, 1 - p.x)]
    )
    seq = p.lo * 2 + p.c
    z_near = (p.dp(xor(p.z, 1), p.m, p.c), p.x)
    c_near = (p.dp(p.z, p.m, 1 - p.c), p.x)
    x_near = (p.d, 1 - p.x)
    mine = pl.ds(p.x * half, half)
    theirs = pl.ds((1 - p.x) * half, half)
    far_seq = (1 - p.lo) * 2 + p.c
    sends = []

    def go(copy):
        copy.start()
        sends.append(copy)

    locals_ = []

    def here(src, dst, number):
        copy = pltpu.make_async_copy(src, dst, loc.at[number])
        copy.start()
        locals_.append(copy)

    for n, (src, dst) in enumerate(((tok, tokg), (cot, cotg))):
        go(remote(src.at[mine], dst.at[seq, mine], tok_s.at[n, 0], tok_r.at[n, 0], z_near))
        go(remote(src, dst.at[seq], tok_s.at[n, 1], tok_r.at[n, 1], c_near))
        here(src, dst.at[seq], n)
        if n == 0:
            go(remote(ids, idsg.at[seq], ids_s.at[0], ids_r.at[0], z_near))
            go(remote(ids, idsg.at[seq], ids_s.at[1], ids_r.at[1], c_near))
            here(ids, idsg.at[seq], 2)
            block = p.lo * 2 + p.c
            here(wa.at[block], fa.at[p.d], 3)
            here(wm.at[block], fm.at[p.d], 4)
            for src_w, dst_w, s_sem, r_sem, f_sem in ((wa, fa, a_s, a_r, af_s), (wm, fm, m_s, m_r, mf_s)):
                for k in range(7, 0, -1):
                    z, c = p.peer(k)
                    go(
                        remote(
                            src_w.at[(z % 2) * 2 + c], dst_w.at[p.d], s_sem.at[k], r_sem.at[p.d],
                            (p.dp(z, p.m, c), p.x),
                        )
                    )
                for j in range(mid - 1):
                    go(
                        remote(
                            src_w.at[block], dst_w.at[p.d], f_sem.at[0, j], r_sem.at[p.d],
                            (p.dp(p.z, p.other_m(j), p.c), p.x),
                        )
                    )

    def arrived(dst, sem):
        pltpu.make_async_copy(dst, dst, sem).wait()

    arrived(idsg.at[far_seq], ids_r.at[0])
    go(remote(idsg.at[far_seq], idsg.at[far_seq], ids_s.at[2], ids_r.at[2], c_near))
    for n, dst in enumerate((tokg, cotg)):
        arrived(dst.at[far_seq, mine], tok_r.at[n, 0])
        go(remote(dst.at[far_seq, mine], dst.at[far_seq, mine], tok_s.at[n, 2], tok_r.at[n, 2], x_near))
        go(remote(dst.at[far_seq, mine], dst.at[far_seq, mine], tok_s.at[n, 3], tok_r.at[n, 3], c_near))
    for n, dst in enumerate((tokg, cotg)):
        arrived(dst.at[far_seq, theirs], tok_r.at[n, 2])
        go(remote(dst.at[far_seq, theirs], dst.at[far_seq, theirs], tok_s.at[n, 4], tok_r.at[n, 4], c_near))
    for dst_w, r_sem, f_sem in ((fa, a_r, af_s), (fm, m_r, mf_s)):
        for k in range(7, 0, -1):
            z, c = p.peer(k)
            src_d = p.dp(z, p.m, c)
            arrived(dst_w.at[src_d], r_sem.at[src_d])
            for j in range(mid - 1):
                go(
                    remote(
                        dst_w.at[src_d], dst_w.at[src_d], f_sem.at[k, j], r_sem.at[src_d],
                        (p.dp(p.z, p.other_m(j), p.c), p.x),
                    )
                )
    c_seq = p.lo * 2 + 1 - p.c
    cc_seq = (1 - p.lo) * 2 + 1 - p.c
    arrived(idsg.at[c_seq], ids_r.at[1])
    arrived(idsg.at[cc_seq], ids_r.at[2])
    for n, dst in enumerate((tokg, cotg)):
        arrived(dst.at[c_seq], tok_r.at[n, 1])
        arrived(dst.at[cc_seq, mine], tok_r.at[n, 3])
        arrived(dst.at[cc_seq, theirs], tok_r.at[n, 4])
    for dst_w, r_sem in ((fa, a_r), (fm, m_r)):
        for k in range(8):
            z, c = p.peer(k)
            for j in range(mid - 1):
                src_d = p.dp(z, p.other_m(j), c)
                arrived(dst_w.at[src_d], r_sem.at[src_d])
    for copy in locals_:
        copy.wait()
    for copy in sends:
        copy.wait_send()


def gather(mid, tok, cot, ids, wa, wm):
    n = mid * 8
    return pl.pallas_call(
        functools.partial(gather_kernel, mid),
        out_shape=(
            jax.ShapeDtypeStruct((4,) + tok.shape, BF16),
            jax.ShapeDtypeStruct((4,) + cot.shape, BF16),
            jax.ShapeDtypeStruct((4,) + ids.shape, ids.dtype),
            jax.ShapeDtypeStruct((n,) + wa.shape[1:], BF16),
            jax.ShapeDtypeStruct((n,) + wm.shape[1:], BF16),
        ),
        in_specs=[ANY] * 5,
        out_specs=(ANY,) * 5,
        scratch_shapes=[
            DMA((2, 5)), DMA((2, 5)), DMA((3,)), DMA((3,)),
            DMA((8,)), DMA((n,)), DMA((8, mid - 1)),
            DMA((8,)), DMA((n,)), DMA((8, mid - 1)),
            DMA((5,)),
        ],
        compiler_params=pltpu.CompilerParams(collective_id=0, has_side_effects=True),
    )(tok, cot, ids, wa, wm)


def scatter_kernel(mid, rows, g, out, ybuf, sums, y_s, y_r, z_s, z_r, loc):
    p = Place(mid)
    greet(
        [(p.dp(z, p.m, c), p.x) for z, c in map(p.peer, range(1, 8))]
        + [(p.dp(p.z, p.other_m(j), p.c), p.x) for j in range(mid - 1)]
    )
    sends = []
    order = list(range(7, -1, -1))
    for k in order:
        z, c = p.peer(k)
        for j in range(mid - 1):
            m = p.other_m(j)
            copy = remote(
                g.at[p.dp(z, m, c)], ybuf.at[mid - 2 - j, k], y_s.at[k, j], y_r.at[k, mid - 2 - j],
                (p.dp(p.z, m, p.c), p.x),
            )
            copy.start()
            sends.append(copy)
    step = 16
    for k in order:
        z, c = p.peer(k)
        for j in range(mid - 1):
            pltpu.make_async_copy(ybuf.at[j, k], ybuf.at[j, k], y_r.at[k, j]).wait()
        own = p.dp(z, p.m, c)

        def add(i, carry):
            at = pl.ds(pl.multiple_of(i * step, step), step)
            total = g[own, at, :].astype(F32)
            for j in range(mid - 1):
                total = total + ybuf[j, k, at, :].astype(F32)
            sums[k, at, :] = total.astype(BF16)
            return carry

        lax.fori_loop(0, rows // step, add, 0)
        me = p.z * 2 + p.c
        if k == 0:
            copy = pltpu.make_async_copy(sums.at[k], out.at[me], loc)
            copy.start()
            copy.wait()
        else:
            copy = remote(sums.at[k], out.at[me], z_s.at[k], z_r.at[me], (p.dp(z, p.m, c), p.x))
            copy.start()
            sends.append(copy)
    for k in range(1, 8):
        z, c = p.peer(k)
        src = z * 2 + c
        pltpu.make_async_copy(out.at[src], out.at[src], z_r.at[src]).wait()
    for copy in sends:
        copy.wait_send()


def scatter(mid, g):
    n, rows, width = g.shape
    return pl.pallas_call(
        functools.partial(scatter_kernel, mid, rows),
        out_shape=jax.ShapeDtypeStruct((8, rows, width), BF16),
        in_specs=[VMEM],
        out_specs=ANY,
        scratch_shapes=[
            pltpu.VMEM((mid - 1, 8, rows, width), BF16),
            pltpu.VMEM((8, rows, width), BF16),
            DMA((8, mid - 1)), DMA((8, mid - 1)), DMA((8,)), DMA((8,)), DMA,
        ],
        compiler_params=pltpu.CompilerParams(
            collective_id=1, has_side_effects=True, vmem_limit_bytes=56 << 20
        ),
    )(g)


def group_devices(p):
    far = xor(p.z, 1)
    return {
        (0, 1): (p.d, 1 - p.x),
        (1, 0): (p.dp(far, p.m, p.c), p.x),
        (1, 1): (p.dp(far, p.m, p.c), 1 - p.x),
    }, (p.dp(p.z, p.m, 1 - p.c), p.x)


def reduce_to_owner(p, part, abuf, sums, bbuf, sems, sends, finish):
    a_s, a_r, b_s, b_r = sems
    chips, sibling = group_devices(p)
    order = ((1, 1), (0, 1), (1, 0), (0, 0))
    for n, (fz, fx) in enumerate(order):
        lo, x = xor(p.lo, fz), xor(p.x, fx)
        copy = remote(part.at[(lo * 2 + 1 - p.c) * 2 + x], abuf.at[n], a_s.at[n], a_r.at[n], sibling)
        copy.start()
        sends.append(copy)
    rows = part.shape[1]
    step = 16
    for n, (fz, fx) in enumerate(order):
        lo, x = xor(p.lo, fz), xor(p.x, fx)
        own = (lo * 2 + p.c) * 2 + x
        pltpu.make_async_copy(abuf.at[n], abuf.at[n], a_r.at[n]).wait()
        if n == 3:
            break

        def add(i, carry):
            at = pl.ds(pl.multiple_of(i * step, step), step)
            sums[n, at, :] = (part[own, at, :].astype(F32) + abuf[n, at, :].astype(F32)).astype(BF16)
            return carry

        lax.fori_loop(0, rows // step, add, 0)
        copy = remote(sums.at[n], bbuf.at[n], b_s.at[n], b_r.at[n], chips[(fz, fx)])
        copy.start()
        sends.append(copy)
    mine = (p.lo * 2 + p.c) * 2 + p.x
    for n in range(3):
        pltpu.make_async_copy(bbuf.at[n], bbuf.at[n], b_r.at[n]).wait()

    def last(i, carry):
        at = pl.ds(pl.multiple_of(i * step, step), step)
        total = part[mine, at, :].astype(F32) + abuf[3, at, :].astype(F32)
        for n in range(3):
            total = total + bbuf[n, at, :].astype(F32)
        finish(at, total)
        return carry

    lax.fori_loop(0, rows // step, last, 0)


def share_with_group(p, gathered, sems, sends):
    s, r = sems
    chips, sibling = group_devices(p)
    mine = (p.lo * 2 + p.c) * 2 + p.x
    order = ((1, 1), (0, 1), (1, 0))
    for n, flips in enumerate(order):
        copy = remote(gathered.at[mine], gathered.at[mine], s.at[n], r.at[n], chips[flips])
        copy.start()
        sends.append(copy)
    copy = remote(gathered.at[mine], gathered.at[mine], s.at[3], r.at[3], sibling)
    copy.start()
    sends.append(copy)
    for n, (fz, fx) in enumerate(order):
        at = (xor(p.lo, fz) * 2 + p.c) * 2 + xor(p.x, fx)
        pltpu.make_async_copy(gathered.at[at], gathered.at[at], r.at[n]).wait()
        copy = remote(gathered.at[at], gathered.at[at], s.at[4 + n], r.at[4 + n], sibling)
        copy.start()
        sends.append(copy)
    for n, (fz, fx) in enumerate(order + ((0, 0),)):
        at = (xor(p.lo, fz) * 2 + 1 - p.c) * 2 + xor(p.x, fx)
        number = 3 if n == 3 else 4 + n
        pltpu.make_async_copy(gathered.at[at], gathered.at[at], r.at[number]).wait()


def group_greet(p):
    chips, sibling = group_devices(p)
    greet(list(chips.values()) + [sibling])


def forward_mid_kernel(mid, part, x, gain, hidden, normed, abuf, sums, bbuf, a_s, a_r, b_s, b_r, g_s, g_r):
    p = Place(mid)
    group_greet(p)
    sends = []
    mine = (p.lo * 2 + p.c) * 2 + p.x

    def finish(at, total):
        value = x[at, :].astype(F32) + total
        hidden[at, :] = value
        root = lax.rsqrt(jnp.mean(value * value, axis=-1, keepdims=True) + EPSILON)
        normed[mine, at, :] = (value * root * gain[...].astype(F32)).astype(BF16)

    reduce_to_owner(p, part, abuf, sums, bbuf, (a_s, a_r, b_s, b_r), sends, finish)
    share_with_group(p, normed, (g_s, g_r), sends)
    for copy in sends:
        copy.wait_send()


def rs_scratch(rows, width):
    return [
        pltpu.VMEM((4, rows, width), BF16),
        pltpu.VMEM((3, rows, width), BF16),
        pltpu.VMEM((3, rows, width), BF16),
        DMA((4,)), DMA((4,)), DMA((3,)), DMA((3,)),
    ]


def forward_mid(mid, part, x, gain):
    eight, rows, width = part.shape
    return pl.pallas_call(
        functools.partial(forward_mid_kernel, mid),
        out_shape=(
            jax.ShapeDtypeStruct((rows, width), F32),
            jax.ShapeDtypeStruct((eight, rows, width), BF16),
        ),
        in_specs=[VMEM] * 3,
        out_specs=(VMEM,) * 2,
        scratch_shapes=rs_scratch(rows, width) + [DMA((7,)), DMA((7,))],
        compiler_params=pltpu.CompilerParams(
            collective_id=2, has_side_effects=True, vmem_limit_bytes=56 << 20
        ),
    )(part, x, gain)


def backward_mid_kernel(
    mid, part, out_part, hid, cot, gain, grad_hidden, low, output, gain_grad,
    abuf, sums, bbuf, a_s, a_r, b_s, b_r, abuf2, sums2, bbuf2, a_s2, a_r2, b_s2, b_r2, g_s, g_r, o_s, o_r,
):
    p = Place(mid)
    group_greet(p)
    sends = []
    mine = (p.lo * 2 + p.c) * 2 + p.x
    rows, width = hid.shape
    gain_grad[...] = jnp.zeros_like(gain_grad)

    def finish(at, total):
        value = hid[at, :]
        root = lax.rsqrt(jnp.mean(value * value, axis=-1, keepdims=True) + EPSILON)
        scaled = total * gain[...].astype(F32)
        back = root * scaled - value * root**3 * jnp.mean(value * scaled, axis=-1, keepdims=True)
        grads = cot[at, :].astype(F32) + back
        grad_hidden[at, :] = grads
        low[mine, at, :] = grads.astype(BF16)
        term = total * value * root
        gain_grad[...] += term[:8] + term[8:]

    reduce_to_owner(p, part, abuf, sums, bbuf, (a_s, a_r, b_s, b_r), sends, finish)
    share_with_group(p, low, (g_s, g_r), sends)

    def finish_out(at, total):
        there = pl.ds(pl.multiple_of(p.x * rows + at.start, 16), 16)
        output[there, :] = (hid[at, :] + total).astype(BF16)

    reduce_to_owner(p, out_part, abuf2, sums2, bbuf2, (a_s2, a_r2, b_s2, b_r2), sends, finish_out)
    half = pl.ds(pl.multiple_of(p.x * rows, rows), rows)
    copy = remote(output.at[half], output.at[half], o_s, o_r, (p.d, 1 - p.x))
    copy.start()
    sends.append(copy)
    copy.wait_recv()
    for copy in sends:
        copy.wait_send()


def backward_mid(mid, part, out_part, hid, cot, gain):
    eight, rows, width = part.shape
    return pl.pallas_call(
        functools.partial(backward_mid_kernel, mid),
        out_shape=(
            jax.ShapeDtypeStruct((rows, width), F32),
            jax.ShapeDtypeStruct((eight, rows, width), BF16),
            jax.ShapeDtypeStruct((2 * rows, width), BF16),
            jax.ShapeDtypeStruct((8, width), F32),
        ),
        in_specs=[VMEM] * 5,
        out_specs=(VMEM,) * 4,
        scratch_shapes=rs_scratch(rows, width) * 2 + [DMA((7,)), DMA((7,)), DMA, DMA],
        compiler_params=pltpu.CompilerParams(
            collective_id=3, has_side_effects=True, vmem_limit_bytes=56 << 20
        ),
    )(part, out_part, hid, cot, gain)


def last_kernel(
    mid, part, grad_hidden, x, gain, result, gain_grad, abuf, sums, bbuf, a_s, a_r, b_s, b_r, o_s, o_r
):
    p = Place(mid)
    group_greet(p)
    sends = []
    rows, width = x.shape
    gain_grad[...] = jnp.zeros_like(gain_grad)

    def finish(at, total):
        value = x[at, :].astype(F32)
        root = lax.rsqrt(jnp.mean(value * value, axis=-1, keepdims=True) + EPSILON)
        scaled = total * gain[...].astype(F32)
        back = root * scaled - value * root**3 * jnp.mean(value * scaled, axis=-1, keepdims=True)
        there = pl.ds(pl.multiple_of(p.x * rows + at.start, 16), 16)
        result[there, :] = (grad_hidden[at, :] + back).astype(BF16)
        term = total * value * root
        gain_grad[...] += term[:8] + term[8:]

    reduce_to_owner(p, part, abuf, sums, bbuf, (a_s, a_r, b_s, b_r), sends, finish)
    half = pl.ds(pl.multiple_of(p.x * rows, rows), rows)
    copy = remote(result.at[half], result.at[half], o_s, o_r, (p.d, 1 - p.x))
    copy.start()
    sends.append(copy)
    copy.wait_recv()
    for copy in sends:
        copy.wait_send()


def last(mid, part, grad_hidden, x, gain):
    eight, rows, width = part.shape
    return pl.pallas_call(
        functools.partial(last_kernel, mid),
        out_shape=(
            jax.ShapeDtypeStruct((2 * rows, width), BF16),
            jax.ShapeDtypeStruct((8, width), F32),
        ),
        in_specs=[VMEM] * 4,
        out_specs=(VMEM,) * 2,
        scratch_shapes=rs_scratch(rows, width) + [DMA, DMA],
        compiler_params=pltpu.CompilerParams(
            collective_id=4, has_side_effects=True, vmem_limit_bytes=56 << 20
        ),
    )(part, grad_hidden, x, gain)


def positions(segments):
    length = segments.shape[1]
    places = jnp.arange(length, dtype=jnp.int32)[None, :]
    earlier = jnp.concatenate([segments[:, :1], segments[:, :-1]], axis=1)
    begins = jnp.where((segments != earlier) | (places == 0), places, jnp.zeros_like(places))
    before = places[0][:, None] >= places[0][None, :]
    return places - jnp.max(jnp.where(before[None], begins[:, None, :], 0), axis=-1)


def rotary(position):
    halves = HEAD_DIM // 2
    inverse = THETA ** (-2.0 * jnp.arange(halves, dtype=jnp.float32) / HEAD_DIM)
    angles = position.astype(jnp.float32)[..., None] * inverse
    return (jnp.cos(angles), jnp.sin(angles))


def rotate(values, cosine, sine_table):
    halves = values.shape[-1] // 2
    front_half = values[..., :halves]
    back_half = values[..., halves:]
    cos_wide = cosine[..., None, :]
    sin_wide = sine_table[..., None, :]
    return jnp.concatenate(
        [
            front_half * cos_wide - back_half * sin_wide,
            back_half * cos_wide + front_half * sin_wide,
        ],
        axis=-1,
    )


def dot(a, b, dims):
    return lax.dot_general(a, b, (dims, ((), ())), preferred_element_type=F32)


def local(
    mid, tokens, attn_gain, w_query, w_key, w_value, w_out, mlp_gain, w_gate, w_up, w_down, segment_ids, cotangent
):
    length, width = tokens.shape
    half = length // 2
    rows = w_query.shape[0]
    x_at = lax.axis_index("tensor")

    def blocks(w):
        return w.reshape(rows, 4, w.shape[1] // 4).transpose(1, 0, 2)

    wm = jnp.concatenate([blocks(w_gate), blocks(w_up), blocks(w_down.T)], axis=-1)
    wa = jnp.concatenate([blocks(w_query), blocks(w_key), blocks(w_value), blocks(w_out.T)], axis=-1)
    ids = jnp.broadcast_to(segment_ids.reshape(1, length), (8, length))
    gains = lax.all_gather(jnp.stack([attn_gain, mlp_gain]), "dp", axis=1, tiled=True)
    gain_one, gain_two = gains[:1].astype(F32), gains[1:].astype(F32)
    tokg, cotg, idsg, fa, fm = gather(mid, tokens, cotangent, ids, wa, wm)
    fa = fa.reshape(width, -1)
    fm = fm.reshape(width, -1)
    units = w_gate.shape[1] // 4
    qw, kw = w_query.shape[1] // 4, w_key.shape[1] // 4
    heads = qw // HEAD_DIM
    gate_w, up_w, down_t = fm[:, :units], fm[:, units : 2 * units], fm[:, 2 * units :]
    qkv_w, out_t = fa[:, : qw + 2 * kw], fa[:, qw + 2 * kw :]

    segments = idsg[:, 0, :]
    cosine, sine = rotary(positions(segments))
    xs = tokg.reshape(4 * length, width)
    inputs = xs.astype(F32)
    root_one = lax.rsqrt(jnp.mean(inputs * inputs, axis=-1, keepdims=True) + EPSILON)
    normed = (inputs * root_one * gain_one).astype(BF16)
    qkv = dot(normed, qkv_w, ((1,), (0,)))
    q = rotate(qkv[:, :qw].reshape(4, length, heads, HEAD_DIM), cosine, sine).astype(BF16)
    k = rotate(qkv[:, qw : qw + kw].reshape(4, length, 1, HEAD_DIM), cosine, sine).astype(BF16)[:, :, 0]
    v = qkv[:, qw + kw :].reshape(4, length, HEAD_DIM).astype(BF16)
    places = jnp.arange(length)
    allowed = (segments[:, :, None] == segments[:, None, :]) & (places[None, :, None] >= places[None, None, :])
    scaling = HEAD_DIM ** (-0.5)
    scores = jnp.einsum("sqgd,spd->sgqp", q, k, preferred_element_type=F32) * scaling
    scores = jnp.where(allowed[:, None], scores, -1e30)
    highest = jnp.max(scores, axis=-1, keepdims=True)
    exponent = jnp.exp(scores - highest)
    probs = exponent / jnp.sum(exponent, axis=-1, keepdims=True)
    probs_low = probs.astype(BF16)
    mixture = jnp.einsum("sgqp,spd->sqgd", probs_low, v, preferred_element_type=F32)
    mixture = mixture.astype(BF16).reshape(4 * length, qw)
    attn_part = dot(mixture, out_t, ((1,), (1,))).astype(BF16)
    own_x = lax.dynamic_slice_in_dim(tokens, x_at * half, half, 0)
    own_cot = lax.dynamic_slice_in_dim(cotangent, x_at * half, half, 0)
    hidden, n2 = forward_mid(mid, attn_part.reshape(8, half, width), own_x, gain_two)
    n2 = n2.reshape(4 * length, width)

    gate = dot(n2, gate_w, ((1,), (0,)))
    up = dot(n2, up_w, ((1,), (0,)))
    sigmoid = 1.0 / (1.0 + jnp.exp(-gate))
    silu = gate / (1.0 + jnp.exp(-gate))
    activated = (silu * up).astype(BF16)
    out_part = dot(activated, down_t, ((1,), (1,))).astype(BF16)
    cots = cotg.reshape(4 * length, width)
    grad_act = dot(cots, down_t, ((1,), (0,)))
    grad_gate = (grad_act * up * sigmoid * (1.0 + gate * (1.0 - sigmoid))).astype(BF16)
    grad_up = (grad_act * silu).astype(BF16)
    grad_gu = jnp.concatenate([grad_gate, grad_up], axis=1)
    part_two = dot(grad_gu, fm[:, : 2 * units], ((1,), (1,))).astype(BF16)
    down_g = dot(cots, activated, ((0,), (0,))).astype(BF16)
    gu_g = dot(n2, grad_gu, ((0,), (0,))).astype(BF16)

    grad_hidden, ghl, output, gain_two_grad = backward_mid(
        mid, part_two.reshape(8, half, width), out_part.reshape(8, half, width), hidden, own_cot, gain_two
    )
    ghl = ghl.reshape(4 * length, width)
    grad_mix = dot(ghl, out_t, ((1,), (0,))).astype(BF16)
    gm = grad_mix.reshape(4, length, heads, HEAD_DIM)
    out_g = dot(ghl, mixture, ((0,), (0,))).astype(BF16)
    grad_probs = jnp.einsum("sqgd,spd->sgqp", gm, v, preferred_element_type=F32)
    grad_v = jnp.einsum("sgqp,sqgd->spd", probs_low, gm, preferred_element_type=F32).astype(BF16)
    centered = jnp.sum(probs * grad_probs, axis=-1, keepdims=True)
    gs = (probs * (grad_probs - centered)).astype(BF16)
    gq_rot = jnp.einsum("sgqp,spd->sqgd", gs, k, preferred_element_type=F32) * scaling
    gk_rot = jnp.einsum("sgqp,sqgd->spd", gs, q, preferred_element_type=F32) * scaling
    gq = rotate(gq_rot, cosine, -sine).astype(BF16).reshape(4 * length, qw)
    gk = rotate(gk_rot[:, :, None], cosine, -sine).astype(BF16).reshape(4 * length, kw)
    gqkv = jnp.concatenate([gq, gk, grad_v.reshape(4 * length, kw)], axis=1)
    part_one = dot(gqkv, qkv_w, ((1,), (1,))).astype(BF16)
    qkv_g = dot(normed, gqkv, ((0,), (0,))).astype(BF16)
    input_grad, gain_one_grad = last(mid, part_one.reshape(8, half, width), grad_hidden, own_x, gain_one)
    grads = jnp.concatenate([gu_g, down_g, qkv_g, out_g], axis=1).reshape(8 * mid, rows, -1)
    parts = scatter(mid, grads).reshape(2, 4, rows, -1).astype(F32)
    total = parts[0] + parts[1]

    def across(block):
        return block.transpose(1, 0, 2).reshape(rows, -1)

    def down(block):
        return block.transpose(0, 2, 1).reshape(-1, rows)

    at = [units, 2 * units, 3 * units, 3 * units + qw, 3 * units + qw + kw, 3 * units + qw + 2 * kw]
    t_gate, t_up, t_down, t_q, t_k, t_v, t_out = jnp.split(total, at, axis=-1)
    gain_grads = jnp.stack([jnp.sum(gain_one_grad, axis=0), jnp.sum(gain_two_grad, axis=0)])
    gain_grads = lax.psum_scatter(lax.psum(gain_grads, "tensor"), "dp", scatter_dimension=1, tiled=True)
    return (
        output,
        input_grad.astype(F32),
        gain_grads[0],
        across(t_q),
        across(t_k),
        across(t_v),
        down(t_out),
        gain_grads[1],
        across(t_gate),
        across(t_up),
        down(t_down),
    )


def solution(mesh):
    in_specs = (
        P("dp", None), P("dp"), P("dp", "tensor"), P("dp", "tensor"), P("dp", "tensor"), P("tensor", "dp"),
        P("dp"), P("dp", "tensor"), P("dp", "tensor"), P("tensor", "dp"), P("dp"), P("dp", None),
    )
    out_specs = (
        P("dp", None), P("dp", None), P("dp"), P("dp", "tensor"), P("dp", "tensor"), P("dp", "tensor"),
        P("tensor", "dp"), P("dp"), P("dp", "tensor"), P("dp", "tensor"), P("tensor", "dp"),
    )
    return jax.shard_map(
        functools.partial(local, mesh.shape["dp"] // 8),
        mesh=mesh, in_specs=in_specs, out_specs=out_specs, check_vma=False,
    )
```

time: 2210 us -> 954 us (0.43)
  waiting for transfers between devices: 1880 us -> 0.02 us
  Pallas kernels: 0 us -> 711 us
  blocking collectives: 103 us -> 27.9 us
  matrix products: 171 us -> 96.8 us
  local copies, waits for them, and re-layouts: 12.5 us -> 61.2 us
    reduce_scatter x7 -> x0, waiting for transfers between devices: 1280 us -> none  [the longest x1 338 us: local(): lax.psum_scatter(grad_down, 'dp', scatter_dimension=1, tiled=True)]
    pallas_call x0 -> x5, Pallas kernels: none -> 711 us  [the longest x1 271 us: gather(): pl.pallas_call(functools.partial(gather_kernel, mid), out_shape=(jax.Shap...]
    all_gather x7 -> x0, waiting for transfers between devices: 502 us -> none  [the longest x1 126 us: local(): lax.all_gather(w_up, 'dp', axis=0, tiled=True)]
    psum x3 -> x0, waiting for transfers between devices: 88.1 us -> none  [the longest x1 47.8 us: local(): grad_normed_two = lax.psum(partial_two, 'tensor')]
    dot_general x27 -> x18, matrix products: 171 us -> 93.4 us  [the longest x13 85.4 us: dot(): return lax.dot_general(a, b, (dims, ((), ())), preferred_element_type=F32)]
    unnamed x1 -> x0, blocking collectives: 61.1 us -> none
  transfers between devices with their start and end apart: 17 -> 1, of which waited for: 15 -> 0; matrix products, arithmetic and copies ran while one was open for 6% -> 9% of each run, Pallas kernels for 0% -> 21%
where the time goes in v1:
time: 954 us; the launch traced here: 950 us
  Pallas kernels  711 us (75%)
  matrix products  96.8 us (10%)
  local copies, waits for them, and re-layouts  61.2 us (6%)
  other arithmetic  38.5 us (4%)
  blocking collectives  27.9 us (3%)
  between operations  15 us (2%)
    pallas_call x1, Pallas kernels, gather(): pl.pallas_call(functools.partial(gather_kernel, mid), out_shape=(jax.Shap...  271 us
    pallas_call x1, Pallas kernels, scatter(): pl.pallas_call(functools.partial(scatter_kernel, mid, rows), out_shape=ja...  196 us
    pallas_call x1, Pallas kernels, backward_mid(): pl.pallas_call(functools.partial(backward_mid_kernel, mid), out_shape=(ja...  104 us
    pallas_call x1, Pallas kernels, forward_mid(): pl.pallas_call(functools.partial(forward_mid_kernel, mid), out_shape=(jax...  94.2 us
    dot_general x13, matrix products, dot(): return lax.dot_general(a, b, (dims, ((), ())), preferred_element_type=F32)  85.4 us
    pallas_call x1, Pallas kernels, last(): pl.pallas_call(functools.partial(last_kernel, mid), out_shape=(jax.ShapeD...  45.6 us
    all_gather x1, blocking collectives, local(): lax.all_gather(jnp.stack([attn_gain, mlp_gain]), 'dp', axis=1, tiled=True)  23 us
    concatenate x1, local copies, waits for them, and re-layouts, local(): jnp.concatenate([gu_g, down_g, qkv_g, out_g], axis=1)  19.1 us
  transfers between devices with their start and end apart: 1, of which 0 were waited for; matrix products, arithmetic and copies ran while one was open for 9% of the time, Pallas kernels for 21%

profile of v1, /device:TPU:0, one launch (start us, length us, event | category | flops | bytes accessed | tf_op | source)
XLA Modules:
  0.0 950.0 jit_solution(9657047056386514478)
XLA Ops:
  8.0 23.0 %all_gather.3 = bf16[2,2048]{1,0:T(2,128)(2,1)S(1)} all-gather(bf16[2,128]{1,0:T(2,128)(2,1)S(1)} %pad_maximum_fusion.16), channel_id=1, replica_groups=mesh['dp'=16,'tensor'=2] {'dp'}, dimensions={1}, use_global_device_ids=true | all-gather | bytes 8704 | tf_op jit(solution)/shard_map/all_gather | solution.py:539
  35.1 1.1 copy.81
  36.4 1.8 copy.87
  38.2 1.6 copy.88
  41.5 1.5 copy.92
  43.1 2.3 pad_maximum_fusion.2.wm
  45.4 1.0 pad_maximum_fusion.5.wa
  47.0 271.2 %shard_map.203 = (bf16[4,256,2048]{2,1,0:T(8,128)(2,1)}, bf16[4,256,2048]{2,1,0:T(8,128)(2,1)}, s32[4,8,256]{2,1,0:T(8,128)}, bf16[16,128,640]{2,1,0:T(8,128)(2,1)}, bf16[16,128,3072]{2,1,0:T(8,128)(2,1)}) custom-call(bf16[256,2048]{1,0:T(8,128)(2,1)} %tok.1, bf16[256,2048]{1,0:T(8,128)(2,1)} %cot.1, s32[8,256]{1,0:T(8,128)} %broadcast_in_dim.50.ids, ...), custom_call_target="tpu_custom_call" | custom-call | tf_op jit(solution)/shard_map/pallas_call | solution.py:172
  318.2 3.2 multiply_reduce_fusion
  321.6 1.0 fusion.4
  323.4 1.9 fusion.24
  326.0 1.0 constant_dynamic-slice_fusion
  329.2 1.0 convert_element_type.106
  332.4 3.5 fusion.74
  335.9 2.8 fusion.27
  339.2 3.3 convolution_convert_fusion.2
  342.5 94.2 %shard_map.204 = (f32[128,2048]{1,0:T(8,128)}, bf16[8,128,2048]{2,1,0:T(8,128)(2,1)}) custom-call(bf16[8,128,2048]{2,1,0:T(8,128)(2,1)} %bitcast.185, bf16[128,2048]{1,0:T(8,128)(2,1)} %get-tuple-element.93.x, f32[1,2048]{1,0:T(1,128)} %get-tuple-element.81.gain), custom_call_target="tpu_custom_call" | custom-call | tf_op jit(solution)/shard_map/pallas_call | solution.py:371
  436.7 7.9 fusion.5
  444.7 8.5 fusion.17
  453.2 10.4 %multiply_convert_fusion = (bf16[1024,1024]{0,1:T(8,128)(2,1)S(1)}, bf16[1024,1024]{0,1:T(8,128)(2,1)S(1)}, bf16[1024,1024]{0,1:T(8,128)(2,1)}) fusion(f32[1024,1024]{0,1:T(8,128)S(1)} %fusion.5, f32[1024,1024]{0,1:T(8,128)} %fusion.17, bf16[1024,2048]{1,0:T(8,128)(2,1)S(1)} %bitcast.245, bf16[2048,3072]{1,0:T(8,128)(2,1)} %bitcast.239), kind=kOutput, calls=%fused_computation.21 | convolution fusion | flops 4310695936 | bytes 23068672 | tf_op jit(solution)/shard_map/dot_general | solution.py:522
  463.6 10.0 %convolution_convert_fusion.4 = bf16[1024,2048]{1,0:T(8,128)(2,1)} fusion(bf16[1024,1024]{0,1:T(8,128)(2,1)S(1)} %get-tuple-element.59, bf16[2048,3072]{1,0:T(8,128)(2,1)} %bitcast.240), kind=kOutput, calls=%fused_computation.31 | convolution fusion | flops 4297064448 | bytes 10485760 | tf_op jit(solution)/shard_map/dot_general | solution.py:522
  473.5 12.9 %fusion.13 = bf16[1024,2048]{1,0:T(8,128)(2,1)} fusion(bf16[2048,3072]{1,0:T(8,128)(2,1)} %bitcast.241, bf16[1024,1024]{0,1:T(8,128)(2,1)S(1)} %copy-done.24, bf16[1024,1024]{0,1:T(8,128)(2,1)S(1)} %get-tuple-element.60), kind=kOutput, calls=%fused_computation.28 | convolution fusion | flops 8600420352 | bytes 16777216 | tf_op jit(solution)/shard_map/dot_general | solution.py:522
  486.4 103.7 %shard_map.205 = (f32[128,2048]{1,0:T(8,128)}, bf16[8,128,2048]{2,1,0:T(8,128)(2,1)}, bf16[256,2048]{1,0:T(8,128)(2,1)}, f32[8,2048]{1,0:T(8,128)}) custom-call(bf16[8,128,2048]{2,1,0:T(8,128)(2,1)} %bitcast.189, bf16[8,128,2048]{2,1,0:T(8,128)(2,1)} %bitcast.188, f32[128,2048]{1,0:T(8,128)} %get-tuple-element.30.hid, ...), custom_call_target="tpu_custom_call" | custom-call | tf_op jit(solution)/shard_map/pallas_call | solution.py:427
  590.1 3.4 convolution_convert_fusion.7
  594.9 3.1 fusion.31
  603.0 4.4 convolution_convert_fusion.1
  607.4 45.6 %shard_map.206 = (bf16[256,2048]{1,0:T(8,128)(2,1)}, f32[8,2048]{1,0:T(8,128)}) custom-call(bf16[8,128,2048]{2,1,0:T(8,128)(2,1)} %bitcast.190, f32[128,2048]{1,0:T(8,128)} %get-tuple-element.33.grad_hidden, bf16[128,2048]{1,0:T(8,128)(2,1)} %get-tuple-element.93.x, f32[1,2048]{1,0:T(1,128)} %copy-done.15), custom_call_target="tpu_custom_call" | custom-call | tf_op jit(solution)/shard_map/pallas_call | solution.py:475
  654.0 1.3 copy.138
  655.4 7.5 convolution_convert_fusion.3
  662.9 9.9 %convolution_convert_fusion = bf16[2048,2048]{0,1:T(8,128)(2,1)S(1)} fusion(bf16[1024,2048]{1,0:T(8,128)(2,1)S(1)} %bitcast.246, bf16[1024,1024]{0,1:T(8,128)(2,1)} %get-tuple-element.61, bf16[1024,1024]{0,1:T(8,128)(2,1)S(1)} %copy-done.23), kind=kOutput, calls=%fused_computation.9 | convolution fusion | flops 8602517504 | bytes 16777216 | tf_op jit(solution)/shard_map/dot_general | solution.py:522
  672.8 3.6 convolution_convert_fusion.6
  676.4 1.8 convolution_convert_fusion.5
  678.3 7.1 pad_maximum_fusion
  685.4 19.1 %copy.112 = bf16[2048,3712]{1,0:T(8,128)(2,1)} copy(bf16[2048,3712]{0,1:T(8,128)(2,1)} %pad_maximum_fusion) | data formatting | bytes 30408704 | tf_op jit(solution)/shard_map/concatenate | solution.py:611
  704.5 195.9 %shard_map.207 = bf16[8,128,3712]{2,1,0:T(8,128)(2,1)} custom-call(bf16[16,128,3712]{2,1,0:T(8,128)(2,1)} %bitcast.184), custom_call_target="tpu_custom_call" | custom-call | tf_op jit(solution)/shard_map/pallas_call | solution.py:246
  900.4 9.6 %convert_element_type.128 = f32[8,128,3712]{2,1,0:T(8,128)} convert(bf16[8,128,3712]{2,1,0:T(8,128)(2,1)} %shard_map.207) | non-fusion elementwise | flops 3801088 | bytes 22806528 | tf_op jit(solution)/shard_map/convert_element_type | solution.py:612
  909.9 6.1 slice_add_fusion
  916.1 2.9 slice_bitcast_fusion
  919.8 1.5 convert_element_type.123
  921.4 1.1 copy.115
  924.1 1.8 copy.119
  925.9 1.0 copy.116
  927.1 1.0 copy.120
  928.1 1.9 copy.118
  930.0 1.8 copy.124
  931.8 2.0 copy.117
  933.8 1.8 copy.123
  936.5 4.9 psum.8
  (122 shorter events, 26.2 us)
Async XLA Ops:
  7.2 33.2 %copy-start.7 = (bf16[128,4096]{1,0:T(8,128)(2,1)S(1)}, bf16[128,4096]{1,0:T(8,128)(2,1)}, u32[]{:S(2)}) copy-start(bf16[128,4096]{1,0:T(8,128)(2,1)} %param.20) | copy-start | bytes 3145732
  7.2 928.4 %reduce-scatter.4.cloned.1.call-start = ((), (), s32[]{:S(2)}) async-start(), calls=%async_computation.1 | async-start | bytes 1114112
  31.6 289.8 %copy-start.15 = (f32[1,2048]{1,0:T(1,128)}, f32[1,2048]{1,0:T(1,128)S(1)}, u32[]{:S(2)}) copy-start(f32[1,2048]{1,0:T(1,128)S(1)} %get-tuple-element.82.gain) | copy-start | bytes 24580
  43.0 2.3 copy-start.9
  43.1 2.3 copy-start.10
  43.1 2.3 copy-start.11
  43.1 3.3 copy-start.17
  318.2 3.5 copy-start
  321.6 1.7 copy-start.12
  322.7 2.6 copy-start.1
  323.4 2.7 copy-start.4
  323.4 2.7 copy-start.5
  335.9 3.3 copy-start.13
  436.7 8.0 copy-start.18
  444.6 8.5 copy-start.19
  463.6 10.0 %copy-start.21 = (bf16[1024,1024]{0,1:T(8,128)(2,1)}, bf16[1024,1024]{0,1:T(8,128)(2,1)S(1)}, u32[]{:S(2)}) copy-start(bf16[1024,1024]{0,1:T(8,128)(2,1)S(1)} %get-tuple-element.59) | copy-start | bytes 6291460
  463.6 10.0 %copy-start.22 = (bf16[1024,1024]{0,1:T(8,128)(2,1)}, bf16[1024,1024]{0,1:T(8,128)(2,1)S(1)}, u32[]{:S(2)}) copy-start(bf16[1024,1024]{0,1:T(8,128)(2,1)S(1)} %get-tuple-element.60) | copy-start | bytes 6291460
  463.6 10.0 %copy-start.24 = (bf16[1024,1024]{0,1:T(8,128)(2,1)S(1)}, bf16[1024,1024]{0,1:T(8,128)(2,1)}, u32[]{:S(2)}) copy-start(bf16[1024,1024]{0,1:T(8,128)(2,1)} %get-tuple-element.61) | copy-start | bytes 6291460
  594.9 3.5 copy-start.3
  601.3 1.7 copy-start.14
  603.0 4.4 copy-start.16
  655.3 7.5 copy-start.20
  655.4 7.5 copy-start.23
  672.8 3.6 copy-start.2
  916.1 3.7 copy-start.6
  931.8 10.2 %copy-start.8 = (bf16[256,2048]{1,0:T(8,128)(2,1)S(1)}, bf16[256,2048]{1,0:T(8,128)(2,1)}, u32[]{:S(2)}) copy-start(bf16[256,2048]{1,0:T(8,128)(2,1)} %get-tuple-element.105) | copy-start | bytes 3145732
Sparse Core Ops, SparseCore 0:
  655.5 57.7 reduce-scatter.3

commit v2 on v1

v2 whole, which is shorter than its diff:
```python
import functools

import jax
import jax.numpy as jnp
from jax import lax
from jax.experimental import pallas as pl
from jax.experimental.pallas import tpu as pltpu
from jax.sharding import PartitionSpec as P

HEAD_DIM = 64
EPSILON = 1e-05
THETA = 500000.0
MESH = pl.DeviceIdType.MESH
ANY = pl.BlockSpec(memory_space=pl.ANY)
VMEM = pl.BlockSpec(memory_space=pltpu.VMEM)
F32 = jnp.float32
BF16 = jnp.bfloat16
DMA = pltpu.SemaphoreType.DMA


class Place:
    def __init__(self, mid):
        self.mid = mid
        self.d = lax.axis_index("dp")
        self.x = lax.axis_index("tensor")
        self.c = self.d % 2
        self.m = (self.d // 2) % mid
        self.z = self.d // (2 * mid)
        self.lo = self.z % 2

    def dp(self, z, m, c):
        return (z * self.mid + m) * 2 + c

    def peer(self, k):
        return xor(self.z, k // 2), xor(self.c, k % 2)

    def other_m(self, j):
        return (self.m + 1 + j) % self.mid


def xor(a, k):
    if k == 0:
        return a
    low = a % 2
    high = a // 2
    if k % 2:
        low = 1 - low
    if k // 2:
        high = 1 - high
    return high * 2 + low


def remote(src, dst, send, recv, device):
    copy = pltpu.make_async_remote_copy(
        src_ref=src, dst_ref=dst, send_sem=send, recv_sem=recv, device_id=device, device_id_type=MESH
    )
    return copy


def greet(devices):
    barrier = pltpu.get_barrier_semaphore()
    for device in devices:
        pl.semaphore_signal(barrier, inc=1, device_id=device, device_id_type=MESH)
    pl.semaphore_wait(barrier, len(devices))


def arrived(dst, sem):
    pltpu.make_async_copy(dst, dst, sem).wait()


class Gather:
    def __init__(self, p, w, full, sems, waves):
        self.p, self.w, self.full, self.waves = p, w, full, waves
        self.z_s, self.r, self.f_s, self.loc = sems
        self.rows = w.shape[1] // waves
        self.block = p.lo * 2 + p.c
        self.order = list(range(7, 0, -1))
        self.pushes, self.sends = {}, []

    def at(self, wave):
        return pl.ds(wave * self.rows, self.rows)

    def push(self, wave):
        p, at = self.p, self.at(wave)
        for k in self.order:
            z, c = p.peer(k)
            copy = remote(
                self.w.at[(z % 2) * 2 + c, at], self.full.at[p.d, at], self.z_s.at[k, wave], self.r.at[p.d, wave],
                (p.dp(z, p.m, c), p.x),
            )
            copy.start()
            self.pushes[k, wave] = copy
        self.forward_one(self.w.at[self.block, at], p.d, wave, 0)

    def forward_one(self, src, d, wave, k):
        p = self.p
        for j in range(p.mid - 1):
            copy = remote(
                src, self.full.at[d, self.at(wave)], self.f_s.at[k, wave, j], self.r.at[d, wave],
                (p.dp(p.z, p.other_m(j), p.c), p.x),
            )
            copy.start()
            self.sends.append(copy)

    def forward(self, wave):
        p = self.p
        for k in self.order:
            z, c = p.peer(k)
            d = p.dp(z, p.m, c)
            here = self.full.at[d, self.at(wave)]
            arrived(here, self.r.at[d, wave])
            self.forward_one(here, d, wave, k)

    def start_own(self):
        self.own = pltpu.make_async_copy(self.w.at[self.block], self.full.at[self.p.d], self.loc)
        self.own.start()

    def pushed(self, wave):
        for k in self.order:
            self.pushes[k, wave].wait_send()

    def finish(self):
        p = self.p
        for wave in range(self.waves):
            for k in range(8):
                z, c = p.peer(k)
                for j in range(p.mid - 1):
                    d = p.dp(z, p.other_m(j), c)
                    arrived(self.full.at[d, self.at(wave)], self.r.at[d, wave])
        self.own.wait()
        for copy in self.sends:
            copy.wait_send()


def gather_steps(*gathers, lag=2):
    for g in gathers:
        g.start_own()
    items = [(g, wave) for g in gathers for wave in range(g.waves)]
    for n, (g, wave) in enumerate(items):
        if n >= lag:
            before, old = items[n - lag]
            before.pushed(old)
            before.forward(old)
        g.push(wave)
        yield
    for g, wave in items[max(0, len(items) - lag) :]:
        g.pushed(wave)
        g.forward(wave)
        yield
    for g in gathers:
        g.finish()


def gather_sems(mid, waves):
    return [DMA((8, waves)), DMA((8 * mid, waves)), DMA((8, waves, mid - 1)), DMA]


class Scatter:
    def __init__(self, p, g, own, other, out, sems, waves):
        self.p, self.g, self.own, self.other, self.out, self.waves = p, g, own, other, out, waves
        self.y_s, self.y_r, self.z_s, self.z_r, self.load, self.loc = sems
        self.full_rows = own.shape[1]
        self.rows = self.full_rows // waves
        self.order = list(range(7, -1, -1))
        self.y_sends, self.z_sends, self.loads = {}, [], {}

    def piece(self, d, wave):
        return self.g.at[pl.ds(pl.multiple_of(d * self.full_rows + wave * self.rows, 16), self.rows)]

    def at(self, wave):
        return pl.ds(wave * self.rows, self.rows)

    def start_loads(self):
        p = self.p
        for wave in range(self.waves):
            for k in self.order:
                z, c = p.peer(k)
                copy = pltpu.make_async_copy(
                    self.piece(p.dp(z, p.m, c), wave), self.own.at[k, self.at(wave)], self.load.at[k, wave]
                )
                copy.start()
                self.loads[k, wave] = copy

    def y_send(self, wave):
        p = self.p
        for k in self.order:
            z, c = p.peer(k)
            for j in range(p.mid - 1):
                m = p.other_m(j)
                there = p.mid - 2 - j
                copy = remote(
                    self.piece(p.dp(z, m, c), wave), self.other.at[there, k, self.at(wave)],
                    self.y_s.at[k, wave, j], self.y_r.at[k, wave, there], (p.dp(p.z, m, p.c), p.x),
                )
                copy.start()
                self.y_sends[k, wave, j] = copy

    def z_push(self, wave):
        p = self.p
        at = self.at(wave)
        me = p.z * 2 + p.c
        for k in self.order:
            z, c = p.peer(k)
            for j in range(p.mid - 1):
                arrived(self.other.at[j, k, at], self.y_r.at[k, wave, j])
            self.loads[k, wave].wait()

            def add(i, carry):
                here = pl.ds(pl.multiple_of(wave * self.rows + i * 16, 16), 16)
                total = self.own[k, here, :].astype(F32)
                for j in range(p.mid - 1):
                    total = total + self.other[j, k, here, :].astype(F32)
                self.own[k, here, :] = total.astype(BF16)
                return carry

            lax.fori_loop(0, self.rows // 16, add, 0)
            src, dst = self.own.at[k, at], self.out.at[me, at]
            if k == 0:
                copy = pltpu.make_async_copy(src, dst, self.loc.at[wave])
                copy.start()
                self.z_sends.append((copy, True))
            else:
                copy = remote(src, dst, self.z_s.at[k, wave], self.z_r.at[me, wave], (p.dp(z, p.m, c), p.x))
                copy.start()
                self.z_sends.append((copy, False))

    def y_sent(self, wave):
        for k in self.order:
            for j in range(self.p.mid - 1):
                self.y_sends[k, wave, j].wait_send()

    def finish(self):
        p = self.p
        for wave in range(self.waves):
            for k in range(1, 8):
                z, c = p.peer(k)
                src = z * 2 + c
                arrived(self.out.at[src, self.at(wave)], self.z_r.at[src, wave])
        for copy, here in self.z_sends:
            copy.wait() if here else copy.wait_send()


def scatter_steps(*scatters, lag=2):
    for s in scatters:
        s.start_loads()
    items = [(s, wave) for s in scatters for wave in range(s.waves)]
    for n, (s, wave) in enumerate(items):
        if n >= lag:
            before, old = items[n - lag]
            before.y_sent(old)
        s.y_send(wave)
        if n >= 1:
            before, old = items[n - 1]
            before.z_push(old)
        yield
    s, wave = items[-1]
    s.z_push(wave)
    yield
    for s, wave in items[max(0, len(items) - lag) :]:
        s.y_sent(wave)
    for s in scatters:
        s.finish()


def scatter_scratch(mid, rows, width, waves):
    return [
        pltpu.VMEM((8, rows, width), BF16),
        pltpu.VMEM((mid - 1, 8, rows, width), BF16),
        DMA((8, waves, mid - 1)), DMA((8, waves, mid - 1)), DMA((8, waves)), DMA((8, waves)), DMA((8, waves)),
        DMA((waves,)),
    ]


def waves_of(rows, most):
    return max(w for w in range(1, most + 1) if rows % (16 * w) == 0)


def drive(*streams):
    left = list(streams)
    while left:
        for stream in list(left):
            try:
                next(stream)
            except StopIteration:
                left.remove(stream)


def chain(*streams):
    for stream in streams:
        yield from stream


def all_devices(p):
    return (
        [(p.dp(z, p.m, c), p.x) for z, c in map(p.peer, range(1, 8))]
        + [(p.dp(p.z, p.other_m(j), p.c), p.x) for j in range(p.mid - 1)]
        + [(p.d, 1 - p.x), (p.dp(xor(p.z, 1), p.m, p.c), 1 - p.x)]
    )


def token_steps(p, tok, cot, ids, tokg, cotg, idsg, tok_s, tok_r, ids_s, ids_r, loc):
    half = tok.shape[0] // 2
    seq = p.lo * 2 + p.c
    z_near = (p.dp(xor(p.z, 1), p.m, p.c), p.x)
    c_near = (p.dp(p.z, p.m, 1 - p.c), p.x)
    x_near = (p.d, 1 - p.x)
    mine = pl.ds(pl.multiple_of(p.x * half, 16), half)
    theirs = pl.ds(pl.multiple_of((1 - p.x) * half, 16), half)
    far_seq = (1 - p.lo) * 2 + p.c
    c_seq = p.lo * 2 + 1 - p.c
    cc_seq = (1 - p.lo) * 2 + 1 - p.c
    sends = []

    def go(copy):
        copy.start()
        sends.append(copy)

    here = []
    go(remote(ids, idsg.at[seq], ids_s.at[0], ids_r.at[0], z_near))
    go(remote(ids, idsg.at[seq], ids_s.at[1], ids_r.at[1], c_near))
    for n, (src, dst) in enumerate(((tok, tokg), (cot, cotg))):
        go(remote(src.at[mine], dst.at[seq, mine], tok_s.at[n, 0], tok_r.at[n, 0], z_near))
        go(remote(src, dst.at[seq], tok_s.at[n, 1], tok_r.at[n, 1], c_near))
    for n, (src, dst) in enumerate(((tok, tokg.at[seq]), (cot, cotg.at[seq]), (ids, idsg.at[seq]))):
        copy = pltpu.make_async_copy(src, dst, loc.at[n])
        copy.start()
        here.append(copy)
    yield
    arrived(idsg.at[far_seq], ids_r.at[0])
    go(remote(idsg.at[far_seq], idsg.at[far_seq], ids_s.at[2], ids_r.at[2], c_near))
    for n, dst in enumerate((tokg, cotg)):
        arrived(dst.at[far_seq, mine], tok_r.at[n, 0])
        go(remote(dst.at[far_seq, mine], dst.at[far_seq, mine], tok_s.at[n, 2], tok_r.at[n, 2], x_near))
        go(remote(dst.at[far_seq, mine], dst.at[far_seq, mine], tok_s.at[n, 3], tok_r.at[n, 3], c_near))
        yield
    for n, dst in enumerate((tokg, cotg)):
        arrived(dst.at[far_seq, theirs], tok_r.at[n, 2])
        go(remote(dst.at[far_seq, theirs], dst.at[far_seq, theirs], tok_s.at[n, 4], tok_r.at[n, 4], c_near))
        yield
    arrived(idsg.at[c_seq], ids_r.at[1])
    arrived(idsg.at[cc_seq], ids_r.at[2])
    for n, dst in enumerate((tokg, cotg)):
        arrived(dst.at[c_seq], tok_r.at[n, 1])
        arrived(dst.at[cc_seq, mine], tok_r.at[n, 3])
        arrived(dst.at[cc_seq, theirs], tok_r.at[n, 4])
    for copy in here:
        copy.wait()
    for copy in sends:
        copy.wait_send()


def first_kernel(mid, waves, tok, cot, ids, wa, tokg, cotg, idsg, fa, tok_s, tok_r, ids_s, ids_r, loc, *a_sems):
    p = Place(mid)
    greet(all_devices(p))
    drive(
        token_steps(p, tok, cot, ids, tokg, cotg, idsg, tok_s, tok_r, ids_s, ids_r, loc),
        gather_steps(Gather(p, wa, fa, a_sems, waves)),
    )


def first(mid, tok, cot, ids, wa):
    waves = waves_of(wa.shape[1], 4)
    return pl.pallas_call(
        functools.partial(first_kernel, mid, waves),
        out_shape=(
            jax.ShapeDtypeStruct((4,) + tok.shape, BF16),
            jax.ShapeDtypeStruct((4,) + cot.shape, BF16),
            jax.ShapeDtypeStruct((4,) + ids.shape, ids.dtype),
            jax.ShapeDtypeStruct((8 * mid,) + wa.shape[1:], BF16),
        ),
        in_specs=[ANY] * 4,
        out_specs=(ANY,) * 4,
        scratch_shapes=[DMA((2, 5)), DMA((2, 5)), DMA((3,)), DMA((3,)), DMA((3,))] + gather_sems(mid, waves),
        compiler_params=pltpu.CompilerParams(collective_id=0, has_side_effects=True),
    )(tok, cot, ids, wa)


def group_devices(p):
    far = xor(p.z, 1)
    return {
        (0, 1): (p.d, 1 - p.x),
        (1, 0): (p.dp(far, p.m, p.c), p.x),
        (1, 1): (p.dp(far, p.m, p.c), 1 - p.x),
    }, (p.dp(p.z, p.m, 1 - p.c), p.x)


def reduce_steps(p, part, scratch, finish):
    abuf, sums, bbuf, a_s, a_r, b_s, b_r = scratch
    chips, sibling = group_devices(p)
    order = ((1, 1), (0, 1), (1, 0), (0, 0))
    sends = []
    for n, (fz, fx) in enumerate(order):
        lo, x = xor(p.lo, fz), xor(p.x, fx)
        copy = remote(part.at[(lo * 2 + 1 - p.c) * 2 + x], abuf.at[n], a_s.at[n], a_r.at[n], sibling)
        copy.start()
        sends.append(copy)
    yield
    rows = part.shape[1]
    step = 16
    for n, (fz, fx) in enumerate(order):
        lo, x = xor(p.lo, fz), xor(p.x, fx)
        own = (lo * 2 + p.c) * 2 + x
        arrived(abuf.at[n], a_r.at[n])
        if n == 3:
            break

        def add(i, carry):
            at = pl.ds(pl.multiple_of(i * step, step), step)
            sums[n, at, :] = (part[own, at, :].astype(F32) + abuf[n, at, :].astype(F32)).astype(BF16)
            return carry

        lax.fori_loop(0, rows // step, add, 0)
        copy = remote(sums.at[n], bbuf.at[n], b_s.at[n], b_r.at[n], chips[(fz, fx)])
        copy.start()
        sends.append(copy)
    yield
    yield
    mine = (p.lo * 2 + p.c) * 2 + p.x
    for n in range(3):
        arrived(bbuf.at[n], b_r.at[n])

    def last(i, carry):
        at = pl.ds(pl.multiple_of(i * step, step), step)
        total = part[mine, at, :].astype(F32) + abuf[3, at, :].astype(F32)
        for n in range(3):
            total = total + bbuf[n, at, :].astype(F32)
        finish(at, total)
        return carry

    lax.fori_loop(0, rows // step, last, 0)
    for copy in sends:
        copy.wait_send()


def share_steps(p, gathered, s, r):
    chips, sibling = group_devices(p)
    mine = (p.lo * 2 + p.c) * 2 + p.x
    order = ((1, 1), (0, 1), (1, 0))
    sends = []
    for n, flips in enumerate(order):
        copy = remote(gathered.at[mine], gathered.at[mine], s.at[n], r.at[n], chips[flips])
        copy.start()
        sends.append(copy)
    copy = remote(gathered.at[mine], gathered.at[mine], s.at[3], r.at[3], sibling)
    copy.start()
    sends.append(copy)
    yield
    yield
    for n, (fz, fx) in enumerate(order):
        at = (xor(p.lo, fz) * 2 + p.c) * 2 + xor(p.x, fx)
        arrived(gathered.at[at], r.at[n])
        copy = remote(gathered.at[at], gathered.at[at], s.at[4 + n], r.at[4 + n], sibling)
        copy.start()
        sends.append(copy)
    yield
    for n, (fz, fx) in enumerate(order + ((0, 0),)):
        at = (xor(p.lo, fz) * 2 + 1 - p.c) * 2 + xor(p.x, fx)
        number = 3 if n == 3 else 4 + n
        arrived(gathered.at[at], r.at[number])
    for copy in sends:
        copy.wait_send()


def swap_steps(p, both, o_s, o_r):
    rows = both.shape[0] // 2
    half = pl.ds(pl.multiple_of(p.x * rows, 16), rows)
    copy = remote(both.at[half], both.at[half], o_s, o_r, (p.d, 1 - p.x))
    copy.start()
    yield
    copy.wait()


def norm_root(value):
    return lax.rsqrt(jnp.mean(value * value, axis=-1, keepdims=True) + EPSILON)


def norm_back(value, scaled):
    root = norm_root(value)
    return root * scaled - value * root**3 * jnp.mean(value * scaled, axis=-1, keepdims=True)


def second_kernel(mid, waves, part, x, wm, hidden, normed, fm, *scratch):
    p = Place(mid)
    greet(all_devices(p))
    mine = (p.lo * 2 + p.c) * 2 + p.x

    def finish(at, total):
        value = x[at, :].astype(F32) + total
        hidden[at, :] = value
        normed[mine, at, :] = (value * norm_root(value)).astype(BF16)

    drive(
        chain(reduce_steps(p, part, scratch[:7], finish), share_steps(p, normed, scratch[7], scratch[8])),
        gather_steps(Gather(p, wm, fm, scratch[9:], waves)),
    )


def reduce_scratch(rows, width):
    return [
        pltpu.VMEM((4, rows, width), BF16),
        pltpu.VMEM((3, rows, width), BF16),
        pltpu.VMEM((3, rows, width), BF16),
        DMA((4,)), DMA((4,)), DMA((3,)), DMA((3,)),
    ]


def second(mid, part, x, wm):
    eight, rows, width = part.shape
    waves = waves_of(wm.shape[1], 8)
    return pl.pallas_call(
        functools.partial(second_kernel, mid, waves),
        out_shape=(
            jax.ShapeDtypeStruct((rows, width), F32),
            jax.ShapeDtypeStruct((eight, rows, width), BF16),
            jax.ShapeDtypeStruct((8 * mid,) + wm.shape[1:], BF16),
        ),
        in_specs=[VMEM] * 2 + [ANY],
        out_specs=(VMEM, VMEM, ANY),
        scratch_shapes=reduce_scratch(rows, width) + [DMA((7,)), DMA((7,))] + gather_sems(mid, waves),
        compiler_params=pltpu.CompilerParams(
            collective_id=1, has_side_effects=True, vmem_limit_bytes=56 << 20
        ),
    )(part, x, wm)


def third_kernel(
    mid, waves, part, out_part, hid, cot, gu, down, grad_hidden, low, output, gu_out, down_out, *scratch
):
    p = Place(mid)
    greet(all_devices(p))
    mine = (p.lo * 2 + p.c) * 2 + p.x
    rows = hid.shape[0]

    def finish(at, total):
        grads = cot[at, :].astype(F32) + norm_back(hid[at, :], total)
        grad_hidden[at, :] = grads
        low[mine, at, :] = grads.astype(BF16)

    def finish_out(at, total):
        there = pl.ds(pl.multiple_of(p.x * rows + at.start, 16), 16)
        output[there, :] = (hid[at, :] + total).astype(BF16)

    r1, r2 = scratch[:7], scratch[7:14]
    g_s, g_r, o_s, o_r = scratch[14:18]
    gu_s, down_s = scratch[18:26], scratch[26:34]
    drive(
        chain(
            reduce_steps(p, part, r1, finish),
            share_steps(p, low, g_s, g_r),
            reduce_steps(p, out_part, r2, finish_out),
            swap_steps(p, output, o_s, o_r),
        ),
        scatter_steps(
            Scatter(p, down, down_s[0], down_s[1], down_out, down_s[2:], waves),
            Scatter(p, gu, gu_s[0], gu_s[1], gu_out, gu_s[2:], waves),
        ),
    )


def third(mid, part, out_part, hid, cot, gu, down):
    eight, rows, width = part.shape
    n = 8 * mid
    w_rows = gu.shape[0] // n
    waves = waves_of(w_rows, 4)
    return pl.pallas_call(
        functools.partial(third_kernel, mid, waves),
        out_shape=(
            jax.ShapeDtypeStruct((rows, width), F32),
            jax.ShapeDtypeStruct((eight, rows, width), BF16),
            jax.ShapeDtypeStruct((2 * rows, width), BF16),
            jax.ShapeDtypeStruct((8, w_rows, gu.shape[1]), BF16),
            jax.ShapeDtypeStruct((8, w_rows, down.shape[1]), BF16),
        ),
        in_specs=[VMEM] * 4 + [ANY] * 2,
        out_specs=(VMEM,) * 3 + (ANY,) * 2,
        scratch_shapes=reduce_scratch(rows, width) * 2
        + [DMA((7,)), DMA((7,)), DMA, DMA]
        + scatter_scratch(mid, w_rows, gu.shape[1], waves)
        + scatter_scratch(mid, w_rows, down.shape[1], waves),
        compiler_params=pltpu.CompilerParams(
            collective_id=2, has_side_effects=True, vmem_limit_bytes=60 << 20
        ),
    )(part, out_part, hid, cot, gu, down)


def fourth_kernel(mid, waves, part, grad_hidden, x, ga, result, ga_out, *scratch):
    p = Place(mid)
    greet(all_devices(p))
    rows = x.shape[0]

    def finish(at, total):
        there = pl.ds(pl.multiple_of(p.x * rows + at.start, 16), 16)
        value = x[at, :].astype(F32)
        result[there, :] = (grad_hidden[at, :] + norm_back(value, total)).astype(BF16)

    own = scratch[9:]
    drive(
        chain(reduce_steps(p, part, scratch[:7], finish), swap_steps(p, result, scratch[7], scratch[8])),
        scatter_steps(Scatter(p, ga, own[0], own[1], ga_out, own[2:], waves)),
    )


def fourth(mid, part, grad_hidden, x, ga):
    eight, rows, width = part.shape
    w_rows = ga.shape[0] // (8 * mid)
    waves = waves_of(w_rows, 4)
    return pl.pallas_call(
        functools.partial(fourth_kernel, mid, waves),
        out_shape=(
            jax.ShapeDtypeStruct((2 * rows, width), BF16),
            jax.ShapeDtypeStruct((8, w_rows, ga.shape[1]), BF16),
        ),
        in_specs=[VMEM] * 3 + [ANY],
        out_specs=(VMEM, ANY),
        scratch_shapes=reduce_scratch(rows, width)
        + [DMA, DMA]
        + scatter_scratch(mid, w_rows, ga.shape[1], waves),
        compiler_params=pltpu.CompilerParams(
            collective_id=3, has_side_effects=True, vmem_limit_bytes=56 << 20
        ),
    )(part, grad_hidden, x, ga)


def positions(segments):
    length = segments.shape[1]
    places = jnp.arange(length, dtype=jnp.int32)[None, :]
    earlier = jnp.concatenate([segments[:, :1], segments[:, :-1]], axis=1)
    begins = jnp.where((segments != earlier) | (places == 0), places, jnp.zeros_like(places))
    before = places[0][:, None] >= places[0][None, :]
    return places - jnp.max(jnp.where(before[None], begins[:, None, :], 0), axis=-1)


def rotary(position):
    halves = HEAD_DIM // 2
    inverse = THETA ** (-2.0 * jnp.arange(halves, dtype=jnp.float32) / HEAD_DIM)
    angles = position.astype(jnp.float32)[..., None] * inverse
    return (jnp.cos(angles), jnp.sin(angles))


def rotate(values, cosine, sine_table):
    halves = values.shape[-1] // 2
    front_half = values[..., :halves]
    back_half = values[..., halves:]
    cos_wide = cosine[..., None, :]
    sin_wide = sine_table[..., None, :]
    return jnp.concatenate(
        [
            front_half * cos_wide - back_half * sin_wide,
            back_half * cos_wide + front_half * sin_wide,
        ],
        axis=-1,
    )


def dot(a, b, dims):
    return lax.dot_general(a, b, (dims, ((), ())), preferred_element_type=F32)


def local(
    mid, tokens, attn_gain, w_query, w_key, w_value, w_out, mlp_gain, w_gate, w_up, w_down, segment_ids, cotangent
):
    length, width = tokens.shape
    half = length // 2
    rows = w_query.shape[0]
    x_at = lax.axis_index("tensor")

    def blocks(w):
        return w.reshape(rows, 4, w.shape[1] // 4).transpose(1, 0, 2)

    gain_one, gain_two = attn_gain.astype(F32)[:, None], mlp_gain.astype(F32)[:, None]

    def scaled(w, gain):
        return blocks((w.astype(F32) * gain).astype(BF16))

    wm = jnp.concatenate([scaled(w_gate, gain_two), scaled(w_up, gain_two), blocks(w_down.T)], axis=-1)
    wa = jnp.concatenate(
        [scaled(w_query, gain_one), scaled(w_key, gain_one), scaled(w_value, gain_one), blocks(w_out.T)], axis=-1
    )
    ids = jnp.broadcast_to(segment_ids.reshape(1, length), (8, length))
    tokg, cotg, idsg, fa = first(mid, tokens, cotangent, ids, wa)
    fa = fa.reshape(width, -1)
    units = w_gate.shape[1] // 4
    qw, kw = w_query.shape[1] // 4, w_key.shape[1] // 4
    heads = qw // HEAD_DIM
    qkv_w, out_t = fa[:, : qw + 2 * kw], fa[:, qw + 2 * kw :]

    segments = idsg[:, 0, :]
    cosine, sine = rotary(positions(segments))
    xs = tokg.reshape(4 * length, width)
    inputs = xs.astype(F32)
    root_one = lax.rsqrt(jnp.mean(inputs * inputs, axis=-1, keepdims=True) + EPSILON)
    normed = (inputs * root_one).astype(BF16)
    qkv = dot(normed, qkv_w, ((1,), (0,)))
    q = rotate(qkv[:, :qw].reshape(4, length, heads, HEAD_DIM), cosine, sine).astype(BF16)
    k = rotate(qkv[:, qw : qw + kw].reshape(4, length, 1, HEAD_DIM), cosine, sine).astype(BF16)[:, :, 0]
    v = qkv[:, qw + kw :].reshape(4, length, HEAD_DIM).astype(BF16)
    places = jnp.arange(length)
    allowed = (segments[:, :, None] == segments[:, None, :]) & (places[None, :, None] >= places[None, None, :])
    scaling = HEAD_DIM ** (-0.5)
    scores = jnp.einsum("sqgd,spd->sgqp", q, k, preferred_element_type=F32) * scaling
    scores = jnp.where(allowed[:, None], scores, -1e30)
    highest = jnp.max(scores, axis=-1, keepdims=True)
    exponent = jnp.exp(scores - highest)
    probs = exponent / jnp.sum(exponent, axis=-1, keepdims=True)
    probs_low = probs.astype(BF16)
    mixture = jnp.einsum("sgqp,spd->sqgd", probs_low, v, preferred_element_type=F32)
    mixture = mixture.astype(BF16).reshape(4 * length, qw)
    attn_part = dot(mixture, out_t, ((1,), (1,))).astype(BF16)
    own_x = lax.dynamic_slice_in_dim(tokens, x_at * half, half, 0)
    own_cot = lax.dynamic_slice_in_dim(cotangent, x_at * half, half, 0)
    hidden, n2, fm = second(mid, attn_part.reshape(8, half, width), own_x, wm)
    n2 = n2.reshape(4 * length, width)
    fm = fm.reshape(width, -1)
    gate_w, up_w, down_t = fm[:, :units], fm[:, units : 2 * units], fm[:, 2 * units :]

    gate = dot(n2, gate_w, ((1,), (0,)))
    up = dot(n2, up_w, ((1,), (0,)))
    sigmoid = 1.0 / (1.0 + jnp.exp(-gate))
    silu = gate / (1.0 + jnp.exp(-gate))
    activated = (silu * up).astype(BF16)
    out_part = dot(activated, down_t, ((1,), (1,))).astype(BF16)
    cots = cotg.reshape(4 * length, width)
    grad_act = dot(cots, down_t, ((1,), (0,)))
    grad_gate = (grad_act * up * sigmoid * (1.0 + gate * (1.0 - sigmoid))).astype(BF16)
    grad_up = (grad_act * silu).astype(BF16)
    grad_gu = jnp.concatenate([grad_gate, grad_up], axis=1)
    part_two = dot(grad_gu, fm[:, : 2 * units], ((1,), (1,))).astype(BF16)
    down_g = dot(cots, activated, ((0,), (0,))).astype(BF16)
    gu_g = dot(n2, grad_gu, ((0,), (0,))).astype(BF16)

    grad_hidden, ghl, output, gu_parts, down_parts = third(
        mid, part_two.reshape(8, half, width), out_part.reshape(8, half, width), hidden, own_cot, gu_g, down_g
    )
    ghl = ghl.reshape(4 * length, width)
    grad_mix = dot(ghl, out_t, ((1,), (0,))).astype(BF16)
    gm = grad_mix.reshape(4, length, heads, HEAD_DIM)
    out_g = dot(ghl, mixture, ((0,), (0,))).astype(BF16)
    grad_probs = jnp.einsum("sqgd,spd->sgqp", gm, v, preferred_element_type=F32)
    grad_v = jnp.einsum("sgqp,sqgd->spd", probs_low, gm, preferred_element_type=F32).astype(BF16)
    centered = jnp.sum(probs * grad_probs, axis=-1, keepdims=True)
    gs = (probs * (grad_probs - centered)).astype(BF16)
    gq_rot = jnp.einsum("sgqp,spd->sqgd", gs, k, preferred_element_type=F32) * scaling
    gk_rot = jnp.einsum("sgqp,sqgd->spd", gs, q, preferred_element_type=F32) * scaling
    gq = rotate(gq_rot, cosine, -sine).astype(BF16).reshape(4 * length, qw)
    gk = rotate(gk_rot[:, :, None], cosine, -sine).astype(BF16).reshape(4 * length, kw)
    gqkv = jnp.concatenate([gq, gk, grad_v.reshape(4 * length, kw)], axis=1)
    part_one = dot(gqkv, qkv_w, ((1,), (1,))).astype(BF16)
    qkv_g = dot(normed, gqkv, ((0,), (0,))).astype(BF16)
    grads = jnp.concatenate([qkv_g, out_g], axis=1)
    input_grad, a_parts = fourth(mid, part_one.reshape(8, half, width), grad_hidden, own_x, grads)

    def total(parts):
        parts = parts.reshape(2, 4, rows, -1).astype(F32)
        return parts[0] + parts[1]

    def across(block):
        return block.transpose(1, 0, 2).reshape(rows, -1)

    def down(block):
        return block.transpose(0, 2, 1).reshape(-1, rows)

    t_gate, t_up = jnp.split(total(gu_parts), 2, axis=-1)
    t_q, t_k, t_v, t_out = jnp.split(total(a_parts), [qw, qw + kw, qw + 2 * kw], axis=-1)
    t_gate, t_up, t_q, t_k, t_v = (across(t) for t in (t_gate, t_up, t_q, t_k, t_v))

    def gain_grad(*pairs):
        return sum(jnp.sum(w.astype(F32) * g, axis=1) for w, g in pairs)

    gain_grads = jnp.stack(
        [gain_grad((w_query, t_q), (w_key, t_k), (w_value, t_v)), gain_grad((w_gate, t_gate), (w_up, t_up))]
    )
    gain_grads = lax.psum(gain_grads, "tensor")
    return (
        output,
        input_grad.astype(F32),
        gain_grads[0],
        t_q * gain_one,
        t_k * gain_one,
        t_v * gain_one,
        down(t_out),
        gain_grads[1],
        t_gate * gain_two,
        t_up * gain_two,
        down(total(down_parts)),
    )


def solution(mesh):
    in_specs = (
        P("dp", None), P("dp"), P("dp", "tensor"), P("dp", "tensor"), P("dp", "tensor"), P("tensor", "dp"),
        P("dp"), P("dp", "tensor"), P("dp", "tensor"), P("tensor", "dp"), P("dp"), P("dp", None),
    )
    out_specs = (
        P("dp", None), P("dp", None), P("dp"), P("dp", "tensor"), P("dp", "tensor"), P("dp", "tensor"),
        P("tensor", "dp"), P("dp"), P("dp", "tensor"), P("dp", "tensor"), P("tensor", "dp"),
    )
    return jax.shard_map(
        functools.partial(local, mesh.shape["dp"] // 8),
        mesh=mesh, in_specs=in_specs, out_specs=out_specs, check_vma=False,
    )
```

time: 954 us -> 710 us (0.74)
  Pallas kernels: 711 us -> 519 us
  blocking collectives: 27.9 us -> 4.94 us
  between operations: 15 us -> 1.73 us
  local copies, waits for them, and re-layouts: 61.2 us -> 48.8 us
    pallas_call x5 -> x4, Pallas kernels: 711 us -> 519 us  [the longest x1 192 us: third(): pl.pallas_call(functools.partial(third_kernel, mid, waves), out_shape=(ja...]
    all_gather x1 -> x0, blocking collectives: 23 us -> none  [local(): lax.all_gather(jnp.stack([attn_gain, mlp_gain]), 'dp', axis=1, tiled=True)]
    concatenate x1 -> x0, local copies, waits for them, and re-layouts: 19.1 us -> none  [local(): jnp.concatenate([gu_g, down_g, qkv_g, out_g], axis=1)]
  transfers between devices with their start and end apart: 1 -> 0, of which waited for: 0 -> 0; matrix products, arithmetic and copies ran while one was open for 9% -> 0% of each run, Pallas kernels for 21% -> 0%
where the time goes in v2:
time: 710 us; the launch traced here: 706 us
  Pallas kernels  519 us (73%)
  matrix products  98.8 us (14%)
  local copies, waits for them, and re-layouts  48.8 us (7%)
  other arithmetic  32.8 us (5%)
    pallas_call x1, Pallas kernels, third(): pl.pallas_call(functools.partial(third_kernel, mid, waves), out_shape=(ja...  192 us
    pallas_call x1, Pallas kernels, second(): pl.pallas_call(functools.partial(second_kernel, mid, waves), out_shape=(j...  187 us
    dot_general x13, matrix products, dot(): return lax.dot_general(a, b, (dims, ((), ())), preferred_element_type=F32)  87.5 us
    pallas_call x1, Pallas kernels, first(): pl.pallas_call(functools.partial(first_kernel, mid, waves), out_shape=(ja...  80.5 us
    pallas_call x1, Pallas kernels, fourth(): pl.pallas_call(functools.partial(fourth_kernel, mid, waves), out_shape=(j...  59.7 us
    unnamed x93, local copies, waits for them, and re-layouts  17.4 us

profile of v2, /device:TPU:0, one launch (start us, length us, event | category | flops | bytes accessed | tf_op | source)
XLA Modules:
  0.0 706.0 jit_solution(17269199425574550327)
XLA Ops:
  2.2 1.3 broadcast_in_dim.46.ids
  7.0 1.1 copy.38
  9.1 1.9 copy.44
  10.9 2.2 pad_maximum_fusion.5.wa
  13.1 1.0 constant_dynamic-slice_fusion
  14.8 2.0 copy.55
  16.9 2.6 copy.57
  19.5 1.4 fusion.19
  20.9 1.5 copy.54
  22.9 2.9 pad_maximum_fusion.1.wm
  25.9 80.5 %shard_map.203 = (bf16[4,256,2048]{2,1,0:T(8,128)(2,1)}, bf16[4,256,2048]{2,1,0:T(8,128)(2,1)}, s32[4,8,256]{2,1,0:T(8,128)}, bf16[16,128,640]{2,1,0:T(8,128)(2,1)}) custom-call(bf16[256,2048]{1,0:T(8,128)(2,1)} %tok.1, bf16[256,2048]{1,0:T(8,128)(2,1)} %cot.1, s32[8,256]{1,0:T(8,128)} %broadcast_in_dim.46.ids, bf16[4,128,640]{2,1,0:T(8,128)(2,1)} %pad_maximum_fusion.5.wa), custom_call_target="tpu_custom_call" | custom-call | tf_op jit(solution)/shard_map/pallas_call | solution.py:363
  106.4 3.2 multiply_reduce_fusion
  113.4 1.9 fusion.28
  115.5 1.0 copy-done.14
  116.5 1.3 slice.126
  119.5 3.4 fusion.84
  123.0 2.7 fusion.31
  126.2 4.5 convolution_convert_fusion.2
  130.7 186.7 %shard_map.204 = (f32[128,2048]{1,0:T(8,128)}, bf16[8,128,2048]{2,1,0:T(8,128)(2,1)}, bf16[16,128,3072]{2,1,0:T(8,128)(2,1)}) custom-call(bf16[8,128,2048]{2,1,0:T(8,128)(2,1)} %bitcast.188, bf16[128,2048]{1,0:T(8,128)(2,1)} %get-tuple-element.99.x, bf16[4,128,3072]{2,1,0:T(8,128)(2,1)} %pad_maximum_fusion.1.wm), custom_call_target="tpu_custom_call" | custom-call | tf_op jit(solution)/shard_map/pallas_call | solution.py:510
  317.5 10.1 %fusion.4 = f32[1024,1024]{0,1:T(8,128)} fusion(bf16[1024,2048]{1,0:T(8,128)(2,1)} %bitcast.237, bf16[2048,3072]{1,0:T(8,128)(2,1)} %bitcast.230), kind=kOutput, calls=%fused_computation.8 | convolution fusion | flops 4294967296 | bytes 12582912 | tf_op jit(solution)/shard_map/dot_general | solution.py:656
  327.6 6.2 fusion.16
  333.8 10.8 %multiply_convert_fusion = (bf16[1024,1024]{0,1:T(8,128)(2,1)S(1)}, bf16[1024,1024]{0,1:T(8,128)(2,1)S(1)}, bf16[1024,1024]{0,1:T(8,128)(2,1)}) fusion(f32[1024,1024]{0,1:T(8,128)} %fusion.4, f32[1024,1024]{0,1:T(8,128)} %fusion.16, bf16[1024,2048]{1,0:T(8,128)(2,1)} %bitcast.238, bf16[2048,3072]{1,0:T(8,128)(2,1)S(1)} %bitcast.233), kind=kOutput, calls=%fused_computation.19 | convolution fusion | flops 4310695936 | bytes 23068672 | tf_op jit(solution)/shard_map/dot_general | solution.py:656
  344.6 8.9 %convolution_convert_fusion.3.down = bf16[2048,1024]{1,0:T(8,128)(2,1)} fusion(bf16[1024,2048]{1,0:T(8,128)(2,1)} %bitcast.235, bf16[1024,1024]{0,1:T(8,128)(2,1)S(1)} %get-tuple-element.50), kind=kOutput, calls=%fused_computation.28 | convolution fusion | flops 4297064448 | bytes 10485760 | tf_op jit(solution)/shard_map/dot_general | solution.py:656
  353.5 6.2 convolution_convert_fusion.4
  359.7 13.5 %fusion.12 = bf16[1024,2048]{1,0:T(8,128)(2,1)} fusion(bf16[2048,3072]{1,0:T(8,128)(2,1)} %bitcast.231, bf16[1024,1024]{0,1:T(8,128)(2,1)} %get-tuple-element.52, bf16[1024,1024]{0,1:T(8,128)(2,1)S(1)} %get-tuple-element.51), kind=kOutput, calls=%fused_computation.26 | convolution fusion | flops 8600420352 | bytes 16777216 | tf_op jit(solution)/shard_map/dot_general | solution.py:656
  373.2 12.4 %convolution_convert_fusion.gu = bf16[2048,2048]{1,0:T(8,128)(2,1)} fusion(bf16[1024,2048]{1,0:T(8,128)(2,1)S(1)} %bitcast.239, bf16[1024,1024]{0,1:T(8,128)(2,1)S(1)} %copy-done.35, bf16[1024,1024]{0,1:T(8,128)(2,1)S(1)} %get-tuple-element.51), kind=kOutput, calls=%fused_computation.6 | convolution fusion | flops 8602517504 | bytes 16777216 | tf_op jit(solution)/shard_map/dot_general | solution.py:656
  385.7 192.0 %shard_map.205 = (f32[128,2048]{1,0:T(8,128)}, bf16[8,128,2048]{2,1,0:T(8,128)(2,1)}, bf16[256,2048]{1,0:T(8,128)(2,1)}, bf16[8,128,2048]{2,1,0:T(8,128)(2,1)}, bf16[8,128,1024]{2,1,0:T(8,128)(2,1)}) custom-call(bf16[8,128,2048]{2,1,0:T(8,128)(2,1)} %bitcast.196, bf16[8,128,2048]{2,1,0:T(8,128)(2,1)} %bitcast.195, f32[128,2048]{1,0:T(8,128)} %get-tuple-element.31.hid, ...), custom_call_target="tpu_custom_call" | custom-call | tf_op jit(solution)/shard_map/pallas_call | solution.py:565
  577.7 3.7 convolution_convert_fusion.6
  581.4 2.5 convolution_convert_fusion.7
  585.1 3.1 fusion.35
  593.6 2.5 convolution_convert_fusion.5
  596.1 1.8 pad_maximum_fusion.4.ga
  598.8 4.3 convolution_convert_fusion.1
  603.1 59.7 %shard_map.206 = (bf16[256,2048]{1,0:T(8,128)(2,1)}, bf16[8,128,640]{2,1,0:T(8,128)(2,1)}) custom-call(bf16[8,128,2048]{2,1,0:T(8,128)(2,1)} %bitcast.191, f32[128,2048]{1,0:T(8,128)} %get-tuple-element.34.grad_hidden, bf16[128,2048]{1,0:T(8,128)(2,1)} %get-tuple-element.99.x, bf16[2048,640]{1,0:T(8,128)(2,1)} %pad_maximum_fusion.4.ga), custom_call_target="tpu_custom_call" | custom-call | tf_op jit(solution)/shard_map/pallas_call | solution.py:607
  662.9 2.8 convert_element_type.180
  665.6 1.5 convert_element_type.181
  669.3 1.1 copy.72
  670.3 1.1 copy.73
  675.2 1.8 copy.77
  677.1 3.3 convert_element_type.182
  680.3 1.1 slice_add_fusion
  681.4 2.3 slice_bitcast_fusion
  683.7 3.0 copy.75
  686.8 2.9 copy.74
  689.7 4.8 bitcast_multiply_fusion.2
  694.4 3.0 copy.82
  697.5 4.9 psum.7
  702.9 1.8 copy.81
  (147 shorter events, 27.9 us)
Async XLA Ops:
  0.6 12.5 %copy-start.10 = (bf16[256,2048]{1,0:T(8,128)(2,1)S(1)}, bf16[256,2048]{1,0:T(8,128)(2,1)}, u32[]{:S(2)}) copy-start(bf16[256,2048]{1,0:T(8,128)(2,1)} %cot.1) | copy-start | bytes 3145732
  0.7 12.5 %copy-start.9 = (bf16[256,2048]{1,0:T(8,128)(2,1)S(1)}, bf16[256,2048]{1,0:T(8,128)(2,1)}, u32[]{:S(2)}) copy-start(bf16[256,2048]{1,0:T(8,128)(2,1)} %tok.1) | copy-start | bytes 3145732
  1.5 6.7 copy-start.27
  2.1 17.4 %copy-start.29 = (f32[128]{0:T(128)}, f32[128]{0:T(128)S(1)}, u32[]{:S(2)}) copy-start(f32[128]{0:T(128)S(1)} %convert_element_type.162) | copy-start | bytes 1540
  4.4 2.6 copy-start.17
  5.4 1.6 copy-start.19
  8.1 8.7 %copy-start.11 = (bf16[128,1024]{0,1:T(8,128)(2,1)}, bf16[128,1024]{0,1:T(8,128)(2,1)S(1)}, u32[]{:S(2)}) copy-start(bf16[128,1024]{0,1:T(8,128)(2,1)S(1)} %copy.38) | copy-start | bytes 786436
  9.1 5.1 copy-start.15
  14.8 6.1 copy-start.1
  16.8 5.5 copy-start.3
  106.4 3.5 copy-start
  109.8 3.6 copy-start.21
  110.6 4.7 copy-start.7
  115.3 1.1 copy-start.14
  115.5 7.5 %copy-start.23 = (bf16[4,256,64]{1,0,2:T(4,128)(2,1)}, bf16[4,256,64]{1,0,2:T(4,128)(2,1)S(1)}, u32[]{:S(2)}) copy-start(bf16[4,256,64]{1,0,2:T(4,128)(2,1)S(1)} %convert_element_type.155) | copy-start | bytes 393220
  116.5 1.8 slice-start
  123.0 2.7 copy-start.25
  317.4 10.2 %copy-start.31 = (bf16[16,128,3072]{2,1,0:T(8,128)(2,1)S(1)}, bf16[16,128,3072]{2,1,0:T(8,128)(2,1)}, u32[]{:S(2)}) copy-start(bf16[16,128,3072]{2,1,0:T(8,128)(2,1)} %get-tuple-element.29) | copy-start | bytes 37748740
  317.4 10.1 %copy-start.32 = (bf16[4,256,2048]{2,1,0:T(8,128)(2,1)S(1)}, bf16[4,256,2048]{2,1,0:T(8,128)(2,1)}, u32[]{:S(2)}) copy-start(bf16[4,256,2048]{2,1,0:T(8,128)(2,1)} %get-tuple-element.25) | copy-start | bytes 12582916
  359.7 13.5 %copy-start.33 = (bf16[8,128,2048]{2,1,0:T(8,128)(2,1)S(1)}, bf16[8,128,2048]{2,1,0:T(8,128)(2,1)}, u32[]{:S(2)}) copy-start(bf16[8,128,2048]{2,1,0:T(8,128)(2,1)} %get-tuple-element.30) | copy-start | bytes 12582916
  359.7 13.5 %copy-start.35 = (bf16[1024,1024]{0,1:T(8,128)(2,1)S(1)}, bf16[1024,1024]{0,1:T(8,128)(2,1)}, u32[]{:S(2)}) copy-start(bf16[1024,1024]{0,1:T(8,128)(2,1)} %get-tuple-element.52) | copy-start | bytes 6291460
  577.7 3.7 copy-start.34
  585.0 3.5 copy-start.6
  585.1 3.5 copy-start.24
  585.1 3.4 copy-start.26
  591.4 2.2 copy-start.8
  596.1 2.7 copy-start.22
  667.1 4.3 copy-start.18
  667.2 4.3 copy-start.20
  667.2 4.3 copy-start.28
  667.3 5.9 copy-start.12
  668.2 6.2 copy-start.13
  683.7 5.9 copy-start.2
  683.7 5.9 copy-start.4
  683.7 5.9 copy-start.30
  694.4 8.5 %copy-start.5 = (f32[128,4096]{0,1:T(8,128)S(1)}, f32[128,4096]{0,1:T(8,128)}, u32[]{:S(2)}) copy-start(f32[128,4096]{0,1:T(8,128)} %get-tuple-element.87) | copy-start | bytes 6291460
  694.4 10.3 %copy-start.16 = (bf16[256,2048]{1,0:T(8,128)(2,1)S(1)}, bf16[256,2048]{1,0:T(8,128)(2,1)}, u32[]{:S(2)}) copy-start(bf16[256,2048]{1,0:T(8,128)(2,1)} %get-tuple-element.111) | copy-start | bytes 3145732

commit v3 on v2

v3 whole, which is shorter than its diff:
```python
import functools

import jax
import jax.numpy as jnp
from jax import lax
from jax.experimental import pallas as pl
from jax.experimental.pallas import tpu as pltpu
from jax.sharding import PartitionSpec as P

HEAD_DIM = 64
EPSILON = 1e-05
THETA = 500000.0
MESH = pl.DeviceIdType.MESH
ANY = pl.BlockSpec(memory_space=pl.ANY)
VMEM = pl.BlockSpec(memory_space=pltpu.VMEM)
F32 = jnp.float32
BF16 = jnp.bfloat16
DMA = pltpu.SemaphoreType.DMA
COT_AT = 7
OUT_AT = 4


class Place:
    def __init__(self, mid):
        self.mid = mid
        self.d = lax.axis_index("dp")
        self.x = lax.axis_index("tensor")
        self.c = self.d % 2
        self.m = (self.d // 2) % mid
        self.z = self.d // (2 * mid)
        self.lo = self.z % 2

    def dp(self, z, m, c):
        return (z * self.mid + m) * 2 + c

    def peer(self, k):
        return xor(self.z, k // 2), xor(self.c, k % 2)

    def other_m(self, j):
        return (self.m + 1 + j) % self.mid


def xor(a, k):
    if k == 0:
        return a
    low = a % 2
    high = a // 2
    if k % 2:
        low = 1 - low
    if k // 2:
        high = 1 - high
    return high * 2 + low


def remote(src, dst, send, recv, device):
    copy = pltpu.make_async_remote_copy(
        src_ref=src, dst_ref=dst, send_sem=send, recv_sem=recv, device_id=device, device_id_type=MESH
    )
    return copy


def greet(devices):
    barrier = pltpu.get_barrier_semaphore()
    for device in devices:
        pl.semaphore_signal(barrier, inc=1, device_id=device, device_id_type=MESH)
    pl.semaphore_wait(barrier, len(devices))


def arrived(dst, sem):
    pltpu.make_async_copy(dst, dst, sem).wait()


class Gather:
    def __init__(self, p, w, full, sems, waves):
        self.p, self.w, self.full, self.waves = p, w, full, waves
        self.z_s, self.r, self.f_s, self.loc = sems
        self.rows = w.shape[1] // waves
        self.block = p.lo * 2 + p.c
        self.order = list(range(7, 0, -1))
        self.pushes, self.sends = {}, []

    def at(self, wave):
        return pl.ds(wave * self.rows, self.rows)

    def there(self, d, wave):
        return self.full.at[pl.ds(pl.multiple_of(d * self.w.shape[1] + wave * self.rows, 16), self.rows)]

    def push(self, wave):
        p, at = self.p, self.at(wave)
        for k in self.order:
            z, c = p.peer(k)
            copy = remote(
                self.w.at[(z % 2) * 2 + c, at], self.there(p.d, wave), self.z_s.at[k, wave], self.r.at[p.d, wave],
                (p.dp(z, p.m, c), p.x),
            )
            copy.start()
            self.pushes[k, wave] = copy
        self.forward_one(self.w.at[self.block, at], p.d, wave, 0)

    def forward_one(self, src, d, wave, k):
        p = self.p
        for j in range(p.mid - 1):
            copy = remote(
                src, self.there(d, wave), self.f_s.at[k, wave, j], self.r.at[d, wave],
                (p.dp(p.z, p.other_m(j), p.c), p.x),
            )
            copy.start()
            self.sends.append(copy)

    def forward(self, wave):
        p = self.p
        for k in self.order:
            z, c = p.peer(k)
            d = p.dp(z, p.m, c)
            here = self.there(d, wave)
            arrived(here, self.r.at[d, wave])
            self.forward_one(here, d, wave, k)
        if wave == self.waves - 1:
            self.all_forwarded = True

    def start_own(self):
        self.all_forwarded = False
        rows = self.w.shape[1]
        at = pl.ds(pl.multiple_of(self.p.d * rows, 16), rows)
        self.own = pltpu.make_async_copy(self.w.at[self.block], self.full.at[at], self.loc)
        self.own.start()

    def pushed(self, wave):
        for k in self.order:
            self.pushes[k, wave].wait_send()

    def landed(self):
        p = self.p
        for wave in range(self.waves):
            for k in range(8):
                z, c = p.peer(k)
                for j in range(p.mid - 1):
                    d = p.dp(z, p.other_m(j), c)
                    arrived(self.there(d, wave), self.r.at[d, wave])
        self.own.wait()
        self.done = True

    def finish(self):
        if not getattr(self, "done", False):
            self.landed()
        for copy in self.sends:
            copy.wait_send()


def gather_steps(*gathers, lag=2):
    for g in gathers:
        g.start_own()
    items = [(g, wave) for g in gathers for wave in range(g.waves)]
    for n, (g, wave) in enumerate(items):
        if n >= lag:
            before, old = items[n - lag]
            before.pushed(old)
            before.forward(old)
        g.push(wave)
        yield
    for g, wave in items[max(0, len(items) - lag) :]:
        g.pushed(wave)
        g.forward(wave)
        yield
    for g in gathers:
        g.finish()


def gather_sems(mid, waves):
    return [DMA((8, waves)), DMA((8 * mid, waves)), DMA((8, waves, mid - 1)), DMA]


class Scatter:
    def __init__(self, p, g, own, other, out, sems, waves):
        self.p, self.g, self.own, self.other, self.out, self.waves = p, g, own, other, out, waves
        self.y_s, self.y_r, self.z_s, self.z_r, self.load, self.loc = sems
        self.full_rows = own.shape[1]
        self.rows = self.full_rows // waves
        self.order = list(range(7, -1, -1))
        self.y_sends, self.z_sends, self.loads = {}, [], {}
        self.ready = True

    def piece(self, d, wave):
        return self.g.at[pl.ds(pl.multiple_of(d * self.full_rows + wave * self.rows, 16), self.rows)]

    def at(self, wave):
        return pl.ds(wave * self.rows, self.rows)

    def start_loads(self):
        p = self.p
        for wave in range(self.waves):
            for k in self.order:
                z, c = p.peer(k)
                copy = pltpu.make_async_copy(
                    self.piece(p.dp(z, p.m, c), wave), self.own.at[k, self.at(wave)], self.load.at[k, wave]
                )
                copy.start()
                self.loads[k, wave] = copy

    def y_send(self, wave):
        p = self.p
        for k in self.order:
            z, c = p.peer(k)
            for j in range(p.mid - 1):
                m = p.other_m(j)
                there = p.mid - 2 - j
                copy = remote(
                    self.piece(p.dp(z, m, c), wave), self.other.at[there, k, self.at(wave)],
                    self.y_s.at[k, wave, j], self.y_r.at[k, wave, there], (p.dp(p.z, m, p.c), p.x),
                )
                copy.start()
                self.y_sends[k, wave, j] = copy

    def z_push(self, wave):
        p = self.p
        at = self.at(wave)
        me = p.z * 2 + p.c
        for k in self.order:
            z, c = p.peer(k)
            for j in range(p.mid - 1):
                arrived(self.other.at[j, k, at], self.y_r.at[k, wave, j])
            self.loads[k, wave].wait()

            def add(i, carry):
                here = pl.ds(pl.multiple_of(wave * self.rows + i * 16, 16), 16)
                total = self.own[k, here, :].astype(F32)
                for j in range(p.mid - 1):
                    total = total + self.other[j, k, here, :].astype(F32)
                self.own[k, here, :] = total.astype(BF16)
                return carry

            lax.fori_loop(0, self.rows // 16, add, 0)
            src, dst = self.own.at[k, at], self.out.at[me, at]
            if k == 0:
                copy = pltpu.make_async_copy(src, dst, self.loc.at[wave])
                copy.start()
                self.z_sends.append((copy, True))
            else:
                copy = remote(src, dst, self.z_s.at[k, wave], self.z_r.at[me, wave], (p.dp(z, p.m, c), p.x))
                copy.start()
                self.z_sends.append((copy, False))

    def y_sent(self, wave):
        for k in self.order:
            for j in range(self.p.mid - 1):
                self.y_sends[k, wave, j].wait_send()

    def finish(self):
        p = self.p
        for wave in range(self.waves):
            for k in range(1, 8):
                z, c = p.peer(k)
                src = z * 2 + c
                arrived(self.out.at[src, self.at(wave)], self.z_r.at[src, wave])
        for copy, here in self.z_sends:
            copy.wait() if here else copy.wait_send()


def scatter_steps(*scatters, lag=2):
    items = [(s, wave) for s in scatters for wave in range(s.waves)]
    pushed = 0
    for n, (s, wave) in enumerate(items):
        if not s.ready:
            while pushed < n:
                before, old = items[pushed]
                before.z_push(old)
                pushed += 1
            while not s.ready:
                yield
        if wave == 0:
            s.start_loads()
        if n >= lag:
            before, old = items[n - lag]
            before.y_sent(old)
        s.y_send(wave)
        while pushed < n:
            before, old = items[pushed]
            before.z_push(old)
            pushed += 1
        yield
    s, wave = items[-1]
    s.z_push(wave)
    yield
    for s, wave in items[max(0, len(items) - lag) :]:
        s.y_sent(wave)
    for s in scatters:
        s.finish()


def scatter_scratch(mid, rows, width, waves):
    return [
        pltpu.VMEM((8, rows, width), BF16),
        pltpu.VMEM((mid - 1, 8, rows, width), BF16),
        DMA((8, waves, mid - 1)), DMA((8, waves, mid - 1)), DMA((8, waves)), DMA((8, waves)), DMA((8, waves)),
        DMA((waves,)),
    ]


def waves_of(rows, most):
    return max(w for w in range(1, most + 1) if rows % (16 * w) == 0)


def drive(*streams):
    left = list(streams)
    while left:
        for stream in list(left):
            try:
                next(stream)
            except StopIteration:
                left.remove(stream)


def after(steps, stream):
    for _ in range(steps):
        yield
    yield from stream


def chain(*streams):
    for stream in streams:
        yield from stream


def all_devices(p):
    return (
        [(p.dp(z, p.m, c), p.x) for z, c in map(p.peer, range(1, 8))]
        + [(p.dp(p.z, p.other_m(j), p.c), p.x) for j in range(p.mid - 1)]
        + [(p.d, 1 - p.x)]
    )


def token_steps(p, tok, tokg, t_s, t_r, loc, whole):
    rows = tok.shape[0]
    half = rows // 2
    seq = p.lo * 2 + p.c
    z_near = (p.dp(xor(p.z, 1), p.m, p.c), p.x)
    c_near = (p.dp(p.z, p.m, 1 - p.c), p.x)
    x_near = (p.d, 1 - p.x)
    mine = pl.ds(pl.multiple_of(p.x * half, 16), half)
    theirs = pl.ds(pl.multiple_of((1 - p.x) * half, 16), half)
    if whole:
        mine = pl.ds(0, rows)
    far_seq = (1 - p.lo) * 2 + p.c
    c_seq = p.lo * 2 + 1 - p.c
    cc_seq = (1 - p.lo) * 2 + 1 - p.c
    sends = []

    def go(copy):
        copy.start()
        sends.append(copy)

    go(remote(tok.at[mine], tokg.at[seq, mine], t_s.at[0], t_r.at[0], z_near))
    go(remote(tok, tokg.at[seq], t_s.at[1], t_r.at[1], c_near))
    here = pltpu.make_async_copy(tok, tokg.at[seq], loc)
    here.start()
    yield
    arrived(tokg.at[far_seq, mine], t_r.at[0])
    if not whole:
        go(remote(tokg.at[far_seq, mine], tokg.at[far_seq, mine], t_s.at[2], t_r.at[2], x_near))
    go(remote(tokg.at[far_seq, mine], tokg.at[far_seq, mine], t_s.at[3], t_r.at[3], c_near))
    yield
    if not whole:
        arrived(tokg.at[far_seq, theirs], t_r.at[2])
        go(remote(tokg.at[far_seq, theirs], tokg.at[far_seq, theirs], t_s.at[4], t_r.at[4], c_near))
        yield
    here.wait()
    arrived(tokg.at[c_seq], t_r.at[1])
    arrived(tokg.at[cc_seq, mine], t_r.at[3])
    if not whole:
        arrived(tokg.at[cc_seq, theirs], t_r.at[4])
    for copy in sends:
        copy.wait_send()


def token_sems():
    return [DMA((5,)), DMA((5,)), DMA]


def lanes_of(shape):
    return lax.broadcasted_iota(jnp.int32, shape, 1)


def wide_tables(table):
    lanes = lanes_of(table.shape)
    half = HEAD_DIM // 2
    cosine = jnp.where(lanes < half, table, 0.0)
    sine = pltpu.roll(jnp.where((lanes >= half) & (lanes < 2 * half), table, 0.0), 128 - half, 1)
    spread = cosine + pltpu.roll(cosine, half, 1)
    spread = spread + pltpu.roll(spread, 2 * half, 1)
    signed = pltpu.roll(sine, half, 1) - sine
    signed = signed + pltpu.roll(signed, 2 * half, 1)
    return spread, signed


def turn(values, cosine, signed):
    half = HEAD_DIM // 2
    lanes = lanes_of(values.shape) % HEAD_DIM
    swapped = jnp.where(lanes < half, pltpu.roll(values, 128 - half, 1), pltpu.roll(values, half, 1))
    return values * cosine + swapped * signed


def attention_steps(p, tokg, tabg, fa, n1, qkv, probs, mixture, part, gather_a):
    length = tokg.shape[1]
    qw = mixture.shape[1]
    heads = qw // HEAD_DIM
    scaling = HEAD_DIM ** (-0.5)
    for s in range(4):

        def norm(i, carry):
            at = pl.ds(pl.multiple_of(i * 32, 32), 32)
            value = tokg[s, at, :].astype(F32)
            n1[pl.ds(pl.multiple_of(s * length + i * 32, 32), 32), :] = (value * norm_root(value)).astype(BF16)
            return carry

        lax.fori_loop(0, length // 32, norm, 0)
    yield
    while not gather_a.all_forwarded:
        yield
    gather_a.landed()
    for s in range(4):
        here = pl.ds(s * length, length)
        table = tabg[s]
        cosine, signed = wide_tables(table)
        pre = dot(n1[here, :], fa[:, : qw + 128], ((1,), (0,)))
        for b in range(qw // 128):
            at = slice(128 * b, 128 * b + 128)
            qkv[here, at] = turn(pre[:, at], cosine, signed).astype(BF16)
        last = pre[:, qw:]
        keys = turn(last, cosine, signed)
        lanes = lanes_of(last.shape)
        qkv[here, qw:] = jnp.where(lanes < HEAD_DIM, keys, last).astype(BF16)
        key = qkv[here, qw : qw + HEAD_DIM]
        value = qkv[here, qw + HEAD_DIM :]
        begin = table[:, 2 * HEAD_DIM // 2 : 2 * HEAD_DIM // 2 + 1]
        columns = lanes_of((length, length))
        allowed = (columns.astype(F32) >= begin) & (
            columns <= lax.broadcasted_iota(jnp.int32, (length, length), 0)
        )
        for h in range(heads):
            at = slice(HEAD_DIM * h, HEAD_DIM * h + HEAD_DIM)
            scores = dot(qkv[here, at], key, ((1,), (1,))) * scaling
            scores = jnp.where(allowed, scores, -1e30)
            exponent = jnp.exp(scores - jnp.max(scores, axis=-1, keepdims=True))
            share = exponent / jnp.sum(exponent, axis=-1, keepdims=True)
            probs[s, h] = share
            mixture[here, at] = dot(share.astype(BF16), value, ((1,), (0,))).astype(BF16)
        half = length // 2
        for x in range(2):
            rows = pl.ds(s * length + x * half, half)
            part[s * 2 + x] = dot(mixture[rows, :], fa[:, qw + 128 :], ((1,), (1,))).astype(BF16)
        yield


def first_kernel(
    mid, a_waves, waves, tok, cot, table, wa, wg, wu, wd,
    cotg, tabg, fa, fg, fu, fd, n1, qkv, probs, mixture, hidden, n2, *scratch
):
    p = Place(mid)
    scratch = list(scratch)

    def take(count):
        taken = scratch[:count]
        del scratch[:count]
        return taken

    tokg, part = take(2)
    tok_sems, cot_sems, tab_sems = take(3), take(3), take(3)
    reduce_refs, share_refs = take(10), take(2)
    greet(all_devices(p))
    gather_a = Gather(p, wa, fa, take(4), a_waves)
    rest = [Gather(p, w, f, take(4), waves) for w, f in ((wg, fg), (wu, fu), (wd, fd))]
    seq = p.lo * 2 + p.c
    mine = seq * 2 + p.x
    half = hidden.shape[0]

    def finish(at, total):
        there = pl.ds(pl.multiple_of(p.x * half + at.start, 16), 16)
        value = tokg[seq, there, :].astype(F32) + total
        hidden[at, :] = value
        n2[mine, at, :] = (value * norm_root(value)).astype(BF16)

    tab = token_steps(p, table, tabg, *tab_sems, whole=True)
    tokens = token_steps(p, tok, tokg, *tok_sems, whole=False)
    next(tokens)
    next(tab)
    drive(
        gather_steps(gather_a, *rest),
        chain(
            tokens,
            attention_steps(p, tokg, tabg, fa, n1, qkv, probs, mixture, part, gather_a),
            reduce_steps(p, part, reduce_refs, finish),
            share_steps(p, n2, *share_refs),
        ),
        tab,
        after(COT_AT, token_steps(p, cot, cotg, *cot_sems, whole=False)),
    )


def first(mid, tok, cot, table, wa, wg, wu, wd, qw):
    a_waves, waves = waves_of(wa.shape[1], 4), waves_of(wg.shape[1], 4)
    length, width = tok.shape
    n = 8 * mid
    heads = qw // HEAD_DIM

    def full(w):
        return jax.ShapeDtypeStruct((n * w.shape[1], w.shape[2]), BF16)

    return pl.pallas_call(
        functools.partial(first_kernel, mid, a_waves, waves),
        out_shape=(
            jax.ShapeDtypeStruct((4,) + cot.shape, BF16),
            jax.ShapeDtypeStruct((4,) + table.shape, F32),
            full(wa), full(wg), full(wu), full(wd),
            jax.ShapeDtypeStruct((4 * length, width), BF16),
            jax.ShapeDtypeStruct((4 * length, qw + 128), BF16),
            jax.ShapeDtypeStruct((4, heads, length, length), F32),
            jax.ShapeDtypeStruct((4 * length, qw), BF16),
            jax.ShapeDtypeStruct((length // 2, width), F32),
            jax.ShapeDtypeStruct((8, length // 2, width), BF16),
        ),
        in_specs=[ANY] * 7,
        out_specs=(ANY, VMEM, VMEM, ANY, ANY, ANY) + (VMEM,) * 6,
        scratch_shapes=[
            pltpu.VMEM((4, length, width), BF16),
            pltpu.VMEM((8, length // 2, width), BF16),
        ]
        + token_sems() * 3
        + reduce_scratch(length // 2, width)
        + [DMA((7,)), DMA((7,))]
        + gather_sems(mid, a_waves)
        + gather_sems(mid, waves) * 3,
        compiler_params=pltpu.CompilerParams(
            collective_id=0, has_side_effects=True, vmem_limit_bytes=60 << 20
        ),
    )(tok, cot, table, wa, wg, wu, wd)


def reduce_steps(p, part, scratch, finish):
    abuf, sums, bbuf, cbuf, a_s, a_r, b_s, b_r, c_s, c_r = scratch
    sibling = (p.dp(p.z, p.m, 1 - p.c), p.x)
    x_near = (p.d, 1 - p.x)
    z_near = (p.dp(xor(p.z, 1), p.m, p.c), p.x)
    order = ((1, 1), (0, 1), (1, 0), (0, 0))
    sends = []

    def owner(n, c):
        fz, fx = order[n]
        return (xor(p.lo, fz) * 2 + c) * 2 + xor(p.x, fx)

    def go(copy):
        copy.start()
        sends.append(copy)

    for n in range(4):
        go(remote(part.at[owner(n, 1 - p.c)], abuf.at[n], a_s.at[n], a_r.at[n], sibling))
    yield
    rows = part.shape[1]
    step = 16

    def add(n, *more):
        own = owner(n, p.c)

        def body(i, carry):
            at = pl.ds(pl.multiple_of(i * step, step), step)
            total = part[own, at, :].astype(F32) + abuf[n, at, :].astype(F32)
            for other in more:
                total = total + other[at, :].astype(F32)
            sums[n, at, :] = total.astype(BF16)
            return carry

        lax.fori_loop(0, rows // step, body, 0)

    for n in range(2):
        arrived(abuf.at[n], a_r.at[n])
        add(n)
        go(remote(sums.at[n], bbuf.at[n], b_s.at[n], b_r.at[n], x_near))
    yield
    arrived(abuf.at[2], a_r.at[2])
    arrived(bbuf.at[0], b_r.at[0])
    add(2, bbuf.at[0])
    go(remote(sums.at[2], cbuf, c_s, c_r, z_near))
    yield
    arrived(abuf.at[3], a_r.at[3])
    arrived(bbuf.at[1], b_r.at[1])
    arrived(cbuf, c_r)
    mine = owner(3, p.c)

    def last(i, carry):
        at = pl.ds(pl.multiple_of(i * step, step), step)
        total = part[mine, at, :].astype(F32) + abuf[3, at, :].astype(F32)
        finish(at, total + bbuf[1, at, :].astype(F32) + cbuf[at, :].astype(F32))
        return carry

    lax.fori_loop(0, rows // step, last, 0)
    for copy in sends:
        copy.wait_send()


def share_steps(p, gathered, s, r):
    sibling = (p.dp(p.z, p.m, 1 - p.c), p.x)
    x_near = (p.d, 1 - p.x)
    z_near = (p.dp(xor(p.z, 1), p.m, p.c), p.x)
    sends = []

    def at(fz, fx, c):
        return gathered.at[(xor(p.lo, fz) * 2 + c) * 2 + xor(p.x, fx)]

    def go(ref, number, device):
        copy = remote(ref, ref, s.at[number], r.at[number], device)
        copy.start()
        sends.append(copy)

    own = at(0, 0, p.c)
    go(own, 0, z_near)
    go(own, 1, x_near)
    go(own, 2, sibling)
    yield
    far = at(1, 0, p.c)
    arrived(far, r.at[0])
    go(far, 3, x_near)
    go(far, 4, sibling)
    beside = at(0, 1, p.c)
    arrived(beside, r.at[1])
    go(beside, 5, sibling)
    yield
    across = at(1, 1, p.c)
    arrived(across, r.at[3])
    go(across, 6, sibling)
    yield
    for number, (fz, fx) in ((2, (0, 0)), (4, (1, 0)), (5, (0, 1)), (6, (1, 1))):
        arrived(at(fz, fx, 1 - p.c), r.at[number])
    for copy in sends:
        copy.wait_send()


def swap_steps(p, both, o_s, o_r):
    rows = both.shape[0] // 2
    half = pl.ds(pl.multiple_of(p.x * rows, 16), rows)
    copy = remote(both.at[half], both.at[half], o_s, o_r, (p.d, 1 - p.x))
    copy.start()
    yield
    copy.wait()


def norm_root(value):
    return lax.rsqrt(jnp.mean(value * value, axis=-1, keepdims=True) + EPSILON)


def norm_back(value, scaled):
    root = norm_root(value)
    return root * scaled - value * root**3 * jnp.mean(value * scaled, axis=-1, keepdims=True)


def reduce_scratch(rows, width):
    return [
        pltpu.VMEM((4, rows, width), BF16),
        pltpu.VMEM((3, rows, width), BF16),
        pltpu.VMEM((2, rows, width), BF16),
        pltpu.VMEM((rows, width), BF16),
        DMA((4,)), DMA((4,)), DMA((2,)), DMA((2,)), DMA, DMA,
    ]


def attention_back_steps(p, low, qkv, probs, p_buf, p_sem, mixture, fa, tabg, n1, n1_copy, gqkv, part, ga, a_scatter):
    length = qkv.shape[0] // 4
    half = length // 2
    qw = mixture.shape[1]
    heads = qw // HEAD_DIM
    scaling = HEAD_DIM ** (-0.5)

    def fetch(s):
        return pltpu.make_async_copy(probs.at[s], p_buf.at[s % 2], p_sem.at[s % 2])

    fetch(0).start()
    for s in range(4):
        if s < 3:
            fetch(s + 1).start()
        fetch(s).wait()
        here = pl.ds(s * length, length)
        cosine, signed = wide_tables(tabg[s])
        grads = low[2 * s : 2 * s + 2].reshape(length, low.shape[2])
        grad_mix = dot(grads, fa[:, qw + 128 :], ((1,), (0,))).astype(BF16)
        key = qkv[here, qw : qw + HEAD_DIM]
        value = qkv[here, qw + HEAD_DIM :]
        grad_value = jnp.zeros((length, HEAD_DIM), F32)
        grad_key = jnp.zeros((length, HEAD_DIM), F32)
        grad_query = []
        for h in range(heads):
            at = slice(HEAD_DIM * h, HEAD_DIM * h + HEAD_DIM)
            share = p_buf[s % 2, h]
            gm = grad_mix[:, at]
            gp = dot(gm, value, ((1,), (1,)))
            grad_value = grad_value + dot(share.astype(BF16), gm, ((0,), (0,)))
            centered = jnp.sum(share * gp, axis=-1, keepdims=True)
            gs = (share * (gp - centered)).astype(BF16)
            grad_query.append(dot(gs, key, ((1,), (0,))) * scaling)
            grad_key = grad_key + dot(gs, qkv[here, at], ((0,), (0,))) * scaling
        for b in range(qw // 128):
            pair = jnp.concatenate(grad_query[2 * b : 2 * b + 2], axis=1)
            gqkv[here, 128 * b : 128 * b + 128] = turn(pair, cosine, -signed).astype(BF16)
        pair = jnp.concatenate([grad_key, grad_value], axis=1)
        lanes = lanes_of(pair.shape)
        gqkv[here, qw:] = jnp.where(lanes < HEAD_DIM, turn(pair, cosine, -signed), pair).astype(BF16)
        for x in range(2):
            rows = pl.ds(s * length + x * half, half)
            part[s * 2 + x] = dot(gqkv[rows, :], fa[:, : qw + 128], ((1,), (1,))).astype(BF16)
        yield


def weight_grad_steps(low, mixture, n1, n1_copy, gqkv, ga, a_scatter):
    qw = mixture.shape[1]
    n1_copy.wait()
    width = low.shape[2]
    tile = 256

    def body(i, carry):
        at = pl.ds(pl.multiple_of(i * tile, tile), tile)
        rows = n1[:, :, at].reshape(-1, tile)
        ga[at, : qw + 128] = dot(rows, gqkv[...], ((0,), (0,))).astype(BF16)
        rows = low[:, :, at].reshape(-1, tile)
        ga[at, qw + 128 :] = dot(rows, mixture[...], ((0,), (0,))).astype(BF16)
        return carry

    lax.fori_loop(0, width // tile, body, 0)
    a_scatter.ready = True
    yield


def last_kernel(
    mid, a_waves, d_waves, g_waves, part_two, out_part, n1, probs, hid, cot, x, qkv, mixture, fa, tabg, gu, down,
    output, result, gu_out, down_out, ga_out, *scratch
):
    p = Place(mid)
    scratch = list(scratch)

    def take(count):
        taken = scratch[:count]
        del scratch[:count]
        return taken

    first_buf, second_buf, grad_hidden, low, gqkv, ga, p_buf, p_sem, in_sems = take(9)
    r1, r2, r3 = take(10), take(10), take(10)
    g_sems, o_sems, i_sems = take(2), take(2), take(2)
    gu_s, down_s, ga_s = take(8), take(8), take(8)
    loads = [
        pltpu.make_async_copy(part_two, first_buf, in_sems.at[0]),
        pltpu.make_async_copy(out_part, second_buf, in_sems.at[1]),
        pltpu.make_async_copy(n1, second_buf, in_sems.at[2]),
    ]
    loads[0].start()
    loads[1].start()
    greet(all_devices(p))
    mine = (p.lo * 2 + p.c) * 2 + p.x
    rows = hid.shape[0]

    def there(at):
        return pl.ds(pl.multiple_of(p.x * rows + at.start, 16), 16)

    def finish(at, total):
        grads = cot[at, :].astype(F32) + norm_back(hid[at, :], total)
        grad_hidden[at, :] = grads
        low[mine, at, :] = grads.astype(BF16)

    def finish_out(at, total):
        output[there(at), :] = (hid[at, :] + total).astype(BF16)

    def finish_in(at, total):
        result[there(at), :] = (grad_hidden[at, :] + norm_back(x[at, :].astype(F32), total)).astype(BF16)

    scatter_d = Scatter(p, down, down_s[0], down_s[1], down_out, down_s[2:], d_waves)
    scatter_g = Scatter(p, gu, gu_s[0], gu_s[1], gu_out, gu_s[2:], g_waves)
    scatter_a = Scatter(p, ga, ga_s[0], ga_s[1], ga_out, ga_s[2:], a_waves)
    scatter_a.ready = False

    def outputs():
        loads[1].wait()
        yield from reduce_steps(p, second_buf, r2, finish_out)
        loads[2].start()
        yield from swap_steps(p, output, *o_sems)

    out = outputs()

    def chained():
        loads[0].wait()
        yield from reduce_steps(p, first_buf, r1, finish)
        yield from share_steps(p, low, *g_sems)
        yield from attention_back_steps(
            p, low, qkv, probs, p_buf, p_sem, mixture, fa, tabg, second_buf, loads[2], gqkv, first_buf, ga, scatter_a
        )
        for _ in out:
            pass
        last = reduce_steps(p, first_buf, r3, finish_in)
        next(last)
        yield from weight_grad_steps(low, mixture, second_buf, loads[2], gqkv, ga, scatter_a)
        yield from last
        yield from swap_steps(p, result, *i_sems)

    drive(scatter_steps(scatter_d, scatter_g, scatter_a), chained(), after(OUT_AT, out))


def last(mid, part_two, out_part, n1, probs, hid, cot, x, qkv, mixture, fa, tabg, gu, down):
    eight, rows, width = part_two.shape
    n = 8 * mid
    w_rows = gu.shape[0] // n
    a_waves, d_waves, g_waves = waves_of(w_rows, 4), waves_of(w_rows, 4), waves_of(w_rows, 8)
    return pl.pallas_call(
        functools.partial(last_kernel, mid, a_waves, d_waves, g_waves),
        out_shape=(
            jax.ShapeDtypeStruct((2 * rows, width), BF16),
            jax.ShapeDtypeStruct((2 * rows, width), BF16),
            jax.ShapeDtypeStruct((8, w_rows, gu.shape[1]), BF16),
            jax.ShapeDtypeStruct((8, w_rows, down.shape[1]), BF16),
            jax.ShapeDtypeStruct((8, w_rows, fa.shape[1]), BF16),
        ),
        in_specs=[ANY] * 4 + [VMEM] * 7 + [ANY] * 2,
        out_specs=(VMEM,) * 2 + (ANY,) * 3,
        scratch_shapes=[
            pltpu.VMEM((eight, rows, width), BF16),
            pltpu.VMEM((eight, rows, width), BF16),
            pltpu.VMEM((rows, width), F32),
            pltpu.VMEM((eight, rows, width), BF16),
            pltpu.VMEM(qkv.shape, BF16),
            pltpu.VMEM(fa.shape, BF16),
            pltpu.VMEM((2,) + probs.shape[1:], F32),
            DMA((2,)),
            DMA((3,)),
        ]
        + reduce_scratch(rows, width) * 3
        + [DMA((7,)), DMA((7,)), DMA, DMA, DMA, DMA]
        + scatter_scratch(mid, w_rows, gu.shape[1], g_waves)
        + scatter_scratch(mid, w_rows, down.shape[1], d_waves)
        + scatter_scratch(mid, w_rows, fa.shape[1], a_waves),
        compiler_params=pltpu.CompilerParams(
            collective_id=1, has_side_effects=True, vmem_limit_bytes=60 << 20
        ),
    )(part_two, out_part, n1, probs, hid, cot, x, qkv, mixture, fa, tabg, gu, down)


def token_table(segments):
    length = segments.shape[0]
    places = jnp.arange(length, dtype=jnp.int32)
    earlier = jnp.concatenate([segments[:1], segments[:-1]])
    begins = jnp.where(segments != earlier, places, 0)
    begin = jnp.max(jnp.where(places[:, None] >= places[None, :], begins[None, :], 0), axis=-1)
    halves = HEAD_DIM // 2
    inverse = THETA ** (-2.0 * jnp.arange(halves, dtype=F32) / HEAD_DIM)
    angles = (places - begin).astype(F32)[:, None] * inverse
    wide = jnp.broadcast_to(begin.astype(F32)[:, None], (length, 128 - 2 * halves))
    return jnp.concatenate([jnp.cos(angles), jnp.sin(angles), wide], axis=-1)


def dot(a, b, dims):
    return lax.dot_general(a, b, (dims, ((), ())), preferred_element_type=F32)


def local(
    mid, tokens, attn_gain, w_query, w_key, w_value, w_out, mlp_gain, w_gate, w_up, w_down, segment_ids, cotangent
):
    length, width = tokens.shape
    half = length // 2
    rows = w_query.shape[0]
    x_at = lax.axis_index("tensor")

    def blocks(w):
        return w.reshape(rows, 4, w.shape[1] // 4).transpose(1, 0, 2)

    gain_one, gain_two = attn_gain.astype(F32)[:, None], mlp_gain.astype(F32)[:, None]

    def scaled(w, gain):
        return blocks((w.astype(F32) * gain).astype(BF16))

    wg, wu, wd = scaled(w_gate, gain_two), scaled(w_up, gain_two), blocks(w_down.T)
    wa = jnp.concatenate(
        [scaled(w_query, gain_one), scaled(w_key, gain_one), scaled(w_value, gain_one), blocks(w_out.T)], axis=-1
    )
    units = w_gate.shape[1] // 4
    qw, kw = w_query.shape[1] // 4, w_key.shape[1] // 4
    heads = qw // HEAD_DIM
    cotg, tabg, fa, gate_w, up_w, down_t, normed, qkv, probs, mixture, hidden, n2 = first(
        mid, tokens, cotangent, token_table(segment_ids), wa, wg, wu, wd, qw
    )
    own_x = lax.dynamic_slice_in_dim(tokens, x_at * half, half, 0)
    own_cot = lax.dynamic_slice_in_dim(cotangent, x_at * half, half, 0)
    n2 = n2.reshape(4 * length, width)

    gate = dot(n2, gate_w, ((1,), (0,)))
    up = dot(n2, up_w, ((1,), (0,)))
    sigmoid = 1.0 / (1.0 + jnp.exp(-gate))
    silu = gate / (1.0 + jnp.exp(-gate))
    activated = (silu * up).astype(BF16)
    out_part = dot(activated, down_t, ((1,), (1,))).astype(BF16)
    cots = cotg.reshape(4 * length, width)
    grad_act = dot(cots, down_t, ((1,), (0,)))
    grad_gate = (grad_act * up * sigmoid * (1.0 + gate * (1.0 - sigmoid))).astype(BF16)
    grad_up = (grad_act * silu).astype(BF16)
    part_two = (dot(grad_gate, gate_w, ((1,), (1,))) + dot(grad_up, up_w, ((1,), (1,)))).astype(BF16)
    down_g = dot(cots, activated, ((0,), (0,))).astype(BF16)
    gu_g = dot(n2, jnp.concatenate([grad_gate, grad_up], axis=1), ((0,), (0,))).astype(BF16)

    eight = (8, half, width)
    output, input_grad, gu_parts, down_parts, a_parts = last(
        mid, part_two.reshape(eight), out_part.reshape(eight), normed.reshape(eight), probs, hidden, own_cot, own_x,
        qkv, mixture, fa, tabg, gu_g, down_g
    )

    def total(parts):
        parts = parts.reshape(2, 4, rows, -1).astype(F32)
        return parts[0] + parts[1]

    def across(block):
        return block.transpose(1, 0, 2).reshape(rows, -1)

    def down(block):
        return block.transpose(0, 2, 1).reshape(-1, rows)

    t_gate, t_up = jnp.split(total(gu_parts), 2, axis=-1)
    t_q, t_k, t_v, t_out = jnp.split(total(a_parts), [qw, qw + kw, qw + 2 * kw], axis=-1)
    t_gate, t_up, t_q, t_k, t_v = (across(t) for t in (t_gate, t_up, t_q, t_k, t_v))

    def gain_grad(*pairs):
        return sum(jnp.sum(w.astype(F32) * g, axis=1) for w, g in pairs)

    gain_grads = jnp.stack(
        [gain_grad((w_query, t_q), (w_key, t_k), (w_value, t_v)), gain_grad((w_gate, t_gate), (w_up, t_up))]
    )
    gain_grads = lax.psum(gain_grads, "tensor")
    return (
        output,
        input_grad.astype(F32),
        gain_grads[0],
        t_q * gain_one,
        t_k * gain_one,
        t_v * gain_one,
        down(t_out),
        gain_grads[1],
        t_gate * gain_two,
        t_up * gain_two,
        down(total(down_parts)),
    )


def solution(mesh):
    in_specs = (
        P("dp", None), P("dp"), P("dp", "tensor"), P("dp", "tensor"), P("dp", "tensor"), P("tensor", "dp"),
        P("dp"), P("dp", "tensor"), P("dp", "tensor"), P("tensor", "dp"), P("dp"), P("dp", None),
    )
    out_specs = (
        P("dp", None), P("dp", None), P("dp"), P("dp", "tensor"), P("dp", "tensor"), P("dp", "tensor"),
        P("tensor", "dp"), P("dp"), P("dp", "tensor"), P("dp", "tensor"), P("tensor", "dp"),
    )
    return jax.shard_map(
        functools.partial(local, mesh.shape["dp"] // 8),
        mesh=mesh, in_specs=in_specs, out_specs=out_specs, check_vma=False,
    )
```

time: 710 us -> 580 us (0.82)
  Pallas kernels: 519 us -> 433 us
  matrix products: 98.8 us -> 71.1 us
  other arithmetic: 32.8 us -> 21.7 us
  local copies, waits for them, and re-layouts: 48.8 us -> 38.1 us
    pallas_call x4 -> x2, Pallas kernels: 519 us -> 433 us  [the longest x1 224 us: first(): pl.pallas_call(functools.partial(first_kernel, mid, a_waves, waves), out_...]
    dot_general x13 -> x8, matrix products: 87.5 us -> 71.1 us  [dot(): return lax.dot_general(a, b, (dims, ((), ())), preferred_element_type=F32)]
    dot_general x5 -> x0, matrix products: 7.79 us -> none  [the longest x1 3.1 us: local(): jnp.einsum('sgqp,sqgd->spd', probs_low, gm, preferred_element_type=F32)]
    unnamed x93 -> x45, local copies, waits for them, and re-layouts: 17.4 us -> 13.5 us
where the time goes in v3:
time: 580 us; the launch traced here: 570 us
  Pallas kernels  433 us (75%)
  matrix products  71.1 us (12%)
  local copies, waits for them, and re-layouts  38.1 us (7%)
  other arithmetic  21.7 us (4%)
    pallas_call x1, Pallas kernels, first(): pl.pallas_call(functools.partial(first_kernel, mid, a_waves, waves), out_...  224 us
    pallas_call x1, Pallas kernels, last(): pl.pallas_call(functools.partial(last_kernel, mid, a_waves, d_waves, g_wa...  209 us
    dot_general x8, matrix products, dot(): return lax.dot_general(a, b, (dims, ((), ())), preferred_element_type=F32)  71.1 us
    unnamed x45, local copies, waits for them, and re-layouts  13.5 us

profile of v3, /device:TPU:0, one launch (start us, length us, event | category | flops | bytes accessed | tf_op | source)
XLA Modules:
  0.0 569.9 jit_solution(15347508630438680459)
XLA Ops:
  0.7 1.3 slice.36
  1.9 1.5 compare_select_fusion
  3.7 0.5 multiply_cosine_fusion
  4.2 0.8 pad_maximum_fusion.1.table
  5.0 1.1 copy.78
  6.1 1.0 copy.74
  7.0 0.7 convert_element_type.94
  7.7 0.9 copy.76
  9.0 1.1 copy.72
  10.3 1.0 pad_maximum_fusion.wa
  11.3 0.7 copy.81
  12.0 0.7 copy.79
  12.7 1.4 fusion.6
  14.1 2.3 copy.80
  16.3 1.3 copy.82
  17.6 2.3 copy.83
  19.9 223.5 %shard_map.203 = (bf16[4,256,2048]{2,1,0:T(8,128)(2,1)}, f32[4,256,128]{2,1,0:T(8,128)}, bf16[2048,640]{1,0:T(8,128)(2,1)}, bf16[2048,1024]{1,0:T(8,128)(2,1)}, ...) custom-call(bf16[256,2048]{1,0:T(8,128)(2,1)} %tok.1, ...), custom_call_target="tpu_custom_call" | custom-call | tf_op jit(solution)/shard_map/pallas_call | solution.py:508
  243.5 10.1 %fusion.17 = f32[1024,1024]{0,1:T(8,128)} fusion(bf16[1024,2048]{1,0:T(8,128)(2,1)} %bitcast.100, bf16[2048,1024]{1,0:T(8,128)(2,1)} %get-tuple-element.32), kind=kOutput, calls=%fused_computation.65 | convolution fusion | flops 4294967296 | bytes 12582912 | tf_op jit(solution)/shard_map/dot_general | solution.py:853
  253.6 6.1 %fusion.16 = f32[1024,1024]{0,1:T(8,128)} fusion(bf16[1024,2048]{1,0:T(8,128)(2,1)S(1)} %bitcast.98, bf16[2048,1024]{1,0:T(8,128)(2,1)S(1)} %copy-done.10), kind=kOutput, calls=%fused_computation.64 | convolution fusion | flops 4294967296 | bytes 12582912 | tf_op jit(solution)/shard_map/dot_general | solution.py:853
  259.7 11.0 %multiply_convert_fusion = (bf16[1024,1024]{0,1:T(8,128)(2,1)}, bf16[1024,1024]{0,1:T(8,128)(2,1)}, bf16[1024,1024]{0,1:T(8,128)(2,1)}) fusion(f32[1024,1024]{0,1:T(8,128)} %fusion.17, f32[1024,1024]{0,1:T(8,128)} %fusion.16, bf16[1024,2048]{1,0:T(8,128)(2,1)S(1)} %bitcast.102, bf16[2048,1024]{1,0:T(8,128)(2,1)S(1)} %copy-done.11), kind=kOutput, calls=%fused_computation.6 | convolution fusion | flops 4310695936 | bytes 23068672 | tf_op jit(solution)/shard_map/dot_general | solution.py:853
  270.7 8.6 %fusion.18 = f32[1024,2048]{1,0:T(8,128)} fusion(bf16[1024,1024]{0,1:T(8,128)(2,1)} %get-tuple-element.79, bf16[2048,1024]{1,0:T(8,128)(2,1)S(1)} %copy-done.12), kind=kOutput, calls=%fused_computation.66 | convolution fusion | flops 4294967296 | bytes 14680064 | tf_op jit(solution)/shard_map/dot_general | solution.py:853
  279.2 8.6 %add_convert_fusion = bf16[1024,2048]{1,0:T(8,128)(2,1)} fusion(f32[1024,2048]{1,0:T(8,128)} %fusion.18, bf16[1024,1024]{0,1:T(8,128)(2,1)S(1)} %copy-done.14, bf16[2048,1024]{1,0:T(8,128)(2,1)S(1)} %copy-done.11), kind=kOutput, calls=%fused_computation | convolution fusion | flops 4299161600 | bytes 18874368 | tf_op jit(solution)/shard_map/dot_general | solution.py:853
  287.8 6.2 %convolution_convert_fusion.2 = bf16[1024,2048]{1,0:T(8,128)(2,1)} fusion(bf16[1024,1024]{0,1:T(8,128)(2,1)S(1)} %copy-done.15, bf16[2048,1024]{1,0:T(8,128)(2,1)S(1)} %copy-done.10), kind=kOutput, calls=%fused_computation.12 | convolution fusion | flops 4297064448 | bytes 10485760 | tf_op jit(solution)/shard_map/dot_general | solution.py:853
  294.0 2.1 constant_dynamic-slice_fusion
  296.1 14.3 %convolution_convert_fusion.gu = bf16[2048,2048]{1,0:T(8,128)(2,1)} fusion(bf16[1024,2048]{1,0:T(8,128)(2,1)} %bitcast.101, bf16[1024,1024]{0,1:T(8,128)(2,1)} %get-tuple-element.80, bf16[1024,1024]{0,1:T(8,128)(2,1)} %get-tuple-element.79), kind=kOutput, calls=%fused_computation.1 | convolution fusion | flops 8602517504 | bytes 16777216 | tf_op jit(solution)/shard_map/dot_general | solution.py:853
  310.3 6.4 %convolution_convert_fusion.1.down = bf16[2048,1024]{1,0:T(8,128)(2,1)} fusion(bf16[1024,2048]{1,0:T(8,128)(2,1)S(1)} %bitcast.99, bf16[1024,1024]{0,1:T(8,128)(2,1)S(1)} %copy-done.16), kind=kOutput, calls=%fused_computation.11 | convolution fusion | flops 4297064448 | bytes 10485760 | tf_op jit(solution)/shard_map/dot_general | solution.py:853
  316.7 209.0 %shard_map.204 = (bf16[256,2048]{1,0:T(8,128)(2,1)}, bf16[256,2048]{1,0:T(8,128)(2,1)}, bf16[8,128,2048]{2,1,0:T(8,128)(2,1)}, bf16[8,128,1024]{2,1,0:T(8,128)(2,1)}, bf16[8,128,640]{2,1,0:T(8,128)(2,1)}) custom-call(bf16[8,128,2048]{2,1,0:T(8,128)(2,1)} %bitcast.79, bf16[8,128,2048]{2,1,0:T(8,128)(2,1)} %bitcast.80, bf16[8,128,2048]{2,1,0:T(8,128)(2,1)} %bitcast.78, ...), custom_call_target="tpu_custom_call" | custom-call | tf_op jit(solution)/shard_map/pallas_call | solution.py:806
  525.7 2.8 convert_element_type.112
  528.5 3.3 convert_element_type.114
  531.8 1.1 slice_add_fusion
  532.8 2.3 slice_bitcast_fusion
  535.2 2.9 copy.88
  538.0 2.9 copy.87
  540.9 4.9 bitcast_multiply_fusion
  546.5 0.7 bitcast_multiply_fusion.3
  547.3 0.9 slice_bitcast_fusion.2
  548.5 5.1 psum.7
  553.6 0.5 slice_bitcast_fusion.6
  554.1 1.0 copy.91
  555.1 1.7 copy.92
  556.8 0.8 copy.93
  557.5 2.0 copy.89
  559.6 2.9 copy.94
  562.5 1.8 copy.95
  564.3 2.0 convert_element_type.115
  566.3 0.4 fusion.8
  566.7 1.8 copy.90
  568.5 1.0 copy.97
  (54 shorter events, 1.8 us)
Async XLA Ops:
  0.6 10.7 %copy-start.3 = (bf16[128,4096]{1,0:T(8,128)(2,1)S(1)}, bf16[128,4096]{1,0:T(8,128)(2,1)}, u32[]{:S(2)}) copy-start(bf16[128,4096]{1,0:T(8,128)(2,1)} %param.20) | copy-start | bytes 3145732
  0.7 11.3 %copy-start.13 = (bf16[128]{0:T(256)(128)(2,1)S(1)}, bf16[128]{0:T(256)(128)(2,1)}, u32[]{:S(2)}) copy-start(bf16[128]{0:T(256)(128)(2,1)} %param.18) | copy-start | bytes 772
  10.3 1.7 copy-start.4
  243.4 10.1 %copy-start.7 = (bf16[4,256,2048]{2,1,0:T(8,128)(2,1)S(1)}, bf16[4,256,2048]{2,1,0:T(8,128)(2,1)}, u32[]{:S(2)}) copy-start(bf16[4,256,2048]{2,1,0:T(8,128)(2,1)} %get-tuple-element.28) | copy-start | bytes 12582916
  243.5 10.1 %copy-start.10 = (bf16[2048,1024]{1,0:T(8,128)(2,1)S(1)}, bf16[2048,1024]{1,0:T(8,128)(2,1)}, u32[]{:S(2)}) copy-start(bf16[2048,1024]{1,0:T(8,128)(2,1)} %get-tuple-element.29) | copy-start | bytes 12582916
  253.6 6.2 %copy-start.9 = (bf16[8,128,2048]{2,1,0:T(8,128)(2,1)S(1)}, bf16[8,128,2048]{2,1,0:T(8,128)(2,1)}, u32[]{:S(2)}) copy-start(bf16[8,128,2048]{2,1,0:T(8,128)(2,1)} %get-tuple-element.30) | copy-start | bytes 12582916
  253.6 6.2 %copy-start.11 = (bf16[2048,1024]{1,0:T(8,128)(2,1)S(1)}, bf16[2048,1024]{1,0:T(8,128)(2,1)}, u32[]{:S(2)}) copy-start(bf16[2048,1024]{1,0:T(8,128)(2,1)} %get-tuple-element.31) | copy-start | bytes 12582916
  259.7 11.0 %copy-start.12 = (bf16[2048,1024]{1,0:T(8,128)(2,1)S(1)}, bf16[2048,1024]{1,0:T(8,128)(2,1)}, u32[]{:S(2)}) copy-start(bf16[2048,1024]{1,0:T(8,128)(2,1)} %get-tuple-element.32) | copy-start | bytes 12582916
  270.7 8.6 %copy-start.14 = (bf16[1024,1024]{0,1:T(8,128)(2,1)S(1)}, bf16[1024,1024]{0,1:T(8,128)(2,1)}, u32[]{:S(2)}) copy-start(bf16[1024,1024]{0,1:T(8,128)(2,1)} %get-tuple-element.80) | copy-start | bytes 6291460
  279.2 8.6 %copy-start.15 = (bf16[1024,1024]{0,1:T(8,128)(2,1)S(1)}, bf16[1024,1024]{0,1:T(8,128)(2,1)}, u32[]{:S(2)}) copy-start(bf16[1024,1024]{0,1:T(8,128)(2,1)} %get-tuple-element.78) | copy-start | bytes 6291460
  287.8 6.2 %copy-start.1 = (bf16[256,2048]{1,0:T(8,128)(2,1)S(1)}, bf16[256,2048]{1,0:T(8,128)(2,1)}, u32[]{:S(2)}) copy-start(bf16[256,2048]{1,0:T(8,128)(2,1)} %tok.1) | copy-start | bytes 3145732
  296.0 14.3 %copy-start.8 = (bf16[4,256,2048]{2,1,0:T(8,128)(2,1)S(1)}, bf16[4,256,2048]{2,1,0:T(8,128)(2,1)}, u32[]{:S(2)}) copy-start(bf16[4,256,2048]{2,1,0:T(8,128)(2,1)} %get-tuple-element.28) | copy-start | bytes 12582916
  296.1 14.3 %copy-start.16 = (bf16[1024,1024]{0,1:T(8,128)(2,1)S(1)}, bf16[1024,1024]{0,1:T(8,128)(2,1)}, u32[]{:S(2)}) copy-start(bf16[1024,1024]{0,1:T(8,128)(2,1)} %get-tuple-element.78) | copy-start | bytes 6291460
  540.9 4.9 copy-start.2
  547.3 9.5 %copy-start.6 = (f32[128,256]{0,1:T(8,128)S(1)}, f32[128,256]{0,1:T(8,128)}, u32[]{:S(2)}) copy-start(f32[128,256]{0,1:T(8,128)} %get-tuple-element.93) | copy-start | bytes 393220
  548.3 14.1 %copy-start = (f32[128,4096]{0,1:T(8,128)S(1)}, f32[128,4096]{0,1:T(8,128)}, u32[]{:S(2)}) copy-start(f32[128,4096]{0,1:T(8,128)} %get-tuple-element.83) | copy-start | bytes 6291460
  566.3 2.2 copy-start.5

commit v4 on v3

--- a/solution.py
+++ b/solution.py
@@ -451,19 +451,72 @@
         yield
 
 
-def first_kernel(
-    mid, a_waves, waves, tok, cot, table, wa, wg, wu, wd,
-    cotg, tabg, fa, fg, fu, fd, n1, qkv, probs, mixture, hidden, n2, *scratch
-):
+class Flag:
+    def __init__(self):
+        self.up = False
+
+
+def then(stream, flag):
+    yield from stream
+    flag.up = True
+
+
+def gated_steps(n2, fg, fu, cotg, act, by_gate, by_up, down, gate_up, cot_here):
+    while not (gate_up[0].all_forwarded and gate_up[1].all_forwarded):
+        yield
+    for g in gate_up:
+        g.landed()
+    width = n2.shape[2]
+    tokens, units = act.shape
+    tile, rows = 256, 512
+
+    for m in range(tokens // rows):
+
+        def body(i, carry, m=m):
+            at = pl.ds(pl.multiple_of(i * tile, tile), tile)
+            here = pl.ds(m * rows, rows)
+            each = n2.shape[1]
+            lines = n2[m * rows // each : (m + 1) * rows // each].reshape(rows, width)
+            gate = dot(lines, fg[:, at], ((1,), (0,)))
+            up = dot(lines, fu[:, at], ((1,), (0,)))
+            sigmoid = 1.0 / (1.0 + jnp.exp(-gate))
+            silu = gate * sigmoid
+            act[here, at] = (silu * up).astype(BF16)
+            by_up[here, at] = silu.astype(BF16)
+            by_gate[here, at] = (up * sigmoid * (1.0 + gate * (1.0 - sigmoid))).astype(BF16)
+            return carry
+
+        lax.fori_loop(0, units // tile, body, 0)
+        yield
+    while not cot_here.up:
+        yield
+    for part in range(2):
+
+        def body(i, carry):
+            at = pl.ds(pl.multiple_of(i * tile, tile), tile)
+            lines = cotg[:, :, at].reshape(tokens, tile)
+            down[at, :] = dot(lines, act[...], ((0,), (0,))).astype(BF16)
+            return carry
+
+        each = width // tile // 2
+        lax.fori_loop(part * each, part * each + each, body, 0)
+        yield
+
+
+def first_kernel(mid, a_waves, waves, tok, cot, table, wa, wg, wu, wd, *refs):
     p = Place(mid)
-    scratch = list(scratch)
+    refs = list(refs)
 
     def take(count):
-        taken = scratch[:count]
-        del scratch[:count]
+        taken = refs[:count]
+        del refs[:count]
         return taken
 
-    tokg, part = take(2)
+    outs = take(FIRST_OUTS)
+    fd = take(1)[0]
+    kept = take(FIRST_OUTS)
+    cotg, tabg, fa, fg, fu, n1, qkv, probs, mixture, hidden, n2, act, by_gate, by_up, down = kept
+    tokg, part, out_sems = take(3)
     tok_sems, cot_sems, tab_sems = take(3), take(3), take(3)
     reduce_refs, share_refs = take(10), take(2)
     greet(all_devices(p))
@@ -472,12 +525,31 @@
     seq = p.lo * 2 + p.c
     mine = seq * 2 + p.x
     half = hidden.shape[0]
+    cot_here = Flag()
+    leaving = []
+
+    def leave(*numbers):
+        for n in numbers:
+            copy = pltpu.make_async_copy(kept[n], outs[n], out_sems.at[n])
+            copy.start()
+            leaving.append(copy)
 
     def finish(at, total):
         there = pl.ds(pl.multiple_of(p.x * half + at.start, 16), 16)
         value = tokg[seq, there, :].astype(F32) + total
         hidden[at, :] = value
         n2[mine, at, :] = (value * norm_root(value)).astype(BF16)
+
+    def chained():
+        yield from tokens
+        yield from attention_steps(p, tokg, tabg, fa, n1, qkv, probs, mixture, part, gather_a)
+        leave(1, 2, 5, 6, 7, 8)
+        yield from reduce_steps(p, part, reduce_refs, finish)
+        leave(9)
+        yield from share_steps(p, n2, *share_refs)
+        leave(10)
+        yield from gated_steps(n2, fg, fu, cotg, act, by_gate, by_up, down, rest[:2], cot_here)
+        leave(0, 3, 4, 11, 12, 13, 14)
 
     tab = token_steps(p, table, tabg, *tab_sems, whole=True)
     tokens = token_steps(p, tok, tokg, *tok_sems, whole=False)
@@ -485,15 +557,15 @@
     next(tab)
     drive(
         gather_steps(gather_a, *rest),
-        chain(
-            tokens,
-            attention_steps(p, tokg, tabg, fa, n1, qkv, probs, mixture, part, gather_a),
-            reduce_steps(p, part, reduce_refs, finish),
-            share_steps(p, n2, *share_refs),
-        ),
+        chained(),
         tab,
-        after(COT_AT, token_steps(p, cot, cotg, *cot_sems, whole=False)),
+        after(COT_AT, then(token_steps(p, cot, cotg, *cot_sems, whole=False), cot_here)),
     )
+    for copy in leaving:
+        copy.wait()
+
+
+FIRST_OUTS = 15
 
 
 def first(mid, tok, cot, table, wa, wg, wu, wd, qw):
@@ -501,28 +573,34 @@
     length, width = tok.shape
     n = 8 * mid
     heads = qw // HEAD_DIM
+    tokens, units = 4 * length, wg.shape[2]
 
     def full(w):
-        return jax.ShapeDtypeStruct((n * w.shape[1], w.shape[2]), BF16)
-
+        return ((n * w.shape[1], w.shape[2]), BF16)
+
+    outs = [
+        ((4,) + cot.shape, BF16),
+        ((4,) + table.shape, F32),
+        full(wa), full(wg), full(wu),
+        ((tokens, width), BF16),
+        ((tokens, qw + 128), BF16),
+        ((4, heads, length, length), F32),
+        ((tokens, qw), BF16),
+        ((length // 2, width), F32),
+        ((8, length // 2, width), BF16),
+        ((tokens, units), BF16), ((tokens, units), BF16), ((tokens, units), BF16),
+        ((width, units), BF16),
+    ]
     return pl.pallas_call(
         functools.partial(first_kernel, mid, a_waves, waves),
-        out_shape=(
-            jax.ShapeDtypeStruct((4,) + cot.shape, BF16),
-            jax.ShapeDtypeStruct((4,) + table.shape, F32),
-            full(wa), full(wg), full(wu), full(wd),
-            jax.ShapeDtypeStruct((4 * length, width), BF16),
-            jax.ShapeDtypeStruct((4 * length, qw + 128), BF16),
-            jax.ShapeDtypeStruct((4, heads, length, length), F32),
-            jax.ShapeDtypeStruct((4 * length, qw), BF16),
-            jax.ShapeDtypeStruct((length // 2, width), F32),
-            jax.ShapeDtypeStruct((8, length // 2, width), BF16),
-        ),
+        out_shape=[jax.ShapeDtypeStruct(*out) for out in outs + [full(wd)]],
         in_specs=[ANY] * 7,
-        out_specs=(ANY, VMEM, VMEM, ANY, ANY, ANY) + (VMEM,) * 6,
-        scratch_shapes=[
+        out_specs=[ANY] * (FIRST_OUTS + 1),
+        scratch_shapes=[pltpu.VMEM(*out) for out in outs]
+        + [
             pltpu.VMEM((4, length, width), BF16),
             pltpu.VMEM((8, length // 2, width), BF16),
+            DMA((FIRST_OUTS,)),
         ]
         + token_sems() * 3
         + reduce_scratch(length // 2, width)
@@ -836,6 +914,93 @@
     )(part_two, out_part, n1, probs, hid, cot, x, qkv, mixture, fa, tabg, gu, down)
 
 
+def settle_kernel(
+    gu, down, own, gains, low, w_gate, w_up, w_query, w_key, w_value,
+    gate_o, up_o, down_o, query_o, key_o, value_o, out_o, gain_o, wide_o
+):
+    u = pl.program_id(0)
+    units, qw = gate_o.shape[1], query_o.shape[1]
+    kw = key_o.shape[1] // 4
+    gain_one, gain_two = gains[:, 0:1], gains[:, 1:2]
+    wide_o[...] = low[...].astype(F32)
+
+    def total(ref, first, width):
+        at = slice(first, first + width)
+        return ref[0, 0, :, at].astype(F32) + ref[1, 0, :, at].astype(F32)
+
+    def weigh(w, grad):
+        return jnp.sum(w.astype(F32) * grad, axis=1, keepdims=True)
+
+    gate, up = total(gu, 0, units), total(gu, units, units)
+    gate_o[...] = gate * gain_two
+    up_o[...] = up * gain_two
+    two = weigh(w_gate[...], gate) + weigh(w_up[...], up)
+    down_o[...] = total(down, 0, units).T
+    query = total(own, 0, qw)
+    query_o[...] = query * gain_one
+    out_o[...] = total(own, qw + 2 * kw, out_o.shape[0]).T
+    both = total(own, qw, 2 * kw)
+    one = weigh(w_query[...], query)
+
+    @pl.when(u == 0)
+    def _():
+        gain_o[...] = jnp.zeros_like(gain_o)
+
+    lanes = lanes_of(gain_o.shape)
+    for i in range(4):
+
+        @pl.when(u == i)
+        def _(i=i):
+            at = slice(i * kw, i * kw + kw)
+            key_o[:, at] = both[:, :kw] * gain_one
+            value_o[:, at] = both[:, kw:] * gain_one
+            more = weigh(w_key[:, at], both[:, :kw]) + weigh(w_value[:, at], both[:, kw:])
+            gain_o[...] += jnp.where(lanes == 0, one + more, jnp.where(lanes == 1, two, 0.0))
+
+
+def settle(gu, down, own, gains, low, w_gate, w_up, w_query, w_key, w_value):
+    rows = gu.shape[1]
+    length, width = low.shape
+    units, qw, kw = w_gate.shape[1] // 4, w_query.shape[1] // 4, w_key.shape[1] // 4
+
+    def parts(ref):
+        return ref.reshape(2, 4, rows, ref.shape[2])
+
+    def part_spec(ref):
+        return pl.BlockSpec((2, 1, rows, ref.shape[2]), lambda u: (0, u, 0, 0))
+
+    def column(w):
+        return pl.BlockSpec((rows, w), lambda u: (0, u))
+
+    def row(w):
+        return pl.BlockSpec((w, rows), lambda u: (u, 0))
+
+    def whole(*shape):
+        return pl.BlockSpec(shape, lambda u: (0, 0))
+
+    def out(*shape):
+        return jax.ShapeDtypeStruct(shape, F32)
+
+    lines = pl.BlockSpec((length // 4, width), lambda u: (u, 0))
+    return pl.pallas_call(
+        settle_kernel,
+        grid=(4,),
+        out_shape=(
+            out(rows, 4 * units), out(rows, 4 * units), out(4 * units, rows), out(rows, 4 * qw), out(rows, 4 * kw),
+            out(rows, 4 * kw), out(4 * qw, rows), out(rows, 128), out(length, width),
+        ),
+        in_specs=[
+            part_spec(gu), part_spec(down), part_spec(own), whole(rows, 2), lines,
+            column(units), column(units), column(qw), whole(rows, 4 * kw), whole(rows, 4 * kw),
+        ],
+        out_specs=(
+            column(units), column(units), row(units), column(qw), whole(rows, 4 * kw), whole(rows, 4 * kw), row(qw),
+            whole(rows, 128), lines,
+        ),
+        compiler_params=pltpu.CompilerParams(vmem_limit_bytes=48 << 20),
+    )(parts(gu), parts(down), parts(own), gains, low, w_gate, w_up, w_query, w_key, w_value)
+
+
 def token_table(segments):
     length = segments.shape[0]
     places = jnp.arange(length, dtype=jnp.int32)
@@ -873,28 +1038,20 @@
     wa = jnp.concatenate(
         [scaled(w_query, gain_one), scaled(w_key, gain_one), scaled(w_value, gain_one), blocks(w_out.T)], axis=-1
     )
-    units = w_gate.shape[1] // 4
-    qw, kw = w_query.shape[1] // 4, w_key.shape[1] // 4
-    heads = qw // HEAD_DIM
-    cotg, tabg, fa, gate_w, up_w, down_t, normed, qkv, probs, mixture, hidden, n2 = first(
-        mid, tokens, cotangent, token_table(segment_ids), wa, wg, wu, wd, qw
-    )
+    qw = w_query.shape[1] // 4
+    (
+        cotg, tabg, fa, gate_w, up_w, normed, qkv, probs, mixture, hidden, n2, activated, by_gate, by_up, down_g, down_t
+    ) = first(mid, tokens, cotangent, token_table(segment_ids), wa, wg, wu, wd, qw)
     own_x = lax.dynamic_slice_in_dim(tokens, x_at * half, half, 0)
     own_cot = lax.dynamic_slice_in_dim(cotangent, x_at * half, half, 0)
     n2 = n2.reshape(4 * length, width)
 
-    gate = dot(n2, gate_w, ((1,), (0,)))
-    up = dot(n2, up_w, ((1,), (0,)))
-    sigmoid = 1.0 / (1.0 + jnp.exp(-gate))
-    silu = gate / (1.0 + jnp.exp(-gate))
-    activated = (silu * up).astype(BF16)
     out_part = dot(activated, down_t, ((1,), (1,))).astype(BF16)
     cots = cotg.reshape(4 * length, width)
     grad_act = dot(cots, down_t, ((1,), (0,)))
-    grad_gate = (grad_act * up * sigmoid * (1.0 + gate * (1.0 - sigmoid))).astype(BF16)
-    grad_up = (grad_act * silu).astype(BF16)
+    grad_gate = (grad_act * by_gate.astype(F32)).astype(BF16)
+    grad_up = (grad_act * by_up.astype(F32)).astype(BF16)
     part_two = (dot(grad_gate, gate_w, ((1,), (1,))) + dot(grad_up, up_w, ((1,), (1,)))).astype(BF16)
-    down_g = dot(cots, activated, ((0,), (0,))).astype(BF16)
     gu_g = dot(n2, jnp.concatenate([grad_gate, grad_up], axis=1), ((0,), (0,))).astype(BF16)
 
     eight = (8, half, width)
@@ -903,39 +1060,13 @@
         qkv, mixture, fa, tabg, gu_g, down_g
     )
 
-    def total(parts):
-        parts = parts.reshape(2, 4, rows, -1).astype(F32)
-        return parts[0] + parts[1]
-
-    def across(block):
-        return block.transpose(1, 0, 2).reshape(rows, -1)
-
-    def down(block):
-        return block.transpose(0, 2, 1).reshape(-1, rows)
-
-    t_gate, t_up = jnp.split(total(gu_parts), 2, axis=-1)
-    t_q, t_k, t_v, t_out = jnp.split(total(a_parts), [qw, qw + kw, qw + 2 * kw], axis=-1)
-    t_gate, t_up, t_q, t_k, t_v = (across(t) for t in (t_gate, t_up, t_q, t_k, t_v))
-
-    def gain_grad(*pairs):
-        return sum(jnp.sum(w.astype(F32) * g, axis=1) for w, g in pairs)
-
-    gain_grads = jnp.stack(
-        [gain_grad((w_query, t_q), (w_key, t_k), (w_value, t_v)), gain_grad((w_gate, t_gate), (w_up, t_up))]
+    gains = jnp.stack([attn_gain, mlp_gain], axis=1).astype(F32)
+    gate_g, up_g, down_g, query_g, key_g, value_g, out_g, gain_sums, input_grad = settle(
+        gu_parts, down_parts, a_parts, gains, input_grad, w_gate, w_up, w_query, w_key, w_value
     )
-    gain_grads = lax.psum(gain_grads, "tensor")
+    gain_g = lax.psum(gain_sums[:, :2], "tensor")
     return (
-        output,
-        input_grad.astype(F32),
-        gain_grads[0],
-        t_q * gain_one,
-        t_k * gain_one,
-        t_v * gain_one,
-        down(t_out),
-        gain_grads[1],
-        t_gate * gain_two,
-        t_up * gain_two,
-        down(total(down_parts)),
+        output, input_grad, gain_g[:, 0], query_g, key_g, value_g, out_g, gain_g[:, 1], gate_g, up_g, down_g
     )
 
 

time: 580 us -> 536 us (0.924)
  matrix products: 71.1 us -> 45.2 us
  local copies, waits for them, and re-layouts: 38.1 us -> 22.2 us
  other arithmetic: 21.7 us -> 7.62 us
  Pallas kernels: 433 us -> 443 us
    dot_general x8 -> x5, matrix products: 71.1 us -> 45.2 us  [dot(): return lax.dot_general(a, b, (dims, ((), ())), preferred_element_type=F32)]
    transpose x10 -> x0, local copies, waits for them, and re-layouts: 13.3 us -> none  [the longest x7 8.61 us: across(): return block.transpose(1, 0, 2).reshape(rows, -1)]
    convert_element_type x4 -> x1, other arithmetic: 8.26 us -> 0.01 us  [local(): gains = jnp.stack([attn_gain, mlp_gain], axis=1).astype(F32)]
    pallas_call x0 -> x1, Pallas kernels: none -> 7.95 us  [settle(): pl.pallas_call(settle_kernel, grid=(4,), out_shape=(out(rows, 4 * units),...]
    unnamed x45 -> x38, local copies, waits for them, and re-layouts: 13.5 us -> 10.5 us
where the time goes in v4:
time: 536 us; the launch traced here: 526 us
  Pallas kernels  443 us (83%)
  matrix products  45.2 us (8%)
  local copies, waits for them, and re-layouts  22.2 us (4%)
  other arithmetic  7.62 us (1%)
  blocking collectives  7.34 us (1%)
    pallas_call x1, Pallas kernels, first(): pl.pallas_call(functools.partial(first_kernel, mid, a_waves, waves), out_...  226 us
    pallas_call x1, Pallas kernels, last(): pl.pallas_call(functools.partial(last_kernel, mid, a_waves, d_waves, g_wa...  208 us
    dot_general x5, matrix products, dot(): return lax.dot_general(a, b, (dims, ((), ())), preferred_element_type=F32)  45.2 us

profile of v4, /device:TPU:0, one launch (start us, length us, event | category | flops | bytes accessed | tf_op | source)
XLA Modules:
  0.0 526.3 jit_solution(3890192561014943600)
XLA Ops:
  0.6 0.0 copy-start
  0.7 0.0 copy-start.9
  0.7 1.3 slice.15
  2.0 1.5 compare_select_fusion
  3.5 0.1 select_reduce_fusion
  3.6 0.1 broadcast_in_dim.32
  3.7 0.5 multiply_cosine_fusion
  4.3 0.8 pad_maximum_fusion.1.table
  5.1 1.1 copy.80
  6.2 1.0 copy.76
  7.1 0.7 convert_element_type.77
  7.8 0.9 copy.78
  8.8 0.1 copy.79
  8.9 0.1 copy.77
  9.0 1.1 copy.74
  10.2 0.1 multiply_convert_fusion.4
  10.2 0.1 copy.75
  10.4 1.0 pad_maximum_fusion.wa
  11.4 1.3 copy.83
  12.7 0.0 copy-done.9
  12.7 1.3 copy.81
  14.0 2.9 multiply_convert_fusion.2
  16.9 2.3 copy.82
  19.2 1.3 copy.84
  20.5 2.3 copy.85
  22.8 226.3 %shard_map.203 = (bf16[4,256,2048]{2,1,0:T(8,128)(2,1)}, f32[4,256,128]{2,1,0:T(8,128)}, bf16[2048,640]{1,0:T(8,128)(2,1)}, bf16[2048,1024]{1,0:T(8,128)(2,1)}, ...) custom-call(bf16[256,2048]{1,0:T(8,128)(2,1)} %tok.1, ...), custom_call_target="tpu_custom_call" | custom-call | tf_op jit(solution)/shard_map/pallas_call | solution.py:594
  249.1 9.4 %multiply_convert_fusion = (bf16[1024,1024]{1,0:T(8,128)(2,1)S(1)}, bf16[1024,1024]{1,0:T(8,128)(2,1)S(1)}) fusion(bf16[1024,1024]{1,0:T(8,128)(2,1)} %get-tuple-element.45, bf16[1024,1024]{1,0:T(8,128)(2,1)} %get-tuple-element.43, bf16[1024,2048]{1,0:T(8,128)(2,1)} %bitcast.64, bf16[2048,1024]{1,0:T(8,128)(2,1)} %get-tuple-element.42), kind=kOutput, calls=%fused_computation.5 | convolution fusion | flops 4301258752 | bytes 16777216 | tf_op jit(solution)/shard_map/dot_general | solution.py:1018
  258.5 0.0 copy-start.15
  258.5 0.0 copy-start.14
  258.6 6.9 %fusion.4 = f32[1024,2048]{1,0:T(8,128)} fusion(bf16[1024,1024]{1,0:T(8,128)(2,1)S(1)} %get-tuple-element.74, bf16[2048,1024]{1,0:T(8,128)(2,1)S(1)} %copy-done.12), kind=kOutput, calls=%fused_computation.28 | convolution fusion | flops 4294967296 | bytes 14680064 | tf_op jit(solution)/shard_map/dot_general | solution.py:1018
  265.5 0.0 copy-done.11
  265.5 0.0 copy-start.10
  265.5 0.0 copy-start.13
  265.5 8.7 %add_convert_fusion = bf16[1024,2048]{1,0:T(8,128)(2,1)} fusion(f32[1024,2048]{1,0:T(8,128)} %fusion.4, bf16[1024,1024]{1,0:T(8,128)(2,1)S(1)} %get-tuple-element.73, bf16[2048,1024]{1,0:T(8,128)(2,1)S(1)} %copy-done.11), kind=kOutput, calls=%fused_computation | convolution fusion | flops 4299161600 | bytes 18874368 | tf_op jit(solution)/shard_map/dot_general | solution.py:1018
  274.2 0.0 copy-start.7
  274.2 6.2 %convolution_convert_fusion.1 = bf16[1024,2048]{1,0:T(8,128)(2,1)} fusion(bf16[1024,1024]{1,0:T(8,128)(2,1)S(1)} %copy-done.13, bf16[2048,1024]{1,0:T(8,128)(2,1)S(1)} %copy-done.10), kind=kOutput, calls=%fused_computation.7 | convolution fusion | flops 4297064448 | bytes 10485760 | tf_op jit(solution)/shard_map/dot_general | solution.py:1018
  280.4 2.1 constant_dynamic-slice_fusion
  282.5 14.0 %convolution_convert_fusion.gu = bf16[2048,2048]{1,0:T(8,128)(2,1)} fusion(bf16[1024,2048]{1,0:T(8,128)(2,1)} %bitcast.63, bf16[1024,1024]{1,0:T(8,128)(2,1)} %copy-done.14, bf16[1024,1024]{1,0:T(8,128)(2,1)} %copy-done.15), kind=kOutput, calls=%fused_computation.1 | convolution fusion | flops 8602517504 | bytes 16777216 | tf_op jit(solution)/shard_map/dot_general | solution.py:1018
  296.5 0.0 copy-start.6
  296.5 208.3 %shard_map.204 = (bf16[256,2048]{1,0:T(8,128)(2,1)}, bf16[256,2048]{1,0:T(8,128)(2,1)}, bf16[8,128,2048]{2,1,0:T(8,128)(2,1)}, bf16[8,128,1024]{2,1,0:T(8,128)(2,1)}, bf16[8,128,640]{2,1,0:T(8,128)(2,1)}) custom-call(bf16[8,128,2048]{2,1,0:T(8,128)(2,1)} %bitcast.42, bf16[8,128,2048]{2,1,0:T(8,128)(2,1)} %bitcast.43, bf16[8,128,2048]{2,1,0:T(8,128)(2,1)} %bitcast.41, ...), custom_call_target="tpu_custom_call" | custom-call | tf_op jit(solution)/shard_map/pallas_call | solution.py:884
  504.8 0.0 copy-done.8
  504.8 0.1 copy.88.gains
  505.0 1.3 copy-done.2
  506.3 1.2 copy-done.4
  507.5 8.0 %shard_map.205 = (f32[128,4096]{1,0:T(8,128)}, f32[128,4096]{1,0:T(8,128)}, f32[4096,128]{1,0:T(8,128)}, f32[128,1024]{1,0:T(8,128)}, f32[128,256]{1,0:T(8,128)}...) custom-call(bf16[2,4,128,2048]{3,2,1,0:T(8,128)(2,1)} %bitcast.46, ...), custom_call_target="tpu_custom_call" | custom-call | tf_op jit(solution)/shard_map/pallas_call | solution.py:985
  515.5 7.3 %psum.7 = f32[128,2]{1,0:T(8,128)S(1)} all-reduce(f32[128,2]{1,0:T(8,128)S(1)} %bitcast.40), channel_id=1, replica_groups=mesh['dp'=16,'tensor'=2] {'tensor'}, use_global_device_ids=true, to_apply=%region_1.2 | all-reduce | flops 256 | bytes 2048 | tf_op jit(solution)/shard_map/psum | solution.py:1067
  522.8 0.7 slice_reduce_fusion
  523.5 2.3 copy.91
  (24 shorter events, 0.1 us)
Async XLA Ops:
  0.6 10.8 %copy-start = (bf16[128,4096]{1,0:T(8,128)(2,1)S(1)}, bf16[128,4096]{1,0:T(8,128)(2,1)}, u32[]{:S(2)}) copy-start(bf16[128,4096]{1,0:T(8,128)(2,1)} %w_up.1) | copy-start | bytes 3145732
  0.7 12.0 %copy-start.9 = (bf16[128]{0:T(256)(128)(2,1)S(1)}, bf16[128]{0:T(256)(128)(2,1)}, u32[]{:S(2)}) copy-start(bf16[128]{0:T(256)(128)(2,1)} %param.18) | copy-start | bytes 772
  0.7 12.0 %copy-start.1 = (bf16[128,4096]{1,0:T(8,128)(2,1)S(1)}, bf16[128,4096]{1,0:T(8,128)(2,1)}, u32[]{:S(2)}) copy-start(bf16[128,4096]{1,0:T(8,128)(2,1)} %w_gate.1) | copy-start | bytes 3145732
  249.1 9.5 %copy-start.12 = (bf16[2048,1024]{1,0:T(8,128)(2,1)S(1)}, bf16[2048,1024]{1,0:T(8,128)(2,1)}, u32[]{:S(2)}) copy-start(bf16[2048,1024]{1,0:T(8,128)(2,1)} %get-tuple-element.44) | copy-start | bytes 12582916
  258.5 6.9 %copy-start.15 = (bf16[1024,1024]{1,0:T(8,128)(2,1)}, bf16[1024,1024]{1,0:T(8,128)(2,1)S(1)}, u32[]{:S(2)}) copy-start(bf16[1024,1024]{1,0:T(8,128)(2,1)S(1)} %get-tuple-element.74) | copy-start | bytes 6291460
  258.5 6.9 %copy-start.14 = (bf16[1024,1024]{1,0:T(8,128)(2,1)}, bf16[1024,1024]{1,0:T(8,128)(2,1)S(1)}, u32[]{:S(2)}) copy-start(bf16[1024,1024]{1,0:T(8,128)(2,1)S(1)} %get-tuple-element.73) | copy-start | bytes 6291460
  258.6 6.9 %copy-start.11 = (bf16[2048,1024]{1,0:T(8,128)(2,1)S(1)}, bf16[2048,1024]{1,0:T(8,128)(2,1)}, u32[]{:S(2)}) copy-start(bf16[2048,1024]{1,0:T(8,128)(2,1)} %get-tuple-element.46) | copy-start | bytes 12582916
  265.5 8.7 %copy-start.10 = (bf16[2048,1024]{1,0:T(8,128)(2,1)S(1)}, bf16[2048,1024]{1,0:T(8,128)(2,1)}, u32[]{:S(2)}) copy-start(bf16[2048,1024]{1,0:T(8,128)(2,1)} %get-tuple-element.42) | copy-start | bytes 12582916
  265.5 8.7 %copy-start.13 = (bf16[1024,1024]{1,0:T(8,128)(2,1)S(1)}, bf16[1024,1024]{1,0:T(8,128)(2,1)}, u32[]{:S(2)}) copy-start(bf16[1024,1024]{1,0:T(8,128)(2,1)} %get-tuple-element.47) | copy-start | bytes 6291460
  274.2 6.2 %copy-start.7 = (bf16[256,2048]{1,0:T(8,128)(2,1)S(1)}, bf16[256,2048]{1,0:T(8,128)(2,1)}, u32[]{:S(2)}) copy-start(bf16[256,2048]{1,0:T(8,128)(2,1)} %tok.1) | copy-start | bytes 3145732
  296.5 208.3 %copy-start.8 = (bf16[128]{0:T(256)(128)(2,1)S(1)}, bf16[128]{0:T(256)(128)(2,1)}, u32[]{:S(2)}) copy-start(bf16[128]{0:T(256)(128)(2,1)} %param.13) | copy-start | bytes 772
  296.5 208.4 %copy-start.3 = (bf16[128,1024]{1,0:T(8,128)(2,1)S(1)}, bf16[128,1024]{1,0:T(8,128)(2,1)}, u32[]{:S(2)}) copy-start(bf16[128,1024]{1,0:T(8,128)(2,1)} %w_query.1) | copy-start | bytes 786436
  296.5 208.4 %copy-start.5 = (bf16[128,256]{1,0:T(8,128)(2,1)S(1)}, bf16[128,256]{1,0:T(8,128)(2,1)}, u32[]{:S(2)}) copy-start(bf16[128,256]{1,0:T(8,128)(2,1)} %w_key.1) | copy-start | bytes 196612
  296.5 208.4 %copy-start.6 = (bf16[128,256]{1,0:T(8,128)(2,1)S(1)}, bf16[128,256]{1,0:T(8,128)(2,1)}, u32[]{:S(2)}) copy-start(bf16[128,256]{1,0:T(8,128)(2,1)} %w_value.1) | copy-start | bytes 196612
  505.0 1.3 copy-start.2
  506.3 1.2 copy-start.4

commit v5 on v4

--- a/solution.py
+++ b/solution.py
@@ -17,7 +17,7 @@
 BF16 = jnp.bfloat16
 DMA = pltpu.SemaphoreType.DMA
 COT_AT = 7
-OUT_AT = 4
+OUT_AT = 1
 
 
 class Place:
@@ -608,7 +608,7 @@
         + gather_sems(mid, a_waves)
         + gather_sems(mid, waves) * 3,
         compiler_params=pltpu.CompilerParams(
-            collective_id=0, has_side_effects=True, vmem_limit_bytes=60 << 20
+            collective_id=0, has_side_effects=True, vmem_limit_bytes=62 << 20
         ),
     )(tok, cot, table, wa, wg, wu, wd)
 
@@ -746,14 +746,12 @@
     heads = qw // HEAD_DIM
     scaling = HEAD_DIM ** (-0.5)
 
-    def fetch(s):
-        return pltpu.make_async_copy(probs.at[s], p_buf.at[s % 2], p_sem.at[s % 2])
-
-    fetch(0).start()
+    def fetch(n):
+        return pltpu.make_async_copy(probs.at[n // heads, n % heads], p_buf.at[n % 4], p_sem.at[n % 4])
+
+    for n in range(3):
+        fetch(n).start()
     for s in range(4):
-        if s < 3:
-            fetch(s + 1).start()
-        fetch(s).wait()
         here = pl.ds(s * length, length)
         cosine, signed = wide_tables(tabg[s])
         grads = low[2 * s : 2 * s + 2].reshape(length, low.shape[2])
@@ -765,7 +763,11 @@
         grad_query = []
         for h in range(heads):
             at = slice(HEAD_DIM * h, HEAD_DIM * h + HEAD_DIM)
-            share = p_buf[s % 2, h]
+            number = s * heads + h
+            if number + 3 < 4 * heads:
+                fetch(number + 3).start()
+            fetch(number).wait()
+            share = p_buf[number % 4]
             gm = grad_mix[:, at]
             gp = dot(gm, value, ((1,), (1,)))
             grad_value = grad_value + dot(share.astype(BF16), gm, ((0,), (0,)))
@@ -782,7 +784,8 @@
         for x in range(2):
             rows = pl.ds(s * length + x * half, half)
             part[s * 2 + x] = dot(gqkv[rows, :], fa[:, : qw + 128], ((1,), (1,))).astype(BF16)
-        yield
+        if s % 2:
+            yield
 
 
 def weight_grad_steps(low, mixture, n1, n1_copy, gqkv, ga, a_scatter):
@@ -805,8 +808,8 @@
 
 
 def last_kernel(
-    mid, a_waves, d_waves, g_waves, part_two, out_part, n1, probs, hid, cot, x, qkv, mixture, fa, tabg, gu, down,
-    output, result, gu_out, down_out, ga_out, *scratch
+    mid, a_waves, d_waves, g_waves, both, act, n2, n1, probs, hid, cot, x, qkv, mixture, fa, tabg, fg, fu, fd, down,
+    output, result, gu_out, down_out, ga_out, gu, *scratch
 ):
     p = Place(mid)
     scratch = list(scratch)
@@ -817,12 +820,13 @@
         return taken
 
     first_buf, second_buf, grad_hidden, low, gqkv, ga, p_buf, p_sem, in_sems = take(9)
-    r1, r2, r3 = take(10), take(10), take(10)
+    act_buf, w_buf, n_buf, g_buf, w_sem, n_sem, g_sem, low_free = take(8)
+    r1, r2 = take(10), take(10)
     g_sems, o_sems, i_sems = take(2), take(2), take(2)
     gu_s, down_s, ga_s = take(8), take(8), take(8)
     loads = [
-        pltpu.make_async_copy(part_two, first_buf, in_sems.at[0]),
-        pltpu.make_async_copy(out_part, second_buf, in_sems.at[1]),
+        pltpu.make_async_copy(both, low, in_sems.at[0]),
+        pltpu.make_async_copy(act, act_buf, in_sems.at[1]),
         pltpu.make_async_copy(n1, second_buf, in_sems.at[2]),
     ]
     loads[0].start()
@@ -848,26 +852,113 @@
     scatter_d = Scatter(p, down, down_s[0], down_s[1], down_out, down_s[2:], d_waves)
     scatter_g = Scatter(p, gu, gu_s[0], gu_s[1], gu_out, gu_s[2:], g_waves)
     scatter_a = Scatter(p, ga, ga_s[0], ga_s[1], ga_out, ga_s[2:], a_waves)
-    scatter_a.ready = False
+    scatter_a.ready = scatter_g.ready = False
 
     def outputs():
-        loads[1].wait()
+        while not scatter_g.ready:
+            yield
         yield from reduce_steps(p, second_buf, r2, finish_out)
         loads[2].start()
         yield from swap_steps(p, output, *o_sems)
 
     out = outputs()
+    width = low.shape[2]
+    tokens, units = act_buf.shape
+    tile = w_buf.shape[2]
+    tiles = width // tile
+
+    def lines(i):
+        return pl.ds(pl.multiple_of(i * tile, tile), tile)
+
+    def weight(i, number, ref):
+        slot = lax.rem(i, 2)
+        return pltpu.make_async_copy(ref.at[lines(i)], w_buf.at[slot, number], w_sem.at[slot, number])
+
+    def rows_in(i):
+        slot = lax.rem(i, 2)
+        return pltpu.make_async_copy(n2.at[:, :, lines(i)], n_buf.at[slot], n_sem.at[slot])
+
+    def grad_out(i):
+        slot = lax.rem(i, 2)
+        return pltpu.make_async_copy(g_buf.at[slot], gu.at[lines(i)], g_sem.at[slot])
+
+    def norm_part():
+        def step(i, carry):
+            weight(i, 0, fg).wait()
+            weight(i, 1, fu).wait()
+
+            @pl.when(i + 1 < tiles)
+            def _():
+                weight(i + 1, 0, fg).start()
+                weight(i + 1, 1, fu).start()
+
+            slot = lax.rem(i, 2)
+            gate = low[:, :, :units].reshape(tokens, units)
+            up = low[:, :, units:].reshape(tokens, units)
+            value = dot(gate, w_buf[slot, 0], ((1,), (1,))) + dot(up, w_buf[slot, 1], ((1,), (1,)))
+            first_buf[:, :, lines(i)] = value.astype(BF16).reshape(8, tokens // 8, tile)
+            return carry
+
+        weight(0, 0, fg).start()
+        weight(0, 1, fu).start()
+        loads[0].wait()
+        lax.fori_loop(0, tiles, step, 0)
+
+    def weight_part():
+        def step(i, carry):
+            weight(i, 0, fd).wait()
+            rows_in(i).wait()
+
+            @pl.when(i + 1 < tiles)
+            def _():
+                weight(i + 1, 0, fd).start()
+                rows_in(i + 1).start()
+
+            slot = lax.rem(i, 2)
+            value = dot(act_buf[...], w_buf[slot, 0], ((1,), (1,)))
+            second_buf[:, :, lines(i)] = value.astype(BF16).reshape(8, tokens // 8, tile)
+
+            @pl.when(i >= 2)
+            def _():
+                grad_out(i - 2).wait()
+
+            grads = low[...].reshape(tokens, 2 * units)
+            g_buf[slot] = dot(n_buf[slot].reshape(tokens, tile), grads, ((0,), (0,))).astype(BF16)
+            grad_out(i).start()
+            return carry
+
+        weight(0, 0, fd).start()
+        rows_in(0).start()
+        loads[1].wait()
+        lax.fori_loop(0, tiles // 2, step, 0)
+        yield
+        lax.fori_loop(tiles // 2, tiles, step, 0)
+        grad_out(tiles - 2).wait()
+        grad_out(tiles - 1).wait()
+        scatter_g.ready = True
 
     def chained():
-        loads[0].wait()
-        yield from reduce_steps(p, first_buf, r1, finish)
+        norm_part()
+        summed = reduce_steps(p, first_buf, r1, finish)
+        next(summed)
+        yield
+        next(summed)
+        yield from weight_part()
+        for device in (
+            (p.dp(p.z, p.m, 1 - p.c), p.x),
+            (p.d, 1 - p.x),
+            (p.dp(xor(p.z, 1), p.m, p.c), p.x),
+        ):
+            pl.semaphore_signal(low_free, inc=1, device_id=device, device_id_type=MESH)
+        yield from summed
+        pl.semaphore_wait(low_free, 3)
         yield from share_steps(p, low, *g_sems)
         yield from attention_back_steps(
             p, low, qkv, probs, p_buf, p_sem, mixture, fa, tabg, second_buf, loads[2], gqkv, first_buf, ga, scatter_a
         )
         for _ in out:
             pass
-        last = reduce_steps(p, first_buf, r3, finish_in)
+        last = reduce_steps(p, first_buf, r1, finish_in)
         next(last)
         yield from weight_grad_steps(low, mixture, second_buf, loads[2], gqkv, ga, scatter_a)
         yield from last
@@ -876,22 +967,25 @@
     drive(scatter_steps(scatter_d, scatter_g, scatter_a), chained(), after(OUT_AT, out))
 
 
-def last(mid, part_two, out_part, n1, probs, hid, cot, x, qkv, mixture, fa, tabg, gu, down):
-    eight, rows, width = part_two.shape
+def last(mid, both, act, n2, n1, probs, hid, cot, x, qkv, mixture, fa, tabg, fg, fu, fd, down):
+    eight, rows, width = n2.shape
     n = 8 * mid
-    w_rows = gu.shape[0] // n
+    units = act.shape[1]
+    w_rows = width // n
+    tile = 256
     a_waves, d_waves, g_waves = waves_of(w_rows, 4), waves_of(w_rows, 4), waves_of(w_rows, 8)
     return pl.pallas_call(
         functools.partial(last_kernel, mid, a_waves, d_waves, g_waves),
         out_shape=(
             jax.ShapeDtypeStruct((2 * rows, width), BF16),
             jax.ShapeDtypeStruct((2 * rows, width), BF16),
-            jax.ShapeDtypeStruct((8, w_rows, gu.shape[1]), BF16),
+            jax.ShapeDtypeStruct((8, w_rows, 2 * units), BF16),
             jax.ShapeDtypeStruct((8, w_rows, down.shape[1]), BF16),
             jax.ShapeDtypeStruct((8, w_rows, fa.shape[1]), BF16),
+            jax.ShapeDtypeStruct((width, 2 * units), BF16),
         ),
-        in_specs=[ANY] * 4 + [VMEM] * 7 + [ANY] * 2,
-        out_specs=(VMEM,) * 2 + (ANY,) * 3,
+        in_specs=[ANY] * 5 + [VMEM] * 7 + [ANY] * 4,
+        out_specs=(VMEM,) * 2 + (ANY,) * 4,
         scratch_shapes=[
             pltpu.VMEM((eight, rows, width), BF16),
             pltpu.VMEM((eight, rows, width), BF16),
@@ -899,19 +993,24 @@
             pltpu.VMEM((eight, rows, width), BF16),
             pltpu.VMEM(qkv.shape, BF16),
             pltpu.VMEM(fa.shape, BF16),
-            pltpu.VMEM((2,) + probs.shape[1:], F32),
-            DMA((2,)),
+            pltpu.VMEM((4,) + probs.shape[2:], F32),
+            DMA((4,)),
             DMA((3,)),
+            pltpu.VMEM(act.shape, BF16),
+            pltpu.VMEM((2, 2, tile, units), BF16),
+            pltpu.VMEM((2, eight, rows, tile), BF16),
+            pltpu.VMEM((2, tile, 2 * units), BF16),
+            DMA((2, 2)), DMA((2,)), DMA((2,)), pltpu.SemaphoreType.REGULAR,
         ]
-        + reduce_scratch(rows, width) * 3
+        + reduce_scratch(rows, width) * 2
         + [DMA((7,)), DMA((7,)), DMA, DMA, DMA, DMA]
-        + scatter_scratch(mid, w_rows, gu.shape[1], g_waves)
+        + scatter_scratch(mid, w_rows, 2 * units, g_waves)
         + scatter_scratch(mid, w_rows, down.shape[1], d_waves)
         + scatter_scratch(mid, w_rows, fa.shape[1], a_waves),
         compiler_params=pltpu.CompilerParams(
-            collective_id=1, has_side_effects=True, vmem_limit_bytes=60 << 20
+            collective_id=1, has_side_effects=True, vmem_limit_bytes=62 << 20
         ),
-    )(part_two, out_part, n1, probs, hid, cot, x, qkv, mixture, fa, tabg, gu, down)
+    )(both, act, n2, n1, probs, hid, cot, x, qkv, mixture, fa, tabg, fg, fu, fd, down)[:5]
 
 
 def settle_kernel(
@@ -1044,20 +1143,15 @@
     ) = first(mid, tokens, cotangent, token_table(segment_ids), wa, wg, wu, wd, qw)
     own_x = lax.dynamic_slice_in_dim(tokens, x_at * half, half, 0)
     own_cot = lax.dynamic_slice_in_dim(cotangent, x_at * half, half, 0)
-    n2 = n2.reshape(4 * length, width)
-
-    out_part = dot(activated, down_t, ((1,), (1,))).astype(BF16)
     cots = cotg.reshape(4 * length, width)
     grad_act = dot(cots, down_t, ((1,), (0,)))
-    grad_gate = (grad_act * by_gate.astype(F32)).astype(BF16)
-    grad_up = (grad_act * by_up.astype(F32)).astype(BF16)
-    part_two = (dot(grad_gate, gate_w, ((1,), (1,))) + dot(grad_up, up_w, ((1,), (1,)))).astype(BF16)
-    gu_g = dot(n2, jnp.concatenate([grad_gate, grad_up], axis=1), ((0,), (0,))).astype(BF16)
-
+    both = jnp.concatenate(
+        [(grad_act * by_gate.astype(F32)).astype(BF16), (grad_act * by_up.astype(F32)).astype(BF16)], axis=1
+    )
     eight = (8, half, width)
     output, input_grad, gu_parts, down_parts, a_parts = last(
-        mid, part_two.reshape(eight), out_part.reshape(eight), normed.reshape(eight), probs, hidden, own_cot, own_x,
-        qkv, mixture, fa, tabg, gu_g, down_g
+        mid, both.reshape(8, half, -1), activated, n2, normed.reshape(eight), probs, hidden, own_cot, own_x,
+        qkv, mixture, fa, tabg, gate_w, up_w, down_t, down_g
     )
 
     gains = jnp.stack([attn_gain, mlp_gain], axis=1).astype(F32)

time: 536 us -> 524 us (0.978)
  matrix products: 45.2 us -> 9.29 us
  Pallas kernels: 443 us -> 463 us
    dot_general x5 -> x1, matrix products: 45.2 us -> 9.29 us  [dot(): return lax.dot_general(a, b, (dims, ((), ())), preferred_element_type=F32)]
    pallas_call x1, Pallas kernels: 208 us -> 229 us  [last(): pl.pallas_call(functools.partial(last_kernel, mid, a_waves, d_waves, g_wa...]
    unnamed x38 -> x32, local copies, waits for them, and re-layouts: 10.5 us -> 11.8 us
where the time goes in v5:
time: 524 us; the launch traced here: 513 us
  Pallas kernels  463 us (88%)
  local copies, waits for them, and re-layouts  21.7 us (4%)
  other arithmetic  9.3 us (2%)
  matrix products  9.29 us (2%)
  blocking collectives  8.44 us (2%)
    pallas_call x1, Pallas kernels, last(): pl.pallas_call(functools.partial(last_kernel, mid, a_waves, d_waves, g_wa...  229 us
    pallas_call x1, Pallas kernels, first(): pl.pallas_call(functools.partial(first_kernel, mid, a_waves, waves), out_...  226 us
    unnamed x32, local copies, waits for them, and re-layouts  11.8 us

profile of v5, /device:TPU:0, one launch (start us, length us, event | category | flops | bytes accessed | tf_op | source)
XLA Modules:
  0.0 513.3 jit_solution(10650917570703770810)
XLA Ops:
  0.6 0.0 copy-start.9
  0.7 0.0 copy-start.10
  0.7 0.7 convert_element_type.68
  1.4 0.9 copy.76
  2.3 0.0 copy-start.1
  2.3 1.0 copy.78
  3.4 0.1 copy.77
  3.5 0.1 copy.79
  3.7 1.1 copy.74
  4.8 0.1 multiply_convert_fusion.4
  4.9 0.1 copy.75
  5.0 0.0 copy-start
  5.0 0.0 copy-done.9
  5.0 0.1 copy.80
  5.2 1.0 pad_maximum_fusion.1.wa
  6.2 0.0 copy-done.10
  6.2 0.5 slice.15
  6.7 0.7 compare_select_fusion
  7.4 0.1 select_reduce_fusion
  7.6 0.5 multiply_cosine_fusion
  8.1 0.1 broadcast_in_dim.32
  8.2 0.8 pad_maximum_fusion.2.table
  9.0 0.0 copy-done.1
  9.0 1.3 copy.81
  10.3 0.0 copy-done
  10.3 1.3 copy.83
  11.6 0.0 copy-done.12
  11.6 2.9 multiply_convert_fusion.2
  14.6 2.3 copy.82
  16.8 1.3 copy.84
  18.1 2.3 copy.85
  20.4 226.3 %shard_map.203 = (bf16[4,256,2048]{2,1,0:T(8,128)(2,1)}, f32[4,256,128]{2,1,0:T(8,128)}, bf16[2048,640]{1,0:T(8,128)(2,1)}, bf16[2048,1024]{1,0:T(8,128)(2,1)}, ...) custom-call(bf16[256,2048]{1,0:T(8,128)(2,1)} %tok.1, ...), custom_call_target="tpu_custom_call" | custom-call | tf_op jit(solution)/shard_map/pallas_call | solution.py:594
  246.7 9.3 %multiply_convert_fusion.1 = (bf16[1024,1024]{1,0:T(8,128)(2,1)S(1)}, bf16[1024,1024]{1,0:T(8,128)(2,1)S(1)}) fusion(bf16[1024,1024]{1,0:T(8,128)(2,1)} %get-tuple-element.43, bf16[1024,1024]{1,0:T(8,128)(2,1)} %get-tuple-element.44, bf16[1024,2048]{1,0:T(8,128)(2,1)} %bitcast.53, bf16[2048,1024]{1,0:T(8,128)(2,1)} %get-tuple-element.42.fd), kind=kOutput, calls=%fused_computation.2 | convolution fusion | flops 4301258752 | bytes 16777216 | tf_op jit(solution)/shard_map/dot_general | solution.py:1117
  256.0 0.0 copy-start.8
  256.0 2.4 pad_maximum_fusion
  258.4 0.0 copy-done.8
  258.4 2.1 constant_dynamic-slice_fusion
  260.5 229.2 %shard_map.204 = (bf16[256,2048]{1,0:T(8,128)(2,1)}, bf16[256,2048]{1,0:T(8,128)(2,1)}, bf16[8,128,2048]{2,1,0:T(8,128)(2,1)}, bf16[8,128,1024]{2,1,0:T(8,128)(2...) custom-call(bf16[8,128,2048]{2,1,0:T(8,128)(2,1)} %bitcast.32, bf16[1024,1024]{1,0:T(8,128)(2,1)} %get-tuple-element.45.act, ...), custom_call_target="tpu_custom_call" | custom-call | tf_op jit(solution)/shard_map/pallas_call | solution.py:977
  489.7 0.0 copy-done.11
  489.7 0.1 copy.88.gains
  489.9 0.0 copy-start.2
  489.9 1.2 copy-done.2
  491.1 1.3 copy-done.3
  492.4 1.2 copy-done.5
  493.6 8.0 %shard_map.205 = (f32[128,4096]{1,0:T(8,128)}, f32[128,4096]{1,0:T(8,128)}, f32[4096,128]{1,0:T(8,128)}, f32[128,1024]{1,0:T(8,128)}, f32[128,256]{1,0:T(8,128)}...) custom-call(bf16[2,4,128,2048]{3,2,1,0:T(8,128)(2,1)} %bitcast.36, ...), custom_call_target="tpu_custom_call" | custom-call | tf_op jit(solution)/shard_map/pallas_call | solution.py:1084
  501.6 8.4 %psum.7 = f32[128,2]{1,0:T(8,128)S(1)} all-reduce(f32[128,2]{1,0:T(8,128)S(1)} %bitcast.31), channel_id=1, replica_groups=mesh['dp'=16,'tensor'=2] {'tensor'}, use_global_device_ids=true, to_apply=%region_1.2 | all-reduce | flops 256 | bytes 2048 | tf_op jit(solution)/shard_map/psum | solution.py:1161
  510.0 0.7 slice_reduce_fusion
  510.7 2.3 copy.91
  (15 shorter events, 0.1 us)
Async XLA Ops:
  0.6 4.4 copy-start.9
  0.7 5.6 %copy-start.10 = (s32[256]{0:T(256)S(1)}, s32[256]{0:T(256)}, u32[]{:S(2)}) copy-start(s32[256]{0:T(256)} %param.22) | copy-start | bytes 3076
  2.3 6.7 %copy-start.1 = (bf16[128,4096]{1,0:T(8,128)(2,1)S(1)}, bf16[128,4096]{1,0:T(8,128)(2,1)}, u32[]{:S(2)}) copy-start(bf16[128,4096]{1,0:T(8,128)(2,1)} %w_gate.1) | copy-start | bytes 3145732
  5.0 5.3 %copy-start = (bf16[128,4096]{1,0:T(8,128)(2,1)S(1)}, bf16[128,4096]{1,0:T(8,128)(2,1)}, u32[]{:S(2)}) copy-start(bf16[128,4096]{1,0:T(8,128)(2,1)} %w_up.1) | copy-start | bytes 3145732
  6.2 5.4 %copy-start.12 = (bf16[128]{0:T(256)(128)(2,1)S(1)}, bf16[128]{0:T(256)(128)(2,1)}, u32[]{:S(2)}) copy-start(bf16[128]{0:T(256)(128)(2,1)} %param.18) | copy-start | bytes 772
  256.0 2.4 copy-start.8
  260.5 229.2 %copy-start.11 = (bf16[128]{0:T(256)(128)(2,1)S(1)}, bf16[128]{0:T(256)(128)(2,1)}, u32[]{:S(2)}) copy-start(bf16[128]{0:T(256)(128)(2,1)} %param.13) | copy-start | bytes 772
  260.5 229.4 %copy-start.4 = (bf16[128,1024]{1,0:T(8,128)(2,1)S(1)}, bf16[128,1024]{1,0:T(8,128)(2,1)}, u32[]{:S(2)}) copy-start(bf16[128,1024]{1,0:T(8,128)(2,1)} %w_query.1) | copy-start | bytes 786436
  260.5 229.4 %copy-start.6 = (bf16[128,256]{1,0:T(8,128)(2,1)S(1)}, bf16[128,256]{1,0:T(8,128)(2,1)}, u32[]{:S(2)}) copy-start(bf16[128,256]{1,0:T(8,128)(2,1)} %w_key.1) | copy-start | bytes 196612
  260.5 229.4 %copy-start.7 = (bf16[128,256]{1,0:T(8,128)(2,1)S(1)}, bf16[128,256]{1,0:T(8,128)(2,1)}, u32[]{:S(2)}) copy-start(bf16[128,256]{1,0:T(8,128)(2,1)} %w_value.1) | copy-start | bytes 196612
  489.9 1.2 copy-start.2
  491.1 1.3 copy-start.3
  492.4 1.2 copy-start.5
